TPU v7x, 256 devices: a whole 4x4x8 slice. The times are simulated.
256 devices in a mesh: sub: 8 (over x, core), grp: 32 (over z, y).
Axes of the slice: x: 4, y: 4, z: 8, core: 2. Of those that a mesh axis runs over, the one named last changes fastest.
Arguments:
- rhs: float32 [32, 8, 2048, 128], P('grp', 'sub')
- schur: bfloat16 [32, 8, 2048, 2048], P('grp', 'sub'), as said below
- stiff: float32 [32, 8, 2048], P('grp', 'sub'), may hold values from 1 to 100
- face_index: int32 [32, 8, 2048], P('grp', 'sub'), may hold values from 0 to 2047, each once within a row
- basis: bfloat16 [32, 8, 2048, 256], P('grp', 'sub'), may hold values from -0.125 to 0.125
- membership: int32 [32, 256], P('grp'), may hold values from 0 to 255
- level1_inv: float32 [32, 256, 256], P('grp'), as said below
- level2_inv: float32 [256, 256], replicated, as said below
Outputs:
- solution: float32 [32, 8, 2048, 128], P('grp', 'sub')
- residual: float32 [32, 8, 2048, 128], P('grp', 'sub')
Inputs may be any that keep to these rules, and one draw needn't show every extreme that they name: `schur`: each subdomain's matrix is symmetric positive definite. `level1_inv`: each group's matrix is symmetric positive definite. `level2_inv`: symmetric positive definite.
All inputs are finite; a program needn't handle non-finite values.
Results may differ from a plain program's by a relative error of at most 0.015.
Values sent between devices are 32-bit elements; how exact they have to be, the bound alone decides.
No kernel may reach another device: no remote copies, remote signals or barrier semaphores. Data moves between devices by JAX's collectives and lax.ppermute only.
A program may use at most 64 MiB of HBM per device.

v0:
```python
import jax
import jax.numpy as jnp
from jax import lax
from jax.sharding import PartitionSpec as P

G2 = 256
ITERS = 2
LOCAL_STEPS = 2


def passed_along(value, axis, steps):
    count = lax.axis_size(axis)
    pairs = [(source, (source + steps) % count) for source in range(count)]
    return lax.ppermute(value, axis, pairs)


def body(rhs, schur, stiff, face_index, basis, membership, level1_inv, level2_inv):
    high = lax.Precision.HIGHEST
    matrix = schur[0, 0]
    face_order = face_index[0, 0]
    coarse_basis = basis[0, 0]
    inverse_one = level1_inv[0]
    dof_count = matrix.shape[0]
    face_size = dof_count // 4

    def incoming(values):
        face_blocks = tuple(
            (vector[face_order].reshape(4, face_size, vector.shape[1]) for vector in values)
        )
        arrived_map = {}
        for offset in (1, -1):
            outgoing = tuple((blocks[1] if offset == 1 else blocks[0] for blocks in face_blocks))
            arrived_map["sub", offset] = passed_along(outgoing, "sub", offset)
        for offset in (1, -1):
            outgoing = tuple((blocks[3] if offset == 1 else blocks[2] for blocks in face_blocks))
            arrived_map["grp", offset] = passed_along(outgoing, "grp", offset)
        placed = []
        for member_pos, vector in enumerate(values):
            arrived = jnp.concatenate(
                [
                    arrived_map["sub", 1][member_pos],
                    arrived_map["sub", -1][member_pos],
                    arrived_map["grp", 1][member_pos],
                    arrived_map["grp", -1][member_pos],
                ],
                axis=0,
            )
            placed.append(jnp.zeros_like(vector).at[face_order].set(arrived))
        return tuple(placed)

    rhs_in, stiff_in = incoming((rhs[0, 0], stiff[0, 0][:, None]))
    residual = rhs[0, 0] + rhs_in
    own_stiff = stiff[0, 0][:, None]
    weight_col = own_stiff / (own_stiff + stiff_in)
    diagonal_part = jnp.diagonal(matrix).astype(jnp.float32)[:, None]
    aggregation = (membership[0][None, :] == jnp.arange(G2, dtype=jnp.int32)[:, None]).astype(
        jnp.float32
    )

    def schur_times(vector):
        return jnp.dot(matrix, vector.astype(jnp.bfloat16), preferred_element_type=jnp.float32)

    def inner(pairs):
        local_terms = tuple((jnp.sum(first * second, axis=0) for first, second in pairs))
        totals = lax.psum(local_terms, ("sub", "grp"))
        return tuple((0.5 * total for total in totals))

    def precondition(current):
        weighted = weight_col * current
        weighted_bf = weighted.astype(jnp.bfloat16)
        local_fix = weighted / diagonal_part
        for sweep in range(LOCAL_STEPS):
            local_fix = local_fix + (weighted - schur_times(local_fix)) / diagonal_part
        partial_value = lax.dot_general(
            coarse_basis, weighted_bf, (((0,), (0,)), ((), ())), preferred_element_type=jnp.float32
        )
        group_total = lax.psum(partial_value, "sub")
        level_two = lax.psum(jnp.dot(aggregation, group_total, precision=high), "grp")
        solved_two = jnp.dot(level2_inv, level_two, precision=high)
        coarse_value = jnp.dot(inverse_one, group_total, precision=high) + lax.dot_general(
            aggregation, solved_two, (((0,), (0,)), ((), ())), precision=high
        )
        correction = jnp.dot(
            coarse_basis, coarse_value.astype(jnp.bfloat16), preferred_element_type=jnp.float32
        )
        local_sum = weight_col * (local_fix + correction)
        return local_sum + incoming((local_sum,))[0]

    solution = jnp.zeros_like(residual)
    z_value = precondition(residual)
    direction = z_value
    r_dot_z = inner(((residual, z_value),))[0]
    for step in range(ITERS):
        product = schur_times(direction)
        image = product + incoming((product,))[0]
        step_len = r_dot_z / inner(((direction, image),))[0]
        solution = solution + step_len * direction
        residual = residual - step_len * image
        if step + 1 < ITERS:
            z_value = precondition(residual)
            next_dot = inner(((residual, z_value),))[0]
            direction = z_value + next_dot / r_dot_z * direction
            r_dot_z = next_dot
    return (solution[None, None], residual[None, None])


def solution(mesh):
    placed = (
        P("grp", "sub", None, None),
        P("grp", "sub", None, None),
        P("grp", "sub", None),
        P("grp", "sub", None),
        P("grp", "sub", None, None),
        P("grp", None),
        P("grp", None, None),
        P(),
    )
    return jax.shard_map(
        body,
        mesh=mesh,
        in_specs=placed,
        out_specs=(P("grp", "sub", None, None), P("grp", "sub", None, None)),
        check_vma=False,
    )
```

profile of v0, /device:TPU:1, one launch (start us, length us, event | category | flops | bytes accessed | tf_op | source)
XLA Modules:
  0.0 911.4 jit_solution(5313100273253266721)
XLA Ops:
  8.1 10.2 %gather_fusion.1 = f32[2048]{0:T(1024)S(1)} fusion(f32[2048]{0:T(1024)} %bitcast.131, s32[2048]{0:T(1024)S(1)} %broadcast_clamp_fusion), kind=kCustom, calls=%fused_computation.1 | custom fusion | bytes 24576 | tf_op jit(solution)/shard_map/gather | solution.py:28
  22.6 6.5 collective-permute-start.7
  37.8 32.0 %gather_fusion.2 = bf16[2048]{0:T(1024)(128)(2,1)S(1)} fusion(bf16[2048,2048]{1,0:T(8,128)(2,1)} %bitcast.134, s32[2048]{0:T(1024)S(1)} %bitcast.132), kind=kCustom, calls=%fused_computation.2 | custom fusion | bytes 24576 | tf_op jit(solution)/shard_map/jit(diagonal)/cond/branch_0_fun/gather | solution.py:55
  75.2 8.0 scatter_custom_fusion.1
  84.7 6.9 scatter_custom_fusion
  95.4 7.3 fusion.15
  102.7 52.1 %all-reduce.6.cloned.1.call-done = f32[256,128]{0,1:T(8,128)} async-done(((f32[256,128]{0,1:T(8,128)}), f32[256,128]{0,1:T(8,128)}) %all-reduce.6.cloned.1.call-update) | async-done | bytes 131088 | tf_op jit(solution)/shard_map/psum | solution.py:77
  157.2 7.8 fusion.13
  165.0 131.8 %all-reduce.8.cloned.1.call-done = f32[256,128]{1,0:T(8,128)} async-done(((f32[256,128]{1,0:T(8,128)}), f32[256,128]{1,0:T(8,128)}) %all-reduce.8.cloned.1.call-update) | async-done | bytes 131088 | tf_op jit(solution)/shard_map/psum | solution.py:78
  300.8 7.6 gather_fusion.3
  309.7 5.5 collective-permute-start.8
  320.0 6.0 collective-permute-done.10
  327.5 6.9 scatter_custom_fusion.2
  337.0 7.2 convolution_bitcast_fusion.3
  345.8 7.6 gather_fusion.4
  360.9 6.1 collective-permute-done.14
  368.4 6.9 scatter_custom_fusion.3
  379.6 75.3 %all-reduce = (f32[128]{0:T(128)S(1)}, f32[128]{0:T(128)S(1)}) all-reduce(f32[128]{0:T(128)S(1)} %get-tuple-element.7, f32[128]{0:T(128)S(1)} %get-tuple-element.6), channel_id=1, replica_groups=mesh['sub'=8,'grp'=32] {'sub','grp'}, use_global_device_ids=true, to_apply=%region_9.10 | all-reduce | flops 256 | bytes 2048 | tf_op jit(solution)/shard_map/psum | solution.py:65
  457.7 7.3 fusion.11
  465.0 49.4 %all-reduce.10.cloned.1.call-done = f32[256,128]{0,1:T(8,128)} async-done(((f32[256,128]{0,1:T(8,128)}), f32[256,128]{0,1:T(8,128)}) %all-reduce.10.cloned.1.call-update) | async-done | bytes 131088 | tf_op jit(solution)/shard_map/psum | solution.py:77
  516.3 7.8 fusion.9
  524.1 132.2 %all-reduce.12.cloned.1.call-done = f32[256,128]{1,0:T(8,128)} async-done(((f32[256,128]{1,0:T(8,128)}), f32[256,128]{1,0:T(8,128)}) %all-reduce.12.cloned.1.call-update) | async-done | bytes 131088 | tf_op jit(solution)/shard_map/psum | solution.py:78
  664.1 7.6 gather_fusion.5
  673.0 5.5 collective-permute-start.16
  683.4 5.8 collective-permute-done.18
  690.7 6.8 scatter_custom_fusion.4
  701.0 75.2 %psum.62 = f32[128]{0:T(128)S(1)} all-reduce(f32[128]{0:T(128)S(1)} %get-tuple-element.12), channel_id=1, replica_groups=mesh['sub'=8,'grp'=32] {'sub','grp'}, use_global_device_ids=true, to_apply=%region_14.15 | all-reduce | flops 128 | bytes 1024 | tf_op jit(solution)/shard_map/psum | solution.py:65
  776.2 7.3 convolution_bitcast_fusion
  785.0 7.6 gather_fusion.6
  799.8 5.5 collective-permute-done.22
  806.0 7.5 scatter_custom_fusion.5
  819.2 77.1 %psum.63 = f32[128]{0:T(128)S(1)} all-reduce(f32[128]{0:T(128)S(1)} %get-tuple-element.10), channel_id=1, replica_groups=mesh['sub'=8,'grp'=32] {'sub','grp'}, use_global_device_ids=true, to_apply=%region_17.18 | all-reduce | flops 128 | bytes 1024 | tf_op jit(solution)/shard_map/psum | solution.py:65
  (154 shorter events, 102.6 us)
Async XLA Ops:
  7.2 147.6 %all-reduce.6.cloned.1.call-start = ((), (), s32[]{:S(2)}) async-start(), calls=%async_computation | async-start | bytes 262144 | tf_op jit(solution)/shard_map/psum | solution.py:77
  8.1 360.3 %copy-start.22 = (s32[2048,1]{0,1:T(1,128)}, s32[2048,1]{0,1:T(1,128)S(1)}, u32[]{:S(2)}) copy-start(s32[2048,1]{0,1:T(1,128)S(1)} %compare_select_fusion) | copy-start | bytes 24580
  18.4 51.5 %collective-permute-start.6 = (f32[512,1]{0,1:T(1,128)S(1)}, f32[512,1]{0,1:T(1,128)S(1)}, u32[]{:S(2)}, u32[]{:S(2)}) collective-permute-start(f32[512,1]{0,1:T(1,128)S(1)} %bitcast.159), channel_id=1, source_target_pairs={{0,1},{1,2},{2,3},{3,4},{4,5},{5,6},{6,7},{7,8},{8,9},{9,10},{10,1... | collective-permute-start | bytes 6152 | tf_op jit(solution)/shard_map/ppermute | solution.py:14
  20.6 49.4 %collective-permute-start.4 = (f32[512,1]{0,1:T(1,128)S(1)}, f32[512,1]{0,1:T(1,128)S(1)}, u32[]{:S(2)}, u32[]{:S(2)}) collective-permute-start(f32[512,1]{0,1:T(1,128)S(1)} %bitcast.158), channel_id=1, source_target_pairs={{0,32},{32,64},{64,96},{96,128},{128,160},{160,192},{192,224},{224... | collective-permute-start | bytes 6152 | tf_op jit(solution)/shard_map/ppermute | solution.py:14
  22.6 47.5 %collective-permute-start.5 = (f32[512,1]{0,1:T(1,128)S(1)}, f32[512,1]{0,1:T(1,128)S(1)}, u32[]{:S(2)}, u32[]{:S(2)}) collective-permute-start(f32[512,1]{0,1:T(1,128)S(1)} %bitcast.157), channel_id=1, source_target_pairs={{0,224},{32,0},{64,32},{96,64},{128,96},{160,128},{192,160},{224,1... | collective-permute-start | bytes 6152 | tf_op jit(solution)/shard_map/ppermute | solution.py:14
  22.6 52.6 %collective-permute-start.7 = (f32[512,1]{0,1:T(1,128)S(1)}, f32[512,1]{0,1:T(1,128)S(1)}, u32[]{:S(2)}, u32[]{:S(2)}) collective-permute-start(f32[512,1]{0,1:T(1,128)S(1)} %bitcast.156), channel_id=1, source_target_pairs={{0,31},{1,0},{2,1},{3,2},{4,3},{5,4},{6,5},{7,6},{8,7},{9,8},{10,9... | collective-permute-start | bytes 6152 | tf_op jit(solution)/shard_map/ppermute | solution.py:14
  35.5 47.8 %collective-permute-start = (f32[512,128]{1,0:T(8,128)}, f32[512,128]{1,0:T(8,128)}, u32[]{:S(2)}, u32[]{:S(2)}) collective-permute-start(f32[512,128]{1,0:T(8,128)} %get-tuple-element.31), channel_id=1, source_target_pairs={{0,32},{32,64},{64,96},{96,128},{128,160},{160,192},{192,224},{224... | collective-permute-start | bytes 786440 | tf_op jit(solution)/shard_map/ppermute | solution.py:14
  69.9 387.8 %copy-start.24 = (f32[2048]{0:T(1024)}, f32[2048]{0:T(1024)S(1)}, u32[]{:S(2)}) copy-start(f32[2048]{0:T(1024)S(1)} %convert_element_type.38) | copy-start | bytes 24580
  69.9 13.4 %collective-permute-start.2 = (f32[512,128]{1,0:T(8,128)}, f32[512,128]{1,0:T(8,128)S(1)}, u32[]{:S(2)}, u32[]{:S(2)}) collective-permute-start(f32[512,128]{1,0:T(8,128)} %get-tuple-element.32), channel_id=1, source_target_pairs={{0,1},{1,2},{2,3},{3,4},{4,5},{5,6},{6,7},{7,8},{8,9},{9,10},{10,1... | collective-permute-start | bytes 786440 | tf_op jit(solution)/shard_map/ppermute | solution.py:14
  70.0 13.3 %collective-permute-start.1 = (f32[512,128]{1,0:T(8,128)}, f32[512,128]{1,0:T(8,128)S(1)}, u32[]{:S(2)}, u32[]{:S(2)}) collective-permute-start(f32[512,128]{1,0:T(8,128)} %get-tuple-element.33), channel_id=1, source_target_pairs={{0,224},{32,0},{64,32},{96,64},{128,96},{160,128},{192,160},{224,1... | collective-permute-start | bytes 786440 | tf_op jit(solution)/shard_map/ppermute | solution.py:14
  70.1 14.6 %collective-permute-start.3 = (f32[512,128]{1,0:T(8,128)S(1)}, f32[512,128]{1,0:T(8,128)}, u32[]{:S(2)}, u32[]{:S(2)}) collective-permute-start(f32[512,128]{1,0:T(8,128)S(1)} %get-tuple-element.34), channel_id=1, source_target_pairs={{0,31},{1,0},{2,1},{3,2},{4,3},{5,4},{6,5},{7,6},{8,7},{9,8},{10,9... | collective-permute-start | bytes 786440 | tf_op jit(solution)/shard_map/ppermute | solution.py:14
  95.3 201.5 %all-reduce.8.cloned.1.call-start = ((), (), s32[]{:S(2)}) async-start(), calls=%async_computation.1 | async-start | bytes 262144 | tf_op jit(solution)/shard_map/psum | solution.py:78
  102.7 194.1 %copy-start.7 = (f32[256,256]{1,0:T(8,128)S(1)}, f32[256,256]{1,0:T(8,128)}, u32[]{:S(2)}) copy-start(f32[256,256]{1,0:T(8,128)} %param.15) | copy-start | bytes 786436
  102.7 195.7 %copy-start.8 = (f32[1,256,256]{2,1,0:T(8,128)S(1)}, f32[1,256,256]{2,1,0:T(8,128)}, u32[]{:S(2)}) copy-start(f32[1,256,256]{2,1,0:T(8,128)} %param.14) | copy-start | bytes 786436
  156.7 357.7 %all-reduce.10.cloned.1.call-start = ((), (), s32[]{:S(2)}) async-start(), calls=%async_computation.2 | async-start | bytes 262144 | tf_op jit(solution)/shard_map/psum | solution.py:77
  309.7 10.3 %collective-permute-start.8 = (f32[512,128]{1,0:T(8,128)S(1)}, f32[512,128]{1,0:T(8,128)S(1)}, u32[]{:S(2)}, u32[]{:S(2)}) collective-permute-start(f32[512,128]{1,0:T(8,128)S(1)} %get-tuple-element.27), channel_id=1, source_target_pairs={{0,32},{32,64},{64,96},{96,128},{128,160},{160,192},{192,224},{224... | collective-permute-start | bytes 786440 | tf_op jit(solution)/shard_map/ppermute | solution.py:14
  315.2 10.8 %collective-permute-start.10 = (f32[512,128]{1,0:T(8,128)S(1)}, f32[512,128]{1,0:T(8,128)S(1)}, u32[]{:S(2)}, u32[]{:S(2)}) collective-permute-start(f32[512,128]{1,0:T(8,128)S(1)} %get-tuple-element.28), channel_id=1, source_target_pairs={{0,1},{1,2},{2,3},{3,4},{4,5},{5,6},{6,7},{7,8},{8,9},{9,10},{10,1... | collective-permute-start | bytes 786440 | tf_op jit(solution)/shard_map/ppermute | solution.py:14
  316.4 9.6 %collective-permute-start.9 = (f32[512,128]{1,0:T(8,128)S(1)}, f32[512,128]{1,0:T(8,128)S(1)}, u32[]{:S(2)}, u32[]{:S(2)}) collective-permute-start(f32[512,128]{1,0:T(8,128)S(1)} %get-tuple-element.29), channel_id=1, source_target_pairs={{0,224},{32,0},{64,32},{96,64},{128,96},{160,128},{192,160},{224,1... | collective-permute-start | bytes 786440 | tf_op jit(solution)/shard_map/ppermute | solution.py:14
  316.4 11.0 %collective-permute-start.11 = (f32[512,128]{1,0:T(8,128)S(1)}, f32[512,128]{1,0:T(8,128)}, u32[]{:S(2)}, u32[]{:S(2)}) collective-permute-start(f32[512,128]{1,0:T(8,128)S(1)} %get-tuple-element.30), channel_id=1, source_target_pairs={{0,31},{1,0},{2,1},{3,2},{4,3},{5,4},{6,5},{7,6},{8,7},{9,8},{10,9... | collective-permute-start | bytes 786440 | tf_op jit(solution)/shard_map/ppermute | solution.py:14
  354.6 6.3 collective-permute-start.12
  355.9 11.0 %collective-permute-start.14 = (f32[512,128]{1,0:T(8,128)S(1)}, f32[512,128]{1,0:T(8,128)S(1)}, u32[]{:S(2)}, u32[]{:S(2)}) collective-permute-start(f32[512,128]{1,0:T(8,128)S(1)} %get-tuple-element.24), channel_id=1, source_target_pairs={{0,1},{1,2},{2,3},{3,4},{4,5},{5,6},{6,7},{7,8},{8,9},{9,10},{10,1... | collective-permute-start | bytes 786440 | tf_op jit(solution)/shard_map/ppermute | solution.py:14
  356.0 11.0 %collective-permute-start.13 = (f32[512,128]{1,0:T(8,128)S(1)}, f32[512,128]{1,0:T(8,128)S(1)}, u32[]{:S(2)}, u32[]{:S(2)}) collective-permute-start(f32[512,128]{1,0:T(8,128)S(1)} %get-tuple-element.25), channel_id=1, source_target_pairs={{0,224},{32,0},{64,32},{96,64},{128,96},{160,128},{192,160},{224,1... | collective-permute-start | bytes 786440 | tf_op jit(solution)/shard_map/ppermute | solution.py:14
  356.0 12.4 %collective-permute-start.15 = (f32[512,128]{1,0:T(8,128)S(1)}, f32[512,128]{1,0:T(8,128)}, u32[]{:S(2)}, u32[]{:S(2)}) collective-permute-start(f32[512,128]{1,0:T(8,128)S(1)} %get-tuple-element.26), channel_id=1, source_target_pairs={{0,31},{1,0},{2,1},{3,2},{4,3},{5,4},{6,5},{7,6},{8,7},{9,8},{10,9... | collective-permute-start | bytes 786440 | tf_op jit(solution)/shard_map/ppermute | solution.py:14
  457.7 198.6 %all-reduce.12.cloned.1.call-start = ((), (), s32[]{:S(2)}) async-start(), calls=%async_computation.3 | async-start | bytes 262144 | tf_op jit(solution)/shard_map/psum | solution.py:78
  673.0 10.5 %collective-permute-start.16 = (f32[512,128]{1,0:T(8,128)S(1)}, f32[512,128]{1,0:T(8,128)S(1)}, u32[]{:S(2)}, u32[]{:S(2)}) collective-permute-start(f32[512,128]{1,0:T(8,128)S(1)} %get-tuple-element.19), channel_id=1, source_target_pairs={{0,32},{32,64},{64,96},{96,128},{128,160},{160,192},{192,224},{224... | collective-permute-start | bytes 786440 | tf_op jit(solution)/shard_map/ppermute | solution.py:14
  678.5 10.8 %collective-permute-start.18 = (f32[512,128]{1,0:T(8,128)S(1)}, f32[512,128]{1,0:T(8,128)S(1)}, u32[]{:S(2)}, u32[]{:S(2)}) collective-permute-start(f32[512,128]{1,0:T(8,128)S(1)} %get-tuple-element.20), channel_id=1, source_target_pairs={{0,1},{1,2},{2,3},{3,4},{4,5},{5,6},{6,7},{7,8},{8,9},{9,10},{10,1... | collective-permute-start | bytes 786440 | tf_op jit(solution)/shard_map/ppermute | solution.py:14
  679.6 9.6 %collective-permute-start.17 = (f32[512,128]{1,0:T(8,128)S(1)}, f32[512,128]{1,0:T(8,128)S(1)}, u32[]{:S(2)}, u32[]{:S(2)}) collective-permute-start(f32[512,128]{1,0:T(8,128)S(1)} %get-tuple-element.21), channel_id=1, source_target_pairs={{0,224},{32,0},{64,32},{96,64},{128,96},{160,128},{192,160},{224,1... | collective-permute-start | bytes 786440 | tf_op jit(solution)/shard_map/ppermute | solution.py:14
  679.7 11.1 %collective-permute-start.19 = (f32[512,128]{1,0:T(8,128)S(1)}, f32[512,128]{1,0:T(8,128)}, u32[]{:S(2)}, u32[]{:S(2)}) collective-permute-start(f32[512,128]{1,0:T(8,128)S(1)} %get-tuple-element.22), channel_id=1, source_target_pairs={{0,31},{1,0},{2,1},{3,2},{4,3},{5,4},{6,5},{7,6},{8,7},{9,8},{10,9... | collective-permute-start | bytes 786440 | tf_op jit(solution)/shard_map/ppermute | solution.py:14
  793.9 5.9 collective-permute-start.20
  794.3 11.0 %collective-permute-start.22 = (f32[512,128]{1,0:T(8,128)S(1)}, f32[512,128]{1,0:T(8,128)}, u32[]{:S(2)}, u32[]{:S(2)}) collective-permute-start(f32[512,128]{1,0:T(8,128)S(1)} %get-tuple-element.16), channel_id=1, source_target_pairs={{0,1},{1,2},{2,3},{3,4},{4,5},{5,6},{6,7},{7,8},{8,9},{9,10},{10,1... | collective-permute-start | bytes 786440 | tf_op jit(solution)/shard_map/ppermute | solution.py:14
  794.4 10.9 %collective-permute-start.21 = (f32[512,128]{1,0:T(8,128)S(1)}, f32[512,128]{1,0:T(8,128)S(1)}, u32[]{:S(2)}, u32[]{:S(2)}) collective-permute-start(f32[512,128]{1,0:T(8,128)S(1)} %get-tuple-element.17), channel_id=1, source_target_pairs={{0,224},{32,0},{64,32},{96,64},{128,96},{160,128},{192,160},{224,1... | collective-permute-start | bytes 786440 | tf_op jit(solution)/shard_map/ppermute | solution.py:14
  794.8 11.3 %collective-permute-start.23 = (f32[512,128]{1,0:T(8,128)S(1)}, f32[512,128]{1,0:T(8,128)}, u32[]{:S(2)}, u32[]{:S(2)}) collective-permute-start(f32[512,128]{1,0:T(8,128)S(1)} %get-tuple-element.18), channel_id=1, source_target_pairs={{0,31},{1,0},{2,1},{3,2},{4,3},{5,4},{6,5},{7,6},{8,7},{9,8},{10,9... | collective-permute-start | bytes 786440 | tf_op jit(solution)/shard_map/ppermute | solution.py:14
  (25 other events, 1074.0 us)
Sparse Core Ops, SparseCore 0:
  95.4 59.3 all-reduce.5
  158.6 138.1 all-reduce.7
  457.8 56.5 all-reduce.9
  518.1 138.1 all-reduce.11
where the time goes:
time: 921 us; the launch traced here: 911 us
  waiting for transfers between devices  389 us (42%)
  blocking collectives  228 us (25%)
  local copies, waits for them, and re-layouts  117 us (13%)
  matrix products  60.3 us (7%)
  other arithmetic  51.8 us (6%)
  starting transfers between devices  51.5 us (6%)
  between operations  14.5 us (2%)
    psum x2, waiting for transfers between devices, precondition(): lax.psum(jnp.dot(aggregation, group_total, precision=high), 'grp')  264 us
    psum x3, blocking collectives, inner(): totals = lax.psum(local_terms, ('sub', 'grp'))  228 us
    psum x2, waiting for transfers between devices, precondition(): group_total = lax.psum(partial_value, 'sub')  102 us
    ppermute x24, starting transfers between devices, passed_along(): return lax.ppermute(value, axis, pairs)  50.9 us
    gather x6, local copies, waits for them, and re-layouts, incoming(): vector[face_order].reshape(4, face_size, vector.shape[1])  46 us
    dot_general x6, matrix products, schur_times(): jnp.dot(matrix, vector.astype(jnp.bfloat16), preferred_element_type=jnp.f...  44.7 us
    scatter x5, other arithmetic, incoming(): placed.append(jnp.zeros_like(vector).at[face_order].set(arrived))  35 us
    gather x1, local copies, waits for them, and re-layouts, body(): diagonal_part = jnp.diagonal(matrix).astype(jnp.float32)[:, None]  32 us
  transfers between devices with their start and end apart: 28, of which 8 were waited for; matrix products, arithmetic and copies ran while one was open for 8% of the time, Pallas kernels for 0%

commit v1 on v0

v1 whole, which is shorter than its diff:
```python
import jax
import jax.numpy as jnp
from jax import lax
from jax.sharding import PartitionSpec as P

LOCAL_STEPS = 2
HIGH = lax.Precision.HIGHEST
BF = jnp.bfloat16
F32 = jnp.float32


def passed_along(value, axis, steps):
    count = lax.axis_size(axis)
    pairs = [(source, (source + steps) % count) for source in range(count)]
    return lax.ppermute(value, axis, pairs)


def spread(chunks, axis, groups=None):
    return lax.all_to_all(chunks, axis, 0, 0, axis_index_groups=groups)


def copies(value, count):
    return jnp.broadcast_to(value[None], (count,) + value.shape)


def dot(first, second, contract, precision=None):
    return lax.dot_general(
        first, second, (contract, ((), ())), precision=precision, preferred_element_type=F32
    )


def split(value):
    top = value.astype(BF)
    return jnp.concatenate([top, (value - top.astype(F32)).astype(BF)], axis=1)


def body(rhs, schur, stiff, face_index, basis, membership, level1_inv, level2_inv):
    matrix_in = schur[0, 0]
    order = face_index[0, 0]
    inverse_one = level1_inv[0]
    dofs, cols = rhs.shape[2], rhs.shape[3]
    face = dofs // 4
    coarse = level1_inv.shape[1]
    coarse_two = level2_inv.shape[0]
    n_sub, n_grp = lax.axis_size("sub"), lax.axis_size("grp")
    inner_y = 4 if n_grp % 4 == 0 else 1
    outer_z = n_grp // inner_y
    groups_y = [[z * inner_y + y for y in range(inner_y)] for z in range(outer_z)]
    groups_z = [[z * inner_y + y for z in range(outer_z)] for y in range(inner_y)]
    share = cols // n_sub

    pick = (order[:, None] == jnp.arange(dofs, dtype=jnp.int32)[None, :]).astype(BF)
    rhs_f = rhs[0, 0][order]
    stiff_col = stiff[0, 0][:, None]
    stiff_hi = stiff_col.astype(BF)
    stiff_mid = (stiff_col - stiff_hi.astype(F32)).astype(BF)
    stiff_lo = (stiff_col - stiff_hi.astype(F32) - stiff_mid.astype(F32)).astype(BF)
    stiff_parts = dot(pick, jnp.concatenate([stiff_hi, stiff_mid, stiff_lo], axis=1), ((1,), (0,)))
    stiff_f = stiff_parts[:, 0:1] + stiff_parts[:, 1:2] + stiff_parts[:, 2:3]

    def exchanged(blocks):
        return [
            passed_along(blocks[1], "sub", 1),
            passed_along(blocks[0], "sub", -1),
            passed_along(blocks[3], "grp", 1),
            passed_along(blocks[2], "grp", -1),
        ]

    def incoming(vector):
        return jnp.concatenate(exchanged([vector[k * face : (k + 1) * face] for k in range(4)]), axis=0)

    stiff_rows = face // cols
    blocks = [
        jnp.concatenate(
            [rhs_f[k * face : (k + 1) * face], stiff_f[k * face : (k + 1) * face].reshape(stiff_rows, cols)],
            axis=0,
        )
        for k in range(4)
    ]
    arrived = exchanged(blocks)
    residual0 = rhs_f + jnp.concatenate([block[:face] for block in arrived], axis=0)
    stiff_in = jnp.concatenate([block[face:].reshape(face, 1) for block in arrived], axis=0)
    weight = stiff_f / (stiff_f + stiff_in)

    basis_f = dot(pick, basis[0, 0], ((1,), (0,))).astype(BF)
    half_way = dot(pick, matrix_in, ((1,), (0,))).astype(BF)
    matrix = dot(half_way, pick, ((1,), (1,))).astype(BF)
    row_id = lax.broadcasted_iota(jnp.int32, (dofs, dofs), 0)
    col_id = lax.broadcasted_iota(jnp.int32, (dofs, dofs), 1)
    diagonal = jnp.sum(jnp.where(row_id == col_id, matrix.astype(F32), 0.0), axis=1)[:, None]
    aggregation = (membership[0][None, :] == jnp.arange(coarse_two, dtype=jnp.int32)[:, None]).astype(F32)

    def schur_times(vector):
        return dot(matrix, vector.astype(BF), ((1,), (0,)))

    def schur_times_split(vector):
        both = dot(matrix, split(vector), ((1,), (0,)))
        return both[:, :cols] + both[:, cols:]

    def corrected(weighted, fix):
        for _ in range(LOCAL_STEPS):
            fix = fix + (weighted - schur_times(fix)) / diagonal
        return fix

    def group_sum(partial):
        chunks = partial.reshape(n_sub, share, partial.shape[1])
        return jnp.sum(spread(chunks, "sub"), axis=0)

    def all_groups(value):
        if inner_y > 1:
            value = jnp.sum(spread(copies(value, inner_y), "grp", groups_y), axis=0)
        return jnp.sum(spread(copies(value, outer_z), "grp", groups_z), axis=0)

    def gathered(value):
        return spread(copies(value, n_sub), "sub").reshape(n_sub * share, value.shape[1])

    def level_two_of(group_total):
        return dot(group_total, aggregation, ((1,), (1,)), HIGH)

    def coarse_solve(group_total, level_two):
        solved_two = dot(level_two, level2_inv, ((1,), (1,)), HIGH)
        return dot(group_total, inverse_one, ((1,), (1,)), HIGH) + dot(
            solved_two, aggregation, ((1,), (0,)), HIGH
        )

    def finish(fix, coarse_value):
        correction = dot(basis_f, coarse_value.astype(BF), ((1,), (1,)))
        local_sum = weight * (fix + correction)
        return local_sum + incoming(local_sum)

    weighted = weight * residual0
    total0 = group_sum(dot(weighted.astype(BF), basis_f, ((0,), (0,))))
    two0 = all_groups(level_two_of(total0))
    coarse0 = 2.0 * gathered(0.5 * coarse_solve(total0, two0))
    z0 = finish(corrected(weighted, weighted / diagonal), coarse0)

    product0 = schur_times_split(z0)
    image0 = product0 + incoming(product0)

    dots0 = jnp.stack([0.5 * jnp.sum(residual0 * z0, axis=0), jnp.sum(z0 * product0, axis=0)], axis=1)
    dots0 = jnp.pad(dots0, ((0, 0), (0, 126)))
    both = dot(split(weight * image0), basis_f, ((0,), (0,)))
    mixed = group_sum(jnp.concatenate([both[:cols] + both[cols:], dots0], axis=1))
    total_q, dots = mixed[:, :coarse], mixed[:, coarse:]
    mixed = all_groups(jnp.concatenate([level_two_of(total_q), dots], axis=1))
    two_q, dots = mixed[:, :coarse_two], mixed[:, coarse_two:]
    step0 = dots[:, 0:1] / dots[:, 1:2]
    coarse1 = coarse_solve(total0 - step0 * total_q, two0 - step0 * two_q)
    lane = lax.broadcasted_iota(jnp.int32, dots.shape, 1)
    mixed = lax.optimization_barrier(
        gathered(jnp.concatenate([coarse1, jnp.where(lane == 2, step0, dots)], axis=1))
    )
    rz0, zaz0, step0 = (mixed[:, coarse + k][None, :] for k in range(3))
    coarse1 = mixed[:, :coarse]

    residual1 = residual0 - step0 * image0
    weighted = weight * residual1
    z1 = finish(corrected(weighted, weighted / diagonal), coarse1)
    product1 = schur_times_split(z1)
    dots1 = jnp.stack(
        [
            0.5 * jnp.sum(residual1 * z1, axis=0),
            jnp.sum(z1 * product1, axis=0),
            jnp.sum(z0 * product1, axis=0),
        ],
        axis=0,
    )
    dots1 = jnp.sum(spread(copies(dots1, n_sub), "sub"), axis=0)
    dots1 = jnp.sum(spread(copies(dots1, n_grp), "grp"), axis=0)
    rz1, zaz1, zaz01 = dots1[0:1], dots1[1:2], dots1[2:3]
    image1 = product1 + incoming(product1)
    ratio = rz1 / rz0
    step1 = rz1 / (zaz1 + 2.0 * ratio * zaz01 + ratio * ratio * zaz0)
    solution_f = step0 * z0 + step1 * (z1 + ratio * z0)
    residual_f = residual1 - step1 * (image1 + ratio * image0)
    outs = [jnp.zeros_like(value).at[order].set(value) for value in (solution_f, residual_f)]
    return outs[0][None, None], outs[1][None, None]


def solution(mesh):
    placed = (
        P("grp", "sub", None, None),
        P("grp", "sub", None, None),
        P("grp", "sub", None),
        P("grp", "sub", None),
        P("grp", "sub", None, None),
        P("grp", None),
        P("grp", None, None),
        P(),
    )
    return jax.shard_map(
        body,
        mesh=mesh,
        in_specs=placed,
        out_specs=(P("grp", "sub", None, None), P("grp", "sub", None, None)),
        check_vma=False,
    )
```

time: 921 us -> 280 us (0.30)
  waiting for transfers between devices: 389 us -> 38.4 us
  blocking collectives: 228 us -> 42.6 us
  local copies, waits for them, and re-layouts: 117 us -> 14.6 us
  matrix products: 60.3 us -> 94 us
  other arithmetic: 51.8 us -> 24.5 us
  between operations: 14.5 us -> 1.58 us
    psum x4 -> x0, waiting for transfers between devices: 365 us -> none  [the longest x2 264 us: precondition(): lax.psum(jnp.dot(aggregation, group_total, precision=high), 'grp')]
    psum x3 -> x0, blocking collectives: 228 us -> none  [inner(): totals = lax.psum(local_terms, ('sub', 'grp'))]
    gather x7 -> x1, local copies, waits for them, and re-layouts: 78 us -> 5.47 us  [body(): rhs_f = rhs[0, 0][order]]
    all_to_all x0 -> x4, blocking collectives: none -> 42.6 us  [spread(): return lax.all_to_all(chunks, axis, 0, 0, axis_index_groups=groups)]
    dot_general x18 -> x22, matrix products: 60.3 us -> 94 us  [dot(): lax.dot_general(first, second, (contract, ((), ())), precision=precision,...]
    all_to_all x0 -> x6, starting transfers between devices: none -> 28.6 us  [spread(): return lax.all_to_all(chunks, axis, 0, 0, axis_index_groups=groups)]
    ppermute x24 -> x20, starting transfers between devices: 50.9 us -> 30 us  [passed_along(): return lax.ppermute(value, axis, pairs)]
    scatter x5 -> x2, other arithmetic: 35 us -> 15.2 us  [body(): jnp.zeros_like(value).at[order].set(value)]
  transfers between devices with their start and end apart: 28 -> 26, of which waited for: 8 -> 10; matrix products, arithmetic and copies ran while one was open for 8% -> 27% of each run, Pallas kernels for 0% -> 0%
where the time goes in v1:
time: 280 us; the launch traced here: 274 us
  matrix products  94 us (34%)
  starting transfers between devices  58.6 us (21%)
  blocking collectives  42.6 us (15%)
  waiting for transfers between devices  38.4 us (14%)
  other arithmetic  24.5 us (9%)
  local copies, waits for them, and re-layouts  14.6 us (5%)
    dot_general x22, matrix products, dot(): lax.dot_general(first, second, (contract, ((), ())), precision=precision,...  94 us
    all_to_all x4, blocking collectives, spread(): return lax.all_to_all(chunks, axis, 0, 0, axis_index_groups=groups)  42.6 us
    ppermute x20, starting transfers between devices, passed_along(): return lax.ppermute(value, axis, pairs)  30 us
    all_to_all x6, starting transfers between devices, spread(): return lax.all_to_all(chunks, axis, 0, 0, axis_index_groups=groups)  28.6 us
    ppermute x20, waiting for transfers between devices, passed_along(): return lax.ppermute(value, axis, pairs)  21.5 us
    all_to_all x6, waiting for transfers between devices, spread(): return lax.all_to_all(chunks, axis, 0, 0, axis_index_groups=groups)  16.8 us
    scatter x2, other arithmetic, body(): jnp.zeros_like(value).at[order].set(value)  15.2 us
  transfers between devices with their start and end apart: 26, of which 10 were waited for; matrix products, arithmetic and copies ran while one was open for 27% of the time, Pallas kernels for 0%

profile of v1, /device:TPU:1, one launch (start us, length us, event | category | flops | bytes accessed | tf_op | source)
XLA Modules:
  0.0 274.3 jit_solution(779821318156693699)
XLA Ops:
  2.9 3.9 %fusion.3 = f32[2048,3]{0,1:T(4,128)S(1)} fusion(s32[2048]{0:T(1024)} %bitcast.112, bf16[2048,1]{0,1:T(2,128)(2,1)S(1)} %get-tuple-element.47, bf16[2048,1]{0,1:T(2,128)(2,1)S(1)} %get-tuple-element.46, bf16[2048,1]{0,1:T(2,128)(2,1)S(1)} %bitcast_convert_fusion), kind=kOutput, calls=%fused_computation.9 | convolution fusion | flops 29396992 | bytes 45056 | tf_op jit(solution)/shard_map/dot_general | solution.py:27
  6.9 5.5 %gather_fusion = f32[2048,128]{1,0:T(8,128)S(1)} fusion(f32[2048,128]{1,0:T(8,128)S(1)} %bitcast.85, s32[2048]{0:T(1024)S(1)} %broadcast_clamp_fusion), kind=kCustom, calls=%fused_computation | custom fusion | bytes 2105344 | tf_op jit(solution)/shard_map/gather | solution.py:53
  12.5 8.9 %collective-permute-start.3 = (f32[516,128]{1,0:T(8,128)S(1)}, f32[516,128]{1,0:T(8,128)S(1)}, u32[]{:S(2)}, u32[]{:S(2)}) collective-permute-start(f32[516,128]{1,0:T(8,128)S(1)} %pad_maximum_fusion.3), channel_id=1, source_target_pairs={{0,31},{1,0},{2,1},{3,2},{4,3},{5,4},{6,5},{7,6},{8,7},{9,8},{10,9... | collective-permute-start | bytes 792584 | tf_op jit(solution)/shard_map/ppermute | solution.py:15
  24.0 22.2 %fusion.1 = bf16[2048,2048]{1,0:T(8,128)(2,1)} fusion(bf16[1,1,2048,2048]{3,2,1,0:T(8,128)(2,1)} %param.9, s32[2048]{0:T(1024)S(1)} %bitcast.113), kind=kOutput, calls=%fused_computation.7 | convolution fusion | flops 17184063488 | bytes 16785408 | tf_op jit(solution)/shard_map/dot_general | solution.py:27
  46.2 3.0 %fusion.13 = bf16[2048,256]{1,0:T(8,128)(2,1)S(1)} fusion(s32[2048]{0:T(1024)S(1)} %bitcast.114, bf16[1,1,2048,256]{3,2,1,0:T(8,128)(2,1)S(1)} %copy-done.12), kind=kOutput, calls=%fused_computation.17 | convolution fusion | flops 2152202240 | bytes 2105344 | tf_op jit(solution)/shard_map/dot_general | solution.py:27
  51.0 5.6 %all-to-all-start = ((f32[8,16,256]{2,1,0:T(8,128)}), f32[8,16,256]{2,1,0:T(8,128)S(1)}, u32[]{:S(2)}, u32[]{:S(2)}) async-start(f32[8,16,256]{2,1,0:T(8,128)} %bitcast.15), calls=%async_computation | async-start | bytes 262144 | tf_op jit(solution)/shard_map/all_to_all | solution.py:19
  56.6 23.1 %select_reduce_fusion = (f32[2048]{0:T(1024)S(1)}, bf16[2048,2048]{0,1:T(8,128)(2,1)}) fusion(bf16[2048,2048]{1,0:T(8,128)(2,1)} %fusion.1, s32[2048]{0:T(1024)S(1)} %bitcast.115), kind=kOutput, calls=%fused_computation.3 | convolution fusion | flops 17205032960 | bytes 16793600 | tf_op jit(solution)/shard_map/dot_general | solution.py:27
  80.5 3.3 %all-to-all-start.1 = ((f32[4,16,256]{2,1,0:T(8,128)}), f32[4,16,256]{2,1,0:T(8,128)S(1)}, u32[]{:S(2)}, u32[]{:S(2)}) async-start(f32[4,16,256]{2,1,0:T(8,128)} %broadcast_in_dim.33), calls=%async_computation.1 | async-start | bytes 131072 | tf_op jit(solution)/shard_map/all_to_all | solution.py:19
  83.9 7.8 %fusion.17 = f32[2048,128]{1,0:T(8,128)} fusion(bf16[2048,2048]{0,1:T(8,128)(2,1)} %get-tuple-element.49, f32[2048,128]{1,0:T(8,128)S(1)} %maximum_add_fusion, f32[2048]{0:T(1024)S(1)} %get-tuple-element.48, f32[2048]{0:T(1024)S(1)} %bitcast.92), kind=kOutput, calls=%fused_computation.27 | convolution fusion | flops 1075838976 | bytes 10502144 | tf_op jit(solution)/shard_map/dot_general | solution.py:27
  92.4 4.4 %all-to-all-start.2 = ((f32[8,16,256]{2,1,0:T(8,128)}), f32[8,16,256]{2,1,0:T(8,128)S(1)}, u32[]{:S(2)}, u32[]{:S(2)}) async-start(f32[8,16,256]{2,1,0:T(8,128)} %broadcast_in_dim.34), calls=%async_computation.2 | async-start | bytes 262144 | tf_op jit(solution)/shard_map/all_to_all | solution.py:19
  97.1 7.8 %all-to-all-done.2 = f32[8,16,256]{2,1,0:T(8,128)S(1)} async-done(((f32[8,16,256]{2,1,0:T(8,128)}), f32[8,16,256]{2,1,0:T(8,128)S(1)}, u32[]{:S(2)}, u32[]{:S(2)}) %all-to-all-start.2) | async-done | bytes 131104 | tf_op jit(solution)/shard_map/all_to_all | solution.py:19
  106.1 6.6 %all-to-all-start.3 = ((f32[8,16,256]{2,1,0:T(8,128)}), f32[8,16,256]{2,1,0:T(8,128)S(1)}, u32[]{:S(2)}, u32[]{:S(2)}) async-start(f32[8,16,256]{2,1,0:T(8,128)} %broadcast_in_dim.35), calls=%async_computation.3 | async-start | bytes 262144 | tf_op jit(solution)/shard_map/all_to_all | solution.py:19
  112.7 7.7 %fusion.19 = f32[2048,128]{1,0:T(8,128)} fusion(f32[2048,128]{1,0:T(8,128)} %fusion.17, bf16[2048,2048]{0,1:T(8,128)(2,1)} %get-tuple-element.49, f32[2048,128]{1,0:T(8,128)S(1)} %maximum_add_fusion, f32[2048]{0:T(1024)S(1)} %get-tuple-element.48, f32[2048]{0:T(1024)S(1)} %bitcast.93), kind=kOutput, calls=%fused_computation.29 | convolution fusion | flops 1075052544 | bytes 11550720 | tf_op jit(solution)/shard_map/dot_general | solution.py:27
  126.4 4.2 %collective-permute-done.7 = f32[512,128]{1,0:T(8,128)S(1)} collective-permute-done((f32[512,128]{1,0:T(8,128)S(1)}, f32[512,128]{1,0:T(8,128)S(1)}, u32[]{:S(2)}, u32[]{:S(2)}) %collective-permute-start.7) | collective-permute-done | bytes 262176 | tf_op jit(solution)/shard_map/ppermute | solution.py:15
  130.6 4.8 %collective-permute-done.6 = f32[512,128]{1,0:T(8,128)S(1)} collective-permute-done((f32[512,128]{1,0:T(8,128)S(1)}, f32[512,128]{1,0:T(8,128)S(1)}, u32[]{:S(2)}, u32[]{:S(2)}) %collective-permute-start.6) | collective-permute-done | bytes 262176 | tf_op jit(solution)/shard_map/ppermute | solution.py:15
  135.7 6.0 %fusion.25 = f32[2048,256]{1,0:T(8,128)S(1)} fusion(bf16[2048,2048]{0,1:T(8,128)(2,1)} %get-tuple-element.49, bf16[2048,128]{1,0:T(8,128)(2,1)S(1)} %get-tuple-element.19, bf16[2048,128]{1,0:T(8,128)(2,1)S(1)} %get-tuple-element.20), kind=kOutput, calls=%fused_computation.41 | convolution fusion | flops 2149580800 | bytes 11534336 | tf_op jit(solution)/shard_map/dot_general | solution.py:27
  143.8 2.7 collective-permute-start.9
  155.0 14.8 %all_to_all.50 = f32[8,16,384]{2,1,0:T(8,128)} all-to-all(f32[8,16,384]{2,1,0:T(8,128)} %bitcast.90), channel_id=1, replica_groups=mesh['sub'=8,'grp'=32] {'sub'}, dimensions={0} | all-to-all | bytes 393216 | tf_op jit(solution)/shard_map/all_to_all | solution.py:19
  171.4 7.0 %all_to_all.51 = f32[4,16,384]{2,1,0:T(8,128)S(1)} all-to-all(f32[4,16,384]{2,1,0:T(8,128)S(1)} %broadcast_in_dim.36), channel_id=1, replica_groups={{0,1,2,3},{4,5,6,7},{8,9,10,11},{12,13,14,15},{16,17,18,19},{20,21,22,2..., dimensions={0} | all-to-all | bytes 196608 | tf_op jit(solution)/shard_map/all_to_all | solution.py:19
  180.4 4.5 %all-to-all-start.6 = ((f32[8,16,384]{2,1,0:T(8,128)}), f32[8,16,384]{2,1,0:T(8,128)}, u32[]{:S(2)}, u32[]{:S(2)}) async-start(f32[8,16,384]{2,1,0:T(8,128)} %broadcast_in_dim.37), calls=%async_computation.6 | async-start | bytes 393216 | tf_op jit(solution)/shard_map/all_to_all | solution.py:19
  184.9 8.8 %all-to-all-done.6 = f32[8,16,384]{2,1,0:T(8,128)} async-done(((f32[8,16,384]{2,1,0:T(8,128)}), f32[8,16,384]{2,1,0:T(8,128)}, u32[]{:S(2)}, u32[]{:S(2)}) %all-to-all-start.6) | async-done | bytes 196640 | tf_op jit(solution)/shard_map/all_to_all | solution.py:19
  197.4 11.7 %all_to_all.52 = f32[8,16,384]{2,1,0:T(8,128)S(1)} all-to-all(f32[8,16,384]{2,1,0:T(8,128)S(1)} %broadcast_in_dim.39), channel_id=1, replica_groups=mesh['sub'=8,'grp'=32] {'sub'}, dimensions={0} | all-to-all | bytes 393216 | tf_op jit(solution)/shard_map/all_to_all | solution.py:19
  209.5 7.3 %fusion.21 = f32[2048,128]{1,0:T(8,128)S(1)} fusion(bf16[2048,2048]{0,1:T(8,128)(2,1)} %get-tuple-element.49, f32[2048,128]{1,0:T(8,128)S(1)} %multiply_subtract_fusion, f32[2048]{0:T(1024)} %copy-done.14, f32[2048]{0:T(1024)S(1)} %bitcast.97), kind=kOutput, calls=%fused_computation.31 | convolution fusion | flops 1075838976 | bytes 10502144 | tf_op jit(solution)/shard_map/dot_general | solution.py:27
  216.8 2.8 %fusion.23 = f32[2048,128]{1,0:T(8,128)S(1)} fusion(f32[2048,128]{1,0:T(8,128)S(1)} %fusion.21, bf16[2048,2048]{0,1:T(8,128)(2,1)S(1)} %bitcast.126, f32[2048,128]{1,0:T(8,128)S(1)} %multiply_subtract_fusion, f32[2048]{0:T(1024)S(1)} %copy-done.15, f32[2048]{0:T(1024)S(1)} %bitcast.98), kind=kOutput, calls=%fused_computation.33 | convolution fusion | flops 1075052544 | bytes 11550720 | tf_op jit(solution)/shard_map/dot_general | solution.py:27
  223.7 3.4 %collective-permute-done.15 = f32[512,128]{1,0:T(8,128)S(1)} collective-permute-done((f32[512,128]{1,0:T(8,128)S(1)}, f32[512,128]{1,0:T(8,128)S(1)}, u32[]{:S(2)}, u32[]{:S(2)}) %collective-permute-start.15) | collective-permute-done | bytes 262176 | tf_op jit(solution)/shard_map/ppermute | solution.py:15
  227.1 3.9 %collective-permute-done.14 = f32[512,128]{1,0:T(8,128)S(1)} collective-permute-done((f32[512,128]{1,0:T(8,128)S(1)}, f32[512,128]{1,0:T(8,128)S(1)}, u32[]{:S(2)}, u32[]{:S(2)}) %collective-permute-start.14) | collective-permute-done | bytes 262176 | tf_op jit(solution)/shard_map/ppermute | solution.py:15
  231.3 2.6 fusion.33
  235.2 9.2 %all_to_all.53 = f32[8,3,128]{2,1,0:T(4,128)S(1)} all-to-all(f32[8,3,128]{2,1,0:T(4,128)S(1)} %broadcast_in_dim.40), channel_id=1, replica_groups=mesh['sub'=8,'grp'=32] {'sub'}, dimensions={0} | all-to-all | bytes 24576 | tf_op jit(solution)/shard_map/all_to_all | solution.py:19
  245.1 4.3 %all-to-all-start.9 = ((f32[32,3,128]{2,1,0:T(4,128)}), f32[32,3,128]{2,1,0:T(4,128)S(1)}, u32[]{:S(2)}, u32[]{:S(2)}) async-start(f32[32,3,128]{2,1,0:T(4,128)} %broadcast_in_dim.41), calls=%async_computation.9 | async-start | bytes 131072 | tf_op jit(solution)/shard_map/all_to_all | solution.py:19
  251.5 4.6 %collective-permute-start.19 = (f32[512,128]{1,0:T(8,128)}, f32[512,128]{1,0:T(8,128)S(1)}, u32[]{:S(2)}, u32[]{:S(2)}) collective-permute-start(f32[512,128]{1,0:T(8,128)} %get-tuple-element.25), channel_id=1, source_target_pairs={{0,31},{1,0},{2,1},{3,2},{4,3},{5,4},{6,5},{7,6},{8,7},{9,8},{10,9... | collective-permute-start | bytes 786440 | tf_op jit(solution)/shard_map/ppermute | solution.py:15
  258.2 7.2 %scatter_custom_fusion = f32[2048,128]{1,0:T(8,128)} fusion(s32[2048]{0:T(1024)} %bitcast.102, f32[2048,128]{1,0:T(8,128)} %copy-done.6, f32[2048,128]{1,0:T(8,128)S(1)} %get-tuple-element.21, f32[128]{0:T(128)S(1)} %bitcast.116, f32[128]{0:T(128)S(1)} %get-tuple-element.10, f32[128]{0:T(128)S(1)} %get-tuple-element.9, f32[]{:T(128)} %constant.6.clone.1), kind=kCustom, calls=%fused_computation.68 | custom fusion | flops 1310720 | bytes 3147776 | tf_op jit(solution)/shard_map/scatter | solution.py:176
  266.0 8.0 %scatter_custom_fusion.1 = f32[2048,128]{1,0:T(8,128)} fusion(s32[2048]{0:T(1024)} %bitcast.103, f32[2048,128]{1,0:T(8,128)} %copy-done.5, f32[2048,128]{1,0:T(8,128)} %get-tuple-element.12, f32[512,128]{1,0:T(8,128)S(1)} %collective-permute-done.19, f32[]{:T(128)} %constant.30, f32[512,128]{1,0:T(8,128)} %collective-permute-done.18, ...), kind=kCustom, calls=%fused_computation.59 | custom fusion | flops 2097152 | bytes 5244928 | tf_op jit(solution)/shard_map/scatter | solution.py:176
  (150 shorter events, 45.1 us)
Async XLA Ops:
  12.5 36.8 %collective-permute-start.3 = (f32[516,128]{1,0:T(8,128)S(1)}, f32[516,128]{1,0:T(8,128)S(1)}, u32[]{:S(2)}, u32[]{:S(2)}) collective-permute-start(f32[516,128]{1,0:T(8,128)S(1)} %pad_maximum_fusion.3), channel_id=1, source_target_pairs={{0,31},{1,0},{2,1},{3,2},{4,3},{5,4},{6,5},{7,6},{8,7},{9,8},{10,9... | collective-permute-start | bytes 792584 | tf_op jit(solution)/shard_map/ppermute | solution.py:15
  21.4 27.9 %collective-permute-start.2 = (f32[516,128]{1,0:T(8,128)S(1)}, f32[516,128]{1,0:T(8,128)S(1)}, u32[]{:S(2)}, u32[]{:S(2)}) collective-permute-start(f32[516,128]{1,0:T(8,128)S(1)} %pad_maximum_fusion.2), channel_id=1, source_target_pairs={{0,1},{1,2},{2,3},{3,4},{4,5},{5,6},{6,7},{7,8},{8,9},{9,10},{10,1... | collective-permute-start | bytes 792584 | tf_op jit(solution)/shard_map/ppermute | solution.py:15
  21.8 27.5 %collective-permute-start.1 = (f32[516,128]{1,0:T(8,128)S(1)}, f32[516,128]{1,0:T(8,128)S(1)}, u32[]{:S(2)}, u32[]{:S(2)}) collective-permute-start(f32[516,128]{1,0:T(8,128)S(1)} %pad_maximum_fusion.1), channel_id=1, source_target_pairs={{0,224},{32,0},{64,32},{96,64},{128,96},{160,128},{192,160},{224,1... | collective-permute-start | bytes 792584 | tf_op jit(solution)/shard_map/ppermute | solution.py:15
  22.8 23.4 %copy-start.12 = (bf16[1,1,2048,256]{3,2,1,0:T(8,128)(2,1)S(1)}, bf16[1,1,2048,256]{3,2,1,0:T(8,128)(2,1)}, u32[]{:S(2)}) copy-start(bf16[1,1,2048,256]{3,2,1,0:T(8,128)(2,1)} %param.12) | copy-start | bytes 3145732
  22.8 26.5 %collective-permute-start = (f32[516,128]{1,0:T(8,128)S(1)}, f32[516,128]{1,0:T(8,128)S(1)}, u32[]{:S(2)}, u32[]{:S(2)}) collective-permute-start(f32[516,128]{1,0:T(8,128)S(1)} %pad_maximum_fusion), channel_id=1, source_target_pairs={{0,32},{32,64},{64,96},{96,128},{128,160},{160,192},{192,224},{224... | collective-permute-start | bytes 792584 | tf_op jit(solution)/shard_map/ppermute | solution.py:15
  49.2 71.2 %copy-start.2 = (bf16[2048,256]{1,0:T(8,128)(2,1)}, bf16[2048,256]{1,0:T(8,128)(2,1)S(1)}, u32[]{:S(2)}) copy-start(bf16[2048,256]{1,0:T(8,128)(2,1)S(1)} %fusion.13) | copy-start | bytes 3145732
  51.0 28.7 %all-to-all-start = ((f32[8,16,256]{2,1,0:T(8,128)}), f32[8,16,256]{2,1,0:T(8,128)S(1)}, u32[]{:S(2)}, u32[]{:S(2)}) async-start(f32[8,16,256]{2,1,0:T(8,128)} %bitcast.15), calls=%async_computation | async-start | bytes 262144 | tf_op jit(solution)/shard_map/all_to_all | solution.py:19
  56.5 23.1 %copy-start.13 = (s32[1,256]{1,0:T(1,128)S(1)}, s32[1,256]{1,0:T(1,128)}, u32[]{:S(2)}) copy-start(s32[1,256]{1,0:T(1,128)} %param.13) | copy-start | bytes 3076
  79.6 33.1 %copy-start.14 = (f32[2048]{0:T(1024)}, f32[2048]{0:T(1024)S(1)}, u32[]{:S(2)}) copy-start(f32[2048]{0:T(1024)S(1)} %get-tuple-element.48) | copy-start | bytes 24580
  80.5 11.2 %all-to-all-start.1 = ((f32[4,16,256]{2,1,0:T(8,128)}), f32[4,16,256]{2,1,0:T(8,128)S(1)}, u32[]{:S(2)}, u32[]{:S(2)}) async-start(f32[4,16,256]{2,1,0:T(8,128)} %broadcast_in_dim.33), calls=%async_computation.1 | async-start | bytes 131072 | tf_op jit(solution)/shard_map/all_to_all | solution.py:19
  92.4 12.5 %all-to-all-start.2 = ((f32[8,16,256]{2,1,0:T(8,128)}), f32[8,16,256]{2,1,0:T(8,128)S(1)}, u32[]{:S(2)}, u32[]{:S(2)}) async-start(f32[8,16,256]{2,1,0:T(8,128)} %broadcast_in_dim.34), calls=%async_computation.2 | async-start | bytes 262144 | tf_op jit(solution)/shard_map/all_to_all | solution.py:19
  106.1 14.4 %all-to-all-start.3 = ((f32[8,16,256]{2,1,0:T(8,128)}), f32[8,16,256]{2,1,0:T(8,128)S(1)}, u32[]{:S(2)}, u32[]{:S(2)}) async-start(f32[8,16,256]{2,1,0:T(8,128)} %broadcast_in_dim.35), calls=%async_computation.3 | async-start | bytes 262144 | tf_op jit(solution)/shard_map/all_to_all | solution.py:19
  122.2 8.4 %collective-permute-start.7 = (f32[512,128]{1,0:T(8,128)S(1)}, f32[512,128]{1,0:T(8,128)S(1)}, u32[]{:S(2)}, u32[]{:S(2)}) collective-permute-start(f32[512,128]{1,0:T(8,128)S(1)} %get-tuple-element.35), channel_id=1, source_target_pairs={{0,31},{1,0},{2,1},{3,2},{4,3},{5,4},{6,5},{7,6},{8,7},{9,8},{10,9... | collective-permute-start | bytes 786440 | tf_op jit(solution)/shard_map/ppermute | solution.py:15
  124.5 10.9 %collective-permute-start.6 = (f32[512,128]{1,0:T(8,128)S(1)}, f32[512,128]{1,0:T(8,128)S(1)}, u32[]{:S(2)}, u32[]{:S(2)}) collective-permute-start(f32[512,128]{1,0:T(8,128)S(1)} %get-tuple-element.36), channel_id=1, source_target_pairs={{0,1},{1,2},{2,3},{3,4},{4,5},{5,6},{6,7},{7,8},{8,9},{9,10},{10,1... | collective-permute-start | bytes 786440 | tf_op jit(solution)/shard_map/ppermute | solution.py:15
  124.5 10.9 %collective-permute-start.5 = (f32[512,128]{1,0:T(8,128)S(1)}, f32[512,128]{1,0:T(8,128)S(1)}, u32[]{:S(2)}, u32[]{:S(2)}) collective-permute-start(f32[512,128]{1,0:T(8,128)S(1)} %get-tuple-element.37), channel_id=1, source_target_pairs={{0,224},{32,0},{64,32},{96,64},{128,96},{160,128},{192,160},{224,1... | collective-permute-start | bytes 786440 | tf_op jit(solution)/shard_map/ppermute | solution.py:15
  124.8 10.6 %collective-permute-start.4 = (f32[512,128]{1,0:T(8,128)S(1)}, f32[512,128]{1,0:T(8,128)S(1)}, u32[]{:S(2)}, u32[]{:S(2)}) collective-permute-start(f32[512,128]{1,0:T(8,128)S(1)} %get-tuple-element.34), channel_id=1, source_target_pairs={{0,32},{32,64},{64,96},{96,128},{128,160},{160,192},{192,224},{224... | collective-permute-start | bytes 786440 | tf_op jit(solution)/shard_map/ppermute | solution.py:15
  142.3 6.8 %collective-permute-start.11 = (f32[512,128]{1,0:T(8,128)S(1)}, f32[512,128]{1,0:T(8,128)S(1)}, u32[]{:S(2)}, u32[]{:S(2)}) collective-permute-start(f32[512,128]{1,0:T(8,128)S(1)} %get-tuple-element.31), channel_id=1, source_target_pairs={{0,31},{1,0},{2,1},{3,2},{4,3},{5,4},{6,5},{7,6},{8,7},{9,8},{10,9... | collective-permute-start | bytes 786440 | tf_op jit(solution)/shard_map/ppermute | solution.py:15
  142.7 8.5 %collective-permute-start.10 = (f32[512,128]{1,0:T(8,128)S(1)}, f32[512,128]{1,0:T(8,128)S(1)}, u32[]{:S(2)}, u32[]{:S(2)}) collective-permute-start(f32[512,128]{1,0:T(8,128)S(1)} %get-tuple-element.32), channel_id=1, source_target_pairs={{0,1},{1,2},{2,3},{3,4},{4,5},{5,6},{6,7},{7,8},{8,9},{9,10},{10,1... | collective-permute-start | bytes 786440 | tf_op jit(solution)/shard_map/ppermute | solution.py:15
  143.8 7.5 %collective-permute-start.9 = (f32[512,128]{1,0:T(8,128)S(1)}, f32[512,128]{1,0:T(8,128)S(1)}, u32[]{:S(2)}, u32[]{:S(2)}) collective-permute-start(f32[512,128]{1,0:T(8,128)S(1)} %get-tuple-element.33), channel_id=1, source_target_pairs={{0,224},{32,0},{64,32},{96,64},{128,96},{160,128},{192,160},{224,1... | collective-permute-start | bytes 786440 | tf_op jit(solution)/shard_map/ppermute | solution.py:15
  146.5 4.8 %collective-permute-start.8 = (f32[512,128]{1,0:T(8,128)S(1)}, f32[512,128]{1,0:T(8,128)S(1)}, u32[]{:S(2)}, u32[]{:S(2)}) collective-permute-start(f32[512,128]{1,0:T(8,128)S(1)} %get-tuple-element.30), channel_id=1, source_target_pairs={{0,32},{32,64},{64,96},{96,128},{128,160},{160,192},{192,224},{224... | collective-permute-start | bytes 786440 | tf_op jit(solution)/shard_map/ppermute | solution.py:15
  180.4 13.3 %all-to-all-start.6 = ((f32[8,16,384]{2,1,0:T(8,128)}), f32[8,16,384]{2,1,0:T(8,128)}, u32[]{:S(2)}, u32[]{:S(2)}) async-start(f32[8,16,384]{2,1,0:T(8,128)} %broadcast_in_dim.37), calls=%async_computation.6 | async-start | bytes 393216 | tf_op jit(solution)/shard_map/all_to_all | solution.py:19
  209.5 24.4 %copy-start.5 = (f32[2048,128]{1,0:T(8,128)}, f32[2048,128]{1,0:T(8,128)S(1)}, u32[]{:S(2)}) copy-start(f32[2048,128]{1,0:T(8,128)S(1)} %multiply_subtract_fusion) | copy-start | bytes 3145732
  220.2 6.9 %collective-permute-start.15 = (f32[512,128]{1,0:T(8,128)S(1)}, f32[512,128]{1,0:T(8,128)S(1)}, u32[]{:S(2)}, u32[]{:S(2)}) collective-permute-start(f32[512,128]{1,0:T(8,128)S(1)} %get-tuple-element.27), channel_id=1, source_target_pairs={{0,31},{1,0},{2,1},{3,2},{4,3},{5,4},{6,5},{7,6},{8,7},{9,8},{10,9... | collective-permute-start | bytes 786440 | tf_op jit(solution)/shard_map/ppermute | solution.py:15
  220.9 10.1 %collective-permute-start.14 = (f32[512,128]{1,0:T(8,128)S(1)}, f32[512,128]{1,0:T(8,128)S(1)}, u32[]{:S(2)}, u32[]{:S(2)}) collective-permute-start(f32[512,128]{1,0:T(8,128)S(1)} %get-tuple-element.28), channel_id=1, source_target_pairs={{0,1},{1,2},{2,3},{3,4},{4,5},{5,6},{6,7},{7,8},{8,9},{9,10},{10,1... | collective-permute-start | bytes 786440 | tf_op jit(solution)/shard_map/ppermute | solution.py:15
  222.0 9.1 %collective-permute-start.13 = (f32[512,128]{1,0:T(8,128)S(1)}, f32[512,128]{1,0:T(8,128)S(1)}, u32[]{:S(2)}, u32[]{:S(2)}) collective-permute-start(f32[512,128]{1,0:T(8,128)S(1)} %get-tuple-element.29), channel_id=1, source_target_pairs={{0,224},{32,0},{64,32},{96,64},{128,96},{160,128},{192,160},{224,1... | collective-permute-start | bytes 786440 | tf_op jit(solution)/shard_map/ppermute | solution.py:15
  223.5 7.6 %collective-permute-start.12 = (f32[512,128]{1,0:T(8,128)S(1)}, f32[512,128]{1,0:T(8,128)S(1)}, u32[]{:S(2)}, u32[]{:S(2)}) collective-permute-start(f32[512,128]{1,0:T(8,128)S(1)} %get-tuple-element.26), channel_id=1, source_target_pairs={{0,32},{32,64},{64,96},{96,128},{128,160},{160,192},{192,224},{224... | collective-permute-start | bytes 786440 | tf_op jit(solution)/shard_map/ppermute | solution.py:15
  233.9 40.2 %copy-start.1 = (f32[1,1,2048,128]{3,2,1,0:T(8,128)S(1)}, f32[1,1,2048,128]{3,2,1,0:T(8,128)}, u32[]{:S(2)}) copy-start(f32[1,1,2048,128]{3,2,1,0:T(8,128)} %param.8) | copy-start | bytes 3145732
  245.1 13.1 %all-to-all-start.9 = ((f32[32,3,128]{2,1,0:T(4,128)}), f32[32,3,128]{2,1,0:T(4,128)S(1)}, u32[]{:S(2)}, u32[]{:S(2)}) async-start(f32[32,3,128]{2,1,0:T(4,128)} %broadcast_in_dim.41), calls=%async_computation.9 | async-start | bytes 131072 | tf_op jit(solution)/shard_map/all_to_all | solution.py:19
  251.5 13.9 %collective-permute-start.19 = (f32[512,128]{1,0:T(8,128)}, f32[512,128]{1,0:T(8,128)S(1)}, u32[]{:S(2)}, u32[]{:S(2)}) collective-permute-start(f32[512,128]{1,0:T(8,128)} %get-tuple-element.25), channel_id=1, source_target_pairs={{0,31},{1,0},{2,1},{3,2},{4,3},{5,4},{6,5},{7,6},{8,7},{9,8},{10,9... | collective-permute-start | bytes 786440 | tf_op jit(solution)/shard_map/ppermute | solution.py:15
  256.1 9.9 %collective-permute-start.18 = (f32[512,128]{1,0:T(8,128)}, f32[512,128]{1,0:T(8,128)}, u32[]{:S(2)}, u32[]{:S(2)}) collective-permute-start(f32[512,128]{1,0:T(8,128)} %get-tuple-element.23), channel_id=1, source_target_pairs={{0,1},{1,2},{2,3},{3,4},{4,5},{5,6},{6,7},{7,8},{8,9},{9,10},{10,1... | collective-permute-start | bytes 786440 | tf_op jit(solution)/shard_map/ppermute | solution.py:15
  256.2 9.9 %collective-permute-start.17 = (f32[512,128]{1,0:T(8,128)}, f32[512,128]{1,0:T(8,128)}, u32[]{:S(2)}, u32[]{:S(2)}) collective-permute-start(f32[512,128]{1,0:T(8,128)} %get-tuple-element.24), channel_id=1, source_target_pairs={{0,224},{32,0},{64,32},{96,64},{128,96},{160,128},{192,160},{224,1... | collective-permute-start | bytes 786440 | tf_op jit(solution)/shard_map/ppermute | solution.py:15
  257.7 8.3 %collective-permute-start.16 = (f32[512,128]{1,0:T(8,128)}, f32[512,128]{1,0:T(8,128)}, u32[]{:S(2)}, u32[]{:S(2)}) collective-permute-start(f32[512,128]{1,0:T(8,128)} %get-tuple-element.22), channel_id=1, source_target_pairs={{0,32},{32,64},{64,96},{96,128},{128,160},{160,192},{192,224},{224... | collective-permute-start | bytes 786440 | tf_op jit(solution)/shard_map/ppermute | solution.py:15
  (12 other events, 109.3 us)

commit v2 on v0

v2 whole, which is shorter than its diff:
```python
import functools

import jax
import jax.numpy as jnp
from jax import lax
from jax.experimental import pallas as pl
from jax.experimental.pallas import tpu as pltpu
from jax.sharding import PartitionSpec as P

LOCAL_STEPS = 2
HIGH = lax.Precision.HIGHEST
BF = jnp.bfloat16
F32 = jnp.float32
LANES = 128
GATHER = 32
CHUNK = 512
VM = pl.BlockSpec(memory_space=pltpu.VMEM)
SM = pl.BlockSpec(memory_space=pltpu.SMEM)


def shape(*dims, kind=F32):
    return jax.ShapeDtypeStruct(dims, kind)


def kernel(body, operands, outs, scratch=(), limit=40, scalars=1, flops=0):
    specs = [SM] * scalars + [VM] * (len(operands) - scalars)
    moved = sum(value.size * value.dtype.itemsize for value in (*operands, *outs))
    return pl.pallas_call(
        body,
        out_shape=list(outs),
        in_specs=specs,
        out_specs=[VM] * len(outs),
        scratch_shapes=list(scratch),
        compiler_params=pltpu.CompilerParams(vmem_limit_bytes=limit << 20),
        cost_estimate=pl.CostEstimate(flops=flops, bytes_accessed=moved, transcendentals=0),
        name=body.func.__name__ if isinstance(body, functools.partial) else body.__name__,
    )(*operands)


def dot(first, second, contract, precision=None):
    return lax.dot_general(
        first, second, (contract, ((), ())), precision=precision, preferred_element_type=F32
    )


def eye():
    return (
        lax.broadcasted_iota(jnp.int32, (LANES, LANES), 0)
        == lax.broadcasted_iota(jnp.int32, (LANES, LANES), 1)
    )


def to_column(row):
    column = jnp.sum(jnp.where(eye(), jnp.broadcast_to(row, (LANES, LANES)), 0.0), axis=1, keepdims=True)
    return jnp.broadcast_to(column, (LANES, LANES))


def to_row(block):
    return jnp.sum(jnp.where(eye(), block, 0.0), axis=0, keepdims=True)


def gather_rows(order, start, count, pairs):
    @pl.loop(0, count // GATHER)
    def _(step):
        base = pl.multiple_of(step * GATHER, GATHER)
        picks = [order[0, start + base + k] for k in range(GATHER)]
        for source, target in pairs:
            target[pl.ds(base, GATHER), :] = jnp.concatenate(
                [source[pl.ds(pick, 1), :] for pick in picks], axis=0
            )


def scatter_rows(order, start, count, pairs):
    @pl.loop(0, count // GATHER)
    def _(step):
        base = pl.multiple_of(step * GATHER, GATHER)
        picks = [order[0, start + base + k] for k in range(GATHER)]
        for source, target in pairs:
            rows = source[pl.ds(base, GATHER), :]
            for k, pick in enumerate(picks):
                target[pl.ds(pick, 1), :] = rows[k : k + 1]


def chunked(rows, work):
    for start in range(0, rows, CHUNK):
        work(pl.ds(start, CHUNK))


def spread_stiff(stiff, target):
    for start in range(0, target.shape[0], LANES):
        target[pl.ds(start, LANES), :] = to_column(stiff[:, pl.ds(start, LANES)])


def split(value):
    top = value.astype(BF)
    return top, (value - top.astype(F32)).astype(BF)


def membership_table(members, levels):
    rows = lax.broadcasted_iota(jnp.int32, (levels, members.shape[1]), 0)
    return (rows == members[...]).astype(F32)


def open_faces(order, rhs, stiff, *rest):
    blocks, (own_stiff, face_stiff) = rest[:4], rest[4:]
    face = rhs.shape[0] // 4
    spread_stiff(stiff, own_stiff)
    for k, block in enumerate(blocks):
        gather_rows(order, k * face, face, [(rhs, block), (own_stiff, face_stiff)])
        block[pl.ds(face, block.shape[0] - face), :] = jnp.concatenate(
            [to_row(face_stiff[pl.ds(t, LANES), :]) for t in range(0, face, LANES)]
            + [jnp.zeros((block.shape[0] - face - face // LANES, LANES), F32)],
            axis=0,
        )


def open_join(order, rhs, stiff, one, two, three, four, basis, residual, weight, weighted, partial, other, face_stiff):
    face = rhs.shape[0] // 4
    for k, block in enumerate((one, two, three, four)):
        for t in range(face // LANES):
            face_stiff[pl.ds(t * LANES, LANES), :] = to_column(block[pl.ds(face + t, 1), :])
        scatter_rows(order, k * face, face, [(block, residual), (face_stiff, other)])
    spread_stiff(stiff, weight)
    residual[...] = rhs[...] + residual[...]
    weight[...] = weight[...] / (weight[...] + other[...])
    weighted[...] = weight[...] * residual[...]
    partial[...] = dot(weighted[...].astype(BF), basis[...], ((0,), (0,)))


def sweeps(matrix, weighted, diagonal, fix, narrow):
    fix[...] = weighted[...] / diagonal[...]
    for _ in range(LOCAL_STEPS):
        narrow[...] = fix[...].astype(BF)

        def work(rows):
            product = dot(matrix[rows, :], narrow[...], ((1,), (0,)))
            fix[rows, :] = fix[rows, :] + (weighted[rows, :] - product) / diagonal[rows, :]

        chunked(matrix.shape[0], work)


def first_fix(matrix, weighted, fix, diagonal, narrow):
    for start in range(0, matrix.shape[0], LANES):
        square = matrix[pl.ds(start, LANES), pl.ds(start, LANES)].astype(F32)
        column = jnp.sum(jnp.where(eye(), square, 0.0), axis=1, keepdims=True)
        diagonal[pl.ds(start, LANES), :] = jnp.broadcast_to(column, (LANES, LANES))
    sweeps(matrix, weighted, diagonal, fix, narrow)


def add_coarse(basis, coarse, weight, fix, local):
    narrow = coarse.astype(BF)

    def work(rows):
        correction = dot(basis[rows, :], narrow, ((1,), (1,)))
        local[rows, :] = weight[rows, :] * (fix[rows, :] + correction)

    chunked(basis.shape[0], work)


def send_faces(order, source, blocks):
    face = source.shape[0] // 4
    for k, block in enumerate(blocks):
        gather_rows(order, k * face, face, [(source, block)])


def first_local(order, weight, fix, basis, coarse, local, *blocks):
    add_coarse(basis, coarse[...], weight, fix, local)
    send_faces(order, local, blocks)


def apply_schur(matrix, vector, product, wide):
    wide[:, :LANES], wide[:, LANES:] = split(vector[...])

    def work(rows):
        both = dot(matrix[rows, :], wide[...], ((1,), (0,)))
        product[rows, :] = both[:, :LANES] + both[:, LANES:]

    chunked(matrix.shape[0], work)


def column_sum(first, second):
    return jnp.sum(first[...] * second[...], axis=0, keepdims=True)


def first_apply(order, matrix, local, residual, one, two, three, four, z_value, product, dots, *rest):
    blocks, wide = rest[:4], rest[4]
    face = local.shape[0] // 4
    for k, block in enumerate((one, two, three, four)):
        scatter_rows(order, k * face, face, [(block, z_value)])
    z_value[...] = local[...] + z_value[...]
    apply_schur(matrix, z_value, product, wide)
    send_faces(order, product, blocks)
    dots[...] = jnp.concatenate(
        [0.5 * column_sum(residual, z_value), column_sum(z_value, product), jnp.zeros((6, LANES), F32)], axis=0
    )


def image_partial(order, product, weight, one, two, three, four, basis, dots, image, payload, wide):
    face = product.shape[0] // 4
    for k, block in enumerate((one, two, three, four)):
        scatter_rows(order, k * face, face, [(block, image)])
    image[...] = product[...] + image[...]
    wide[:, :LANES], wide[:, LANES:] = split(weight[...] * image[...])
    both = dot(wide[...], basis[...], ((0,), (0,)))
    coarse = basis.shape[1]
    payload[:, :coarse] = both[:LANES] + both[LANES:]
    square = jnp.concatenate([dots[...], jnp.zeros((LANES - 8, LANES), F32)], axis=0)
    payload[:, coarse:] = square.T


def group_level(chunks, members, total, copies, *, levels):
    value = jnp.sum(chunks[...], axis=0)
    total[...] = value
    coarse = members.shape[1]
    copies[0, :, :levels] = dot(value[:, :coarse], membership_table(members, levels), ((1,), (1,)), HIGH)
    if value.shape[1] > coarse:
        copies[0, :, levels:] = value[:, coarse:]
    for k in range(1, copies.shape[0]):
        copies[k] = copies[0]


def add_and_copy(chunks, copies):
    value = jnp.sum(chunks[...], axis=0)
    for k in range(copies.shape[0]):
        copies[k] = value


def coarse_solve(total, two, members, inverse_one, inverse_two):
    solved = dot(two, inverse_two[...], ((1,), (1,)), HIGH)
    table = membership_table(members, inverse_two.shape[0])
    return dot(total, inverse_one[...], ((1,), (1,)), HIGH) + dot(solved, table, ((1,), (0,)), HIGH)


def first_coarse(chunks, total, members, inverse_one, inverse_two, two, copies):
    two[...] = jnp.sum(chunks[...], axis=0)
    value = coarse_solve(total[...], two[...], members, inverse_one, inverse_two)
    for k in range(copies.shape[0]):
        copies[k] = value


def second_coarse(chunks, total_q, total, two, members, inverse_one, inverse_two, copies):
    levels, coarse = inverse_two.shape[0], members.shape[1]
    value = jnp.sum(chunks[...], axis=0)
    dots = value[:, levels:]
    step = dots[:, 0:1] / dots[:, 1:2]
    solved = coarse_solve(
        total[...] - step * total_q[:, :coarse], two[...] - step * value[:, :levels], members, inverse_one, inverse_two
    )
    dots = jnp.where(lax.broadcasted_iota(jnp.int32, dots.shape, 1) == 2, step, dots)
    for k in range(copies.shape[0]):
        copies[k, :, :coarse] = solved
        copies[k, :, coarse:] = dots


def second_local(order, matrix, diagonal, weight, basis, residual, image, coarse, residual_out, local, info, *rest):
    blocks, (weighted, fix, narrow) = rest[:4], rest[4:]
    levels = basis.shape[1]
    rows = coarse[:, levels:].T
    info[...] = rows[:8]
    residual_out[...] = residual[...] - rows[2:3] * image[...]
    weighted[...] = weight[...] * residual_out[...]
    sweeps(matrix, weighted, diagonal, fix, narrow)
    add_coarse(basis, coarse[:, :levels], weight, fix, local)
    send_faces(order, local, blocks)


def second_apply(order, matrix, local, residual, z_first, one, two, three, four, z_value, product, copies, *rest):
    blocks, wide = rest[:4], rest[4]
    face = local.shape[0] // 4
    for k, block in enumerate((one, two, three, four)):
        scatter_rows(order, k * face, face, [(block, z_value)])
    z_value[...] = local[...] + z_value[...]
    apply_schur(matrix, z_value, product, wide)
    send_faces(order, product, blocks)
    dots = jnp.concatenate(
        [
            0.5 * column_sum(residual, z_value),
            column_sum(z_value, product),
            column_sum(z_first, product),
            jnp.zeros((5, LANES), F32),
        ],
        axis=0,
    )
    for k in range(copies.shape[0]):
        copies[k] = dots


def last_image(order, product, one, two, three, four, image):
    face = product.shape[0] // 4
    for k, block in enumerate((one, two, three, four)):
        scatter_rows(order, k * face, face, [(block, image)])
    image[...] = product[...] + image[...]


def finish(chunks, info, z_first, z_second, image_first, image_second, residual, solution_out, residual_out):
    dots = jnp.sum(chunks[...], axis=0)
    rz_first, step_first = info[0:1], info[2:3]
    rz = dots[0:1]
    ratio = rz / rz_first
    step = rz / (dots[1:2] + 2.0 * ratio * dots[2:3] + ratio * ratio * info[1:2])
    solution_out[...] = step_first * z_first[...] + step * (z_second[...] + ratio * z_first[...])
    residual_out[...] = residual[...] - step * (image_second[...] + ratio * image_first[...])


def passed_along(value, axis, steps):
    count = lax.axis_size(axis)
    pairs = [(source, (source + steps) % count) for source in range(count)]
    return lax.ppermute(value, axis, pairs)


def exchanged(blocks):
    return [
        passed_along(blocks[1], "sub", 1),
        passed_along(blocks[0], "sub", -1),
        passed_along(blocks[3], "grp", 1),
        passed_along(blocks[2], "grp", -1),
    ]


def spread(chunks, axis, groups=None):
    return lax.all_to_all(chunks, axis, 0, 0, axis_index_groups=groups)


def body(rhs, schur, stiff, face_index, basis, membership, level1_inv, level2_inv):
    matrix, rhs, basis = schur[0, 0], rhs[0, 0], basis[0, 0]
    order, stiff, members, inverse_one = face_index[0], stiff[0], membership, level1_inv[0]
    dofs, cols = rhs.shape
    face = dofs // 4
    coarse, levels = inverse_one.shape[0], level2_inv.shape[0]
    n_sub, n_grp = lax.axis_size("sub"), lax.axis_size("grp")
    inner = 4
    outer = n_grp // inner
    groups_y = [[z * inner + y for y in range(inner)] for z in range(outer)]
    groups_z = [[z * inner + y for z in range(outer)] for y in range(inner)]
    share = cols // n_sub
    vector, block = shape(dofs, cols), shape(face, cols)
    face_rows = face + -(-face // LANES // 8) * 8
    product_flops = 2 * dofs * dofs * cols
    wide, narrow = pltpu.VMEM((dofs, 2 * cols), BF), pltpu.VMEM((dofs, cols), BF)

    blocks = kernel(
        open_faces,
        (order, rhs, stiff),
        [shape(face_rows, cols)] * 4,
        [pltpu.VMEM((dofs, cols), F32), pltpu.VMEM((face, cols), F32)],
    )
    residual0, weight, weighted, partial = kernel(
        open_join,
        (order, rhs, stiff, *exchanged(blocks), basis),
        [vector, vector, vector, shape(cols, coarse)],
        [pltpu.VMEM((dofs, cols), F32), pltpu.VMEM((face, cols), F32)],
    )

    def to_groups(value):
        chunks = spread(value.reshape(n_sub, share, value.shape[1]), "sub")
        width = value.shape[1]
        out = width - coarse + levels
        total, copies = kernel(
            functools.partial(group_level, levels=levels),
            (chunks, members),
            [shape(share, width), shape(inner, share, out)],
            scalars=0,
        )
        chunks = spread(copies, "grp", groups_y)
        (copies,) = kernel(add_and_copy, (chunks,), [shape(outer, share, out)], scalars=0)
        return total, spread(copies, "grp", groups_z)

    def from_groups(copies):
        return spread(copies, "sub").reshape(cols, copies.shape[2])

    total0, chunks = to_groups(partial)
    two0, copies = kernel(
        first_coarse,
        (chunks, total0, members, inverse_one, level2_inv),
        [shape(share, levels), shape(n_sub, share, coarse)],
        scalars=0,
    )
    coarse0 = from_groups(copies)
    fix, diagonal = kernel(
        first_fix, (matrix, weighted), [vector, vector], [narrow], scalars=0, flops=2 * product_flops
    )
    local, *blocks = kernel(first_local, (order, weight, fix, basis, coarse0), [vector] + [block] * 4)

    z0, product0, dots, *blocks = kernel(
        first_apply,
        (order, matrix, local, residual0, *exchanged(blocks)),
        [vector, vector, shape(8, cols)] + [block] * 4,
        [wide],
        flops=product_flops,
    )
    image0, payload = kernel(
        image_partial,
        (order, product0, weight, *exchanged(blocks), basis, dots),
        [vector, shape(cols, coarse + cols)],
        [wide],
    )
    total_q, chunks = to_groups(payload)
    (copies,) = kernel(
        second_coarse,
        (chunks, total_q, total0, two0, members, inverse_one, level2_inv),
        [shape(n_sub, share, coarse + cols)],
        scalars=0,
    )
    coarse1 = from_groups(copies)
    residual1, local, info, *blocks = kernel(
        second_local,
        (order, matrix, diagonal, weight, basis, residual0, image0, coarse1),
        [vector, vector, shape(8, cols)] + [block] * 4,
        [pltpu.VMEM((dofs, cols), F32), pltpu.VMEM((dofs, cols), F32), narrow],
        flops=2 * product_flops,
    )
    z1, product1, copies, *blocks = kernel(
        second_apply,
        (order, matrix, local, residual1, z0, *exchanged(blocks)),
        [vector, vector, shape(n_sub, 8, cols)] + [block] * 4,
        [wide],
        flops=product_flops,
    )
    arrived = exchanged(blocks)
    (copies,) = kernel(add_and_copy, (spread(copies, "sub"),), [shape(n_grp, 8, cols)], scalars=0)
    chunks = spread(copies, "grp")
    (image1,) = kernel(last_image, (order, product1, *arrived), [vector])
    outs = kernel(
        finish, (chunks, info, z0, z1, image0, image1, residual1), [vector, vector], scalars=0
    )
    return outs[0][None, None], outs[1][None, None]


def solution(mesh):
    placed = (
        P("grp", "sub", None, None),
        P("grp", "sub", None, None),
        P("grp", "sub", None),
        P("grp", "sub", None),
        P("grp", "sub", None, None),
        P("grp", None),
        P("grp", None, None),
        P(),
    )
    return jax.shard_map(
        body,
        mesh=mesh,
        in_specs=placed,
        out_specs=(P("grp", "sub", None, None), P("grp", "sub", None, None)),
        check_vma=False,
    )
```

time: 921 us -> 242 us (0.26)
  waiting for transfers between devices: 389 us -> 19.7 us
  blocking collectives: 228 us -> 76.7 us
  local copies, waits for them, and re-layouts: 117 us -> 27.7 us
  matrix products: 60.3 us -> 0 us
  Pallas kernels: 0 us -> 59.6 us
  other arithmetic: 51.8 us -> 0 us
  between operations: 14.5 us -> 0.89 us
    psum x4 -> x0, waiting for transfers between devices: 365 us -> none  [the longest x2 264 us: precondition(): lax.psum(jnp.dot(aggregation, group_total, precision=high), 'grp')]
    psum x3 -> x0, blocking collectives: 228 us -> none  [inner(): totals = lax.psum(local_terms, ('sub', 'grp'))]
    gather x7 -> x0, local copies, waits for them, and re-layouts: 78 us -> none  [the longest x6 46 us: incoming(): vector[face_order].reshape(4, face_size, vector.shape[1])]
    all_to_all x0 -> x7, blocking collectives: none -> 76.7 us  [spread(): return lax.all_to_all(chunks, axis, 0, 0, axis_index_groups=groups)]
    dot_general x18 -> x0, matrix products: 60.3 us -> none  [the longest x6 44.7 us: schur_times(): jnp.dot(matrix, vector.astype(jnp.bfloat16), preferred_element_type=jnp.f...]
    pallas_call x0 -> x17, Pallas kernels: none -> 59.6 us  [kernel(): pl.pallas_call(body, out_shape=list(outs), in_specs=specs, out_specs=[VM]...]
    scatter x5 -> x0, other arithmetic: 35 us -> none  [incoming(): placed.append(jnp.zeros_like(vector).at[face_order].set(arrived))]
    all_to_all x0 -> x3, starting transfers between devices: none -> 19.1 us  [spread(): return lax.all_to_all(chunks, axis, 0, 0, axis_index_groups=groups)]
  transfers between devices with their start and end apart: 28 -> 23, of which waited for: 8 -> 8; matrix products, arithmetic and copies ran while one was open for 8% -> 0% of each run, Pallas kernels for 0% -> 3%
where the time goes in v2:
time: 242 us; the launch traced here: 241 us
  blocking collectives  76.7 us (32%)
  Pallas kernels  59.6 us (25%)
  starting transfers between devices  56.8 us (23%)
  local copies, waits for them, and re-layouts  27.7 us (11%)
  waiting for transfers between devices  19.7 us (8%)
    all_to_all x7, blocking collectives, spread(): return lax.all_to_all(chunks, axis, 0, 0, axis_index_groups=groups)  76.7 us
    pallas_call x17, Pallas kernels, kernel(): pl.pallas_call(body, out_shape=list(outs), in_specs=specs, out_specs=[VM]...  59.6 us
    ppermute x20, starting transfers between devices, passed_along(): return lax.ppermute(value, axis, pairs)  37.7 us
    unnamed x74, local copies, waits for them, and re-layouts  27.7 us
    all_to_all x3, starting transfers between devices, spread(): return lax.all_to_all(chunks, axis, 0, 0, axis_index_groups=groups)  19.1 us
    ppermute x20, waiting for transfers between devices, passed_along(): return lax.ppermute(value, axis, pairs)  18 us
  transfers between devices with their start and end apart: 23, of which 8 were waited for; matrix products, arithmetic and copies ran while one was open for 0% of the time, Pallas kernels for 3%

profile of v2, /device:TPU:1, one launch (start us, length us, event | category | flops | bytes accessed | tf_op | source)
XLA Modules:
  0.0 241.2 jit_solution(452408370859904095)
XLA Ops:
  3.4 4.5 %open_faces.1 = (f32[520,128]{1,0:T(8,128)S(1)}, f32[520,128]{1,0:T(8,128)S(1)}, f32[520,128]{1,0:T(8,128)S(1)}, f32[520,128]{1,0:T(8,128)S(1)}) custom-call(s32[1,2048]{1,0:T(1,128)S(1)} %bitcast.26, f32[2048,128]{1,0:T(8,128)S(1)} %bitcast.20, f32[1,2048]{1,0:T(1,128)S(1)} %bitcast.36), custom_call_target="tpu_custom_call" | custom-call | bytes 2129920 | tf_op jit(solution)/shard_map/open_faces/pallas_call | solution.py:28
  7.8 2.6 %collective-permute-start = (f32[520,128]{1,0:T(8,128)S(1)}, f32[520,128]{1,0:T(8,128)S(1)}, u32[]{:S(2)}, u32[]{:S(2)}) collective-permute-start(f32[520,128]{1,0:T(8,128)S(1)} %get-tuple-element.48), channel_id=1, source_target_pairs={{0,32},{32,64},{64,96},{96,128},{128,160},{160,192},{192,224},{224... | collective-permute-start | bytes 798728 | tf_op jit(solution)/shard_map/ppermute | solution.py:308
  11.8 6.7 %collective-permute-start.3 = (f32[520,128]{1,0:T(8,128)S(1)}, f32[520,128]{1,0:T(8,128)S(1)}, u32[]{:S(2)}, u32[]{:S(2)}) collective-permute-start(f32[520,128]{1,0:T(8,128)S(1)} %get-tuple-element.51), channel_id=1, source_target_pairs={{0,31},{1,0},{2,1},{3,2},{4,3},{5,4},{6,5},{7,6},{8,7},{9,8},{10,9... | collective-permute-start | bytes 798728 | tf_op jit(solution)/shard_map/ppermute | solution.py:308
  18.5 4.8 %collective-permute-done.2.three = f32[520,128]{1,0:T(8,128)S(1)} collective-permute-done((f32[520,128]{1,0:T(8,128)S(1)}, f32[520,128]{1,0:T(8,128)S(1)}, u32[]{:S(2)}, u32[]{:S(2)}) %collective-permute-start.2) | collective-permute-done | bytes 266272 | tf_op jit(solution)/shard_map/ppermute | solution.py:308
  24.6 4.3 %open_join.1 = (f32[2048,128]{1,0:T(8,128)S(1)}, f32[2048,128]{1,0:T(8,128)S(1)}, f32[2048,128]{1,0:T(8,128)S(1)}, f32[128,256]{1,0:T(8,128)S(1)}) custom-call(s32[1,2048]{1,0:T(1,128)S(1)} %bitcast.27, f32[2048,128]{1,0:T(8,128)S(1)} %bitcast.21, f32[1,2048]{1,0:T(1,128)S(1)} %bitcast.37, f32[520,128]{1,0:T(8,128)S(1)} %collective-permute-done.one, ...), custom_call_target="tpu_custom_call" | custom-call | bytes 6455296 | tf_op jit(solution)/shard_map/open_join/pallas_call | solution.py:28
  29.9 11.6 %all_to_all.50.chunks = f32[8,16,256]{2,1,0:T(8,128)S(1)} all-to-all(f32[8,16,256]{2,1,0:T(8,128)S(1)} %bitcast.35), channel_id=1, replica_groups=mesh['sub'=8,'grp'=32] {'sub'}, dimensions={0} | all-to-all | bytes 262144 | tf_op jit(solution)/shard_map/all_to_all | solution.py:321
  42.4 6.8 %all_to_all.51.chunks = f32[4,16,256]{2,1,0:T(8,128)S(1)} all-to-all(f32[4,16,256]{2,1,0:T(8,128)S(1)} %get-tuple-element.58), channel_id=1, replica_groups={{0,1,2,3},{4,5,6,7},{8,9,10,11},{12,13,14,15},{16,17,18,19},{20,21,22,2..., dimensions={0} | all-to-all | bytes 131072 | tf_op jit(solution)/shard_map/all_to_all | solution.py:321
  49.3 14.1 %all_to_all.52.chunks = f32[8,16,256]{2,1,0:T(8,128)S(1)} all-to-all(f32[8,16,256]{2,1,0:T(8,128)S(1)} %add_and_copy.3), channel_id=1, replica_groups={{0,4,8,12,16,20,24,28},{1,5,9,13,17,21,25,29},{2,6,10,14,18,22,26,30},{..., dimensions={0} | all-to-all | bytes 262144 | tf_op jit(solution)/shard_map/all_to_all | solution.py:321
  65.3 1.8 first_coarse.1
  67.1 6.9 %all-to-all-start.3 = ((f32[8,16,256]{2,1,0:T(8,128)}), f32[8,16,256]{2,1,0:T(8,128)S(1)}, u32[]{:S(2)}, u32[]{:S(2)}) async-start(f32[8,16,256]{2,1,0:T(8,128)} %get-tuple-element.60), calls=%async_computation.3 | async-start | bytes 262144 | tf_op jit(solution)/shard_map/all_to_all | solution.py:321
  74.0 3.4 %copy-done = bf16[1,1,2048,2048]{3,2,1,0:T(8,128)(2,1)S(1)} copy-done((bf16[1,1,2048,2048]{3,2,1,0:T(8,128)(2,1)S(1)}, bf16[1,1,2048,2048]{3,2,1,0:T(8,128)(2,1)}, u32[]{:S(2)}) %copy-start) | copy-done | bytes 8388632
  78.6 4.6 %first_fix.1 = (f32[2048,128]{1,0:T(8,128)S(1)}, f32[2048,128]{1,0:T(8,128)S(1)}) custom-call(bf16[2048,2048]{1,0:T(8,128)(2,1)S(1)} %bitcast.15, f32[2048,128]{1,0:T(8,128)S(1)} %copy-done.13), custom_call_target="tpu_custom_call" | custom-call | flops 2147483648 | bytes 11534336 | tf_op jit(solution)/shard_map/first_fix/pallas_call | solution.py:28
  86.5 3.1 %first_local.1 = (f32[2048,128]{1,0:T(8,128)S(1)}, f32[512,128]{1,0:T(8,128)S(1)}, f32[512,128]{1,0:T(8,128)S(1)}, f32[512,128]{1,0:T(8,128)S(1)}, f32[512,128]{1,0:T(8,128)S(1)}) custom-call(s32[1,2048]{1,0:T(1,128)S(1)} %bitcast.28, f32[2048,128]{1,0:T(8,128)S(1)} %get-tuple-element.54.weight, f32[2048,128]{1,0:T(8,128)S(1)} %copy-done.15, ...), custom_call_target="tpu_custom_call" | custom-call | bytes 5382144 | tf_op jit(solution)/shard_map/first_local/pallas_call | solution.py:28
  91.5 4.5 %collective-permute-start.7 = (f32[512,128]{1,0:T(8,128)S(1)}, f32[512,128]{1,0:T(8,128)S(1)}, u32[]{:S(2)}, u32[]{:S(2)}) collective-permute-start(f32[512,128]{1,0:T(8,128)S(1)} %get-tuple-element.65), channel_id=1, source_target_pairs={{0,31},{1,0},{2,1},{3,2},{4,3},{5,4},{6,5},{7,6},{8,7},{9,8},{10,9... | collective-permute-start | bytes 786440 | tf_op jit(solution)/shard_map/ppermute | solution.py:308
  97.3 3.6 %collective-permute-done.6.three = f32[512,128]{1,0:T(8,128)S(1)} collective-permute-done((f32[512,128]{1,0:T(8,128)S(1)}, f32[512,128]{1,0:T(8,128)S(1)}, u32[]{:S(2)}, u32[]{:S(2)}) %collective-permute-start.6) | collective-permute-done | bytes 262176 | tf_op jit(solution)/shard_map/ppermute | solution.py:308
  100.9 10.2 %first_apply.1 = (f32[2048,128]{1,0:T(8,128)S(1)}, f32[2048,128]{1,0:T(8,128)S(1)}, f32[8,128]{1,0:T(8,128)S(1)}, f32[512,128]{1,0:T(8,128)S(1)}, f32[512,128]{1...) custom-call(s32[1,2048]{1,0:T(1,128)S(1)} %bitcast.29, bf16[2048,2048]{1,0:T(8,128)(2,1)} %bitcast.12, ...), custom_call_target="tpu_custom_call" | custom-call | flops 1073741824 | bytes 14692352 | tf_op jit(solution)/shard_map/first_apply/pallas_call | solution.py:28
  111.1 3.4 %collective-permute-start.8 = (f32[512,128]{1,0:T(8,128)S(1)}, f32[512,128]{1,0:T(8,128)S(1)}, u32[]{:S(2)}, u32[]{:S(2)}) collective-permute-start(f32[512,128]{1,0:T(8,128)S(1)} %get-tuple-element.67), channel_id=1, source_target_pairs={{0,32},{32,64},{64,96},{96,128},{128,160},{160,192},{192,224},{224... | collective-permute-start | bytes 786440 | tf_op jit(solution)/shard_map/ppermute | solution.py:308
  114.5 4.8 %collective-permute-start.11 = (f32[512,128]{1,0:T(8,128)S(1)}, f32[512,128]{1,0:T(8,128)S(1)}, u32[]{:S(2)}, u32[]{:S(2)}) collective-permute-start(f32[512,128]{1,0:T(8,128)S(1)} %get-tuple-element.70), channel_id=1, source_target_pairs={{0,31},{1,0},{2,1},{3,2},{4,3},{5,4},{6,5},{7,6},{8,7},{9,8},{10,9... | collective-permute-start | bytes 786440 | tf_op jit(solution)/shard_map/ppermute | solution.py:308
  120.6 3.1 %collective-permute-done.10.three = f32[512,128]{1,0:T(8,128)S(1)} collective-permute-done((f32[512,128]{1,0:T(8,128)S(1)}, f32[512,128]{1,0:T(8,128)S(1)}, u32[]{:S(2)}, u32[]{:S(2)}) %collective-permute-start.10) | collective-permute-done | bytes 262176 | tf_op jit(solution)/shard_map/ppermute | solution.py:308
  123.8 3.2 %image_partial.1 = (f32[2048,128]{1,0:T(8,128)S(1)}, f32[128,384]{1,0:T(8,128)S(1)}) custom-call(s32[1,2048]{1,0:T(1,128)S(1)} %bitcast.30, f32[2048,128]{1,0:T(8,128)S(1)} %get-tuple-element.66.product, f32[2048,128]{1,0:T(8,128)S(1)} %get-tuple-element.54.weight, f32[512,128]{1,0:T(8,128)S(1)} %collective-permute-done.8.one, ...), custom_call_target="tpu_custom_call" | custom-call | bytes 5451776 | tf_op jit(solution)/shard_map/image_partial/pallas_call | solution.py:28
  127.0 11.5 %all_to_all.53.chunks = f32[8,16,384]{2,1,0:T(8,128)S(1)} all-to-all(f32[8,16,384]{2,1,0:T(8,128)S(1)} %bitcast.34), channel_id=1, replica_groups=mesh['sub'=8,'grp'=32] {'sub'}, dimensions={0} | all-to-all | bytes 393216 | tf_op jit(solution)/shard_map/all_to_all | solution.py:321
  138.8 7.0 %all_to_all.54.chunks = f32[4,16,384]{2,1,0:T(8,128)S(1)} all-to-all(f32[4,16,384]{2,1,0:T(8,128)S(1)} %get-tuple-element.74), channel_id=1, replica_groups={{0,1,2,3},{4,5,6,7},{8,9,10,11},{12,13,14,15},{16,17,18,19},{20,21,22,2..., dimensions={0} | all-to-all | bytes 196608 | tf_op jit(solution)/shard_map/all_to_all | solution.py:321
  145.9 13.6 %all_to_all.55.chunks = f32[8,16,384]{2,1,0:T(8,128)S(1)} all-to-all(f32[8,16,384]{2,1,0:T(8,128)S(1)} %add_and_copy.4), channel_id=1, replica_groups={{0,4,8,12,16,20,24,28},{1,5,9,13,17,21,25,29},{2,6,10,14,18,22,26,30},{..., dimensions={0} | all-to-all | bytes 393216 | tf_op jit(solution)/shard_map/all_to_all | solution.py:321
  160.7 12.0 %all_to_all.56 = f32[8,16,384]{2,1,0:T(8,128)S(1)} all-to-all(f32[8,16,384]{2,1,0:T(8,128)S(1)} %second_coarse.1), channel_id=1, replica_groups=mesh['sub'=8,'grp'=32] {'sub'}, dimensions={0} | all-to-all | bytes 393216 | tf_op jit(solution)/shard_map/all_to_all | solution.py:321
  172.7 10.4 %second_local.1 = (f32[2048,128]{1,0:T(8,128)S(1)}, f32[2048,128]{1,0:T(8,128)S(1)}, f32[8,128]{1,0:T(8,128)S(1)}, f32[512,128]{1,0:T(8,128)S(1)}, f32[512,128]{...) custom-call(s32[1,2048]{1,0:T(1,128)S(1)} %bitcast.31, bf16[2048,2048]{1,0:T(8,128)(2,1)} %bitcast.13, ...), custom_call_target="tpu_custom_call" | custom-call | flops 2147483648 | bytes 16986112 | tf_op jit(solution)/shard_map/second_local/pallas_call | solution.py:28
  184.5 4.5 %collective-permute-start.15 = (f32[512,128]{1,0:T(8,128)S(1)}, f32[512,128]{1,0:T(8,128)S(1)}, u32[]{:S(2)}, u32[]{:S(2)}) collective-permute-start(f32[512,128]{1,0:T(8,128)S(1)} %get-tuple-element.83), channel_id=1, source_target_pairs={{0,31},{1,0},{2,1},{3,2},{4,3},{5,4},{6,5},{7,6},{8,7},{9,8},{10,9... | collective-permute-start | bytes 786440 | tf_op jit(solution)/shard_map/ppermute | solution.py:308
  190.4 2.5 %collective-permute-done.14.three = f32[512,128]{1,0:T(8,128)S(1)} collective-permute-done((f32[512,128]{1,0:T(8,128)S(1)}, f32[512,128]{1,0:T(8,128)S(1)}, u32[]{:S(2)}, u32[]{:S(2)}) %collective-permute-start.14) | collective-permute-done | bytes 262176 | tf_op jit(solution)/shard_map/ppermute | solution.py:308
  192.8 10.7 %second_apply.1 = (f32[2048,128]{1,0:T(8,128)S(1)}, f32[2048,128]{1,0:T(8,128)S(1)}, f32[8,8,128]{2,1,0:T(8,128)}, f32[512,128]{1,0:T(8,128)S(1)}, f32[512,128]{...) custom-call(s32[1,2048]{1,0:T(1,128)S(1)} %bitcast.32, bf16[2048,2048]{1,0:T(8,128)(2,1)} %bitcast.14, ...), custom_call_target="tpu_custom_call" | custom-call | flops 1073741824 | bytes 15769600 | tf_op jit(solution)/shard_map/second_apply/pallas_call | solution.py:28
  207.3 7.4 %all-to-all-start.8 = ((f32[8,8,128]{2,1,0:T(8,128)}), f32[8,8,128]{2,1,0:T(8,128)S(1)}, u32[]{:S(2)}, u32[]{:S(2)}) async-start(f32[8,8,128]{2,1,0:T(8,128)} %get-tuple-element.84), calls=%async_computation.8 | async-start | bytes 65536 | tf_op jit(solution)/shard_map/all_to_all | solution.py:321
  216.4 4.8 %collective-permute-start.19 = (f32[512,128]{1,0:T(8,128)}, f32[512,128]{1,0:T(8,128)S(1)}, u32[]{:S(2)}, u32[]{:S(2)}) collective-permute-start(f32[512,128]{1,0:T(8,128)} %copy-done.33), channel_id=1, source_target_pairs={{0,31},{1,0},{2,1},{3,2},{4,3},{5,4},{6,5},{7,6},{8,7},{9,8},{10,9... | collective-permute-start | bytes 786440 | tf_op jit(solution)/shard_map/ppermute | solution.py:308
  221.8 4.8 %all-to-all-start.9 = ((f32[32,8,128]{2,1,0:T(8,128)}), f32[32,8,128]{2,1,0:T(8,128)S(1)}, u32[]{:S(2)}, u32[]{:S(2)}) async-start(f32[32,8,128]{2,1,0:T(8,128)} %add_and_copy.5), calls=%async_computation.9 | async-start | bytes 262144 | tf_op jit(solution)/shard_map/all_to_all | solution.py:321
  231.6 2.6 %last_image.1.image_second = f32[2048,128]{1,0:T(8,128)S(1)} custom-call(s32[1,2048]{1,0:T(1,128)S(1)} %bitcast.33, f32[2048,128]{1,0:T(8,128)S(1)} %get-tuple-element.87.product, f32[512,128]{1,0:T(8,128)S(1)} %collective-permute-done.16.one, f32[512,128]{1,0:T(8,128)S(1)} %copy-done.25, f32[512,128]{1,0:T(8,128)S(1)} %copy-done.27, f32[512,128]{1,0:T(8,128)S(1)} %copy-done.29), custom_call_target="tpu_custom_call" | custom-call | bytes 3153920 | tf_op jit(solution)/shard_map/last_image/pallas_call | solution.py:28
  (112 shorter events, 40.3 us)
Async XLA Ops:
  0.6 84.6 %copy-start.2 = (bf16[1,1,2048,256]{3,2,1,0:T(8,128)(2,1)S(1)}, bf16[1,1,2048,256]{3,2,1,0:T(8,128)(2,1)}, u32[]{:S(2)}) copy-start(bf16[1,1,2048,256]{3,2,1,0:T(8,128)(2,1)} %param.12) | copy-start | bytes 3145732
  3.4 81.9 %copy-start.23 = (s32[1,1,2048]{2,1,0:T(1,128)S(1)}, s32[1,1,2048]{2,1,0:T(1,128)}, u32[]{:S(2)}) copy-start(s32[1,1,2048]{2,1,0:T(1,128)} %param.11) | copy-start | bytes 24580
  7.8 10.6 %collective-permute-start = (f32[520,128]{1,0:T(8,128)S(1)}, f32[520,128]{1,0:T(8,128)S(1)}, u32[]{:S(2)}, u32[]{:S(2)}) collective-permute-start(f32[520,128]{1,0:T(8,128)S(1)} %get-tuple-element.48), channel_id=1, source_target_pairs={{0,32},{32,64},{64,96},{96,128},{128,160},{160,192},{192,224},{224... | collective-permute-start | bytes 798728 | tf_op jit(solution)/shard_map/ppermute | solution.py:308
  10.5 8.0 %collective-permute-start.1 = (f32[520,128]{1,0:T(8,128)S(1)}, f32[520,128]{1,0:T(8,128)S(1)}, u32[]{:S(2)}, u32[]{:S(2)}) collective-permute-start(f32[520,128]{1,0:T(8,128)S(1)} %get-tuple-element.49), channel_id=1, source_target_pairs={{0,224},{32,0},{64,32},{96,64},{128,96},{160,128},{192,160},{224,1... | collective-permute-start | bytes 798728 | tf_op jit(solution)/shard_map/ppermute | solution.py:308
  11.1 12.2 %collective-permute-start.2 = (f32[520,128]{1,0:T(8,128)S(1)}, f32[520,128]{1,0:T(8,128)S(1)}, u32[]{:S(2)}, u32[]{:S(2)}) collective-permute-start(f32[520,128]{1,0:T(8,128)S(1)} %get-tuple-element.50), channel_id=1, source_target_pairs={{0,1},{1,2},{2,3},{3,4},{4,5},{5,6},{6,7},{7,8},{8,9},{9,10},{10,1... | collective-permute-start | bytes 798728 | tf_op jit(solution)/shard_map/ppermute | solution.py:308
  11.8 11.6 %collective-permute-start.3 = (f32[520,128]{1,0:T(8,128)S(1)}, f32[520,128]{1,0:T(8,128)S(1)}, u32[]{:S(2)}, u32[]{:S(2)}) collective-permute-start(f32[520,128]{1,0:T(8,128)S(1)} %get-tuple-element.51), channel_id=1, source_target_pairs={{0,31},{1,0},{2,1},{3,2},{4,3},{5,4},{6,5},{7,6},{8,7},{9,8},{10,9... | collective-permute-start | bytes 798728 | tf_op jit(solution)/shard_map/ppermute | solution.py:308
  67.1 18.1 %all-to-all-start.3 = ((f32[8,16,256]{2,1,0:T(8,128)}), f32[8,16,256]{2,1,0:T(8,128)S(1)}, u32[]{:S(2)}, u32[]{:S(2)}) async-start(f32[8,16,256]{2,1,0:T(8,128)} %get-tuple-element.60), calls=%async_computation.3 | async-start | bytes 262144 | tf_op jit(solution)/shard_map/all_to_all | solution.py:321
  89.5 49.0 %copy-start.32 = (s32[1,256]{1,0:T(1,128)S(1)}, s32[1,256]{1,0:T(1,128)}, u32[]{:S(2)}) copy-start(s32[1,256]{1,0:T(1,128)} %members.7) | copy-start | bytes 3076
  89.6 6.4 %collective-permute-start.4 = (f32[512,128]{1,0:T(8,128)S(1)}, f32[512,128]{1,0:T(8,128)S(1)}, u32[]{:S(2)}, u32[]{:S(2)}) collective-permute-start(f32[512,128]{1,0:T(8,128)S(1)} %get-tuple-element.62), channel_id=1, source_target_pairs={{0,32},{32,64},{64,96},{96,128},{128,160},{160,192},{192,224},{224... | collective-permute-start | bytes 786440 | tf_op jit(solution)/shard_map/ppermute | solution.py:308
  91.2 6.1 %collective-permute-start.5 = (f32[512,128]{1,0:T(8,128)S(1)}, f32[512,128]{1,0:T(8,128)S(1)}, u32[]{:S(2)}, u32[]{:S(2)}) collective-permute-start(f32[512,128]{1,0:T(8,128)S(1)} %get-tuple-element.63), channel_id=1, source_target_pairs={{0,224},{32,0},{64,32},{96,64},{128,96},{160,128},{192,160},{224,1... | collective-permute-start | bytes 786440 | tf_op jit(solution)/shard_map/ppermute | solution.py:308
  91.2 9.7 %collective-permute-start.6 = (f32[512,128]{1,0:T(8,128)S(1)}, f32[512,128]{1,0:T(8,128)S(1)}, u32[]{:S(2)}, u32[]{:S(2)}) collective-permute-start(f32[512,128]{1,0:T(8,128)S(1)} %get-tuple-element.64), channel_id=1, source_target_pairs={{0,1},{1,2},{2,3},{3,4},{4,5},{5,6},{6,7},{7,8},{8,9},{9,10},{10,1... | collective-permute-start | bytes 786440 | tf_op jit(solution)/shard_map/ppermute | solution.py:308
  91.5 9.4 %collective-permute-start.7 = (f32[512,128]{1,0:T(8,128)S(1)}, f32[512,128]{1,0:T(8,128)S(1)}, u32[]{:S(2)}, u32[]{:S(2)}) collective-permute-start(f32[512,128]{1,0:T(8,128)S(1)} %get-tuple-element.65), channel_id=1, source_target_pairs={{0,31},{1,0},{2,1},{3,2},{4,3},{5,4},{6,5},{7,6},{8,7},{9,8},{10,9... | collective-permute-start | bytes 786440 | tf_op jit(solution)/shard_map/ppermute | solution.py:308
  100.9 58.6 %copy-start.17 = (f32[1,256,256]{2,1,0:T(8,128)S(1)}, f32[1,256,256]{2,1,0:T(8,128)}, u32[]{:S(2)}) copy-start(f32[1,256,256]{2,1,0:T(8,128)} %param.14) | copy-start | bytes 786436
  100.9 58.6 %copy-start.19 = (f32[256,256]{1,0:T(8,128)S(1)}, f32[256,256]{1,0:T(8,128)}, u32[]{:S(2)}) copy-start(f32[256,256]{1,0:T(8,128)} %inverse_two.3) | copy-start | bytes 786436
  100.9 71.8 %copy-start.11 = (f32[2048,128]{1,0:T(8,128)S(1)}, f32[2048,128]{1,0:T(8,128)}, u32[]{:S(2)}) copy-start(f32[2048,128]{1,0:T(8,128)} %copy-done.10) | copy-start | bytes 3145732
  111.1 81.7 %copy-start.6 = (f32[2048,128]{1,0:T(8,128)}, f32[2048,128]{1,0:T(8,128)S(1)}, u32[]{:S(2)}) copy-start(f32[2048,128]{1,0:T(8,128)S(1)} %get-tuple-element.79.z_first) | copy-start | bytes 3145732
  111.1 8.2 %collective-permute-start.8 = (f32[512,128]{1,0:T(8,128)S(1)}, f32[512,128]{1,0:T(8,128)S(1)}, u32[]{:S(2)}, u32[]{:S(2)}) collective-permute-start(f32[512,128]{1,0:T(8,128)S(1)} %get-tuple-element.67), channel_id=1, source_target_pairs={{0,32},{32,64},{64,96},{96,128},{128,160},{160,192},{192,224},{224... | collective-permute-start | bytes 786440 | tf_op jit(solution)/shard_map/ppermute | solution.py:308
  114.5 6.1 %collective-permute-start.9 = (f32[512,128]{1,0:T(8,128)S(1)}, f32[512,128]{1,0:T(8,128)S(1)}, u32[]{:S(2)}, u32[]{:S(2)}) collective-permute-start(f32[512,128]{1,0:T(8,128)S(1)} %get-tuple-element.68), channel_id=1, source_target_pairs={{0,224},{32,0},{64,32},{96,64},{128,96},{160,128},{192,160},{224,1... | collective-permute-start | bytes 786440 | tf_op jit(solution)/shard_map/ppermute | solution.py:308
  114.5 9.2 %collective-permute-start.10 = (f32[512,128]{1,0:T(8,128)S(1)}, f32[512,128]{1,0:T(8,128)S(1)}, u32[]{:S(2)}, u32[]{:S(2)}) collective-permute-start(f32[512,128]{1,0:T(8,128)S(1)} %get-tuple-element.69), channel_id=1, source_target_pairs={{0,1},{1,2},{2,3},{3,4},{4,5},{5,6},{6,7},{7,8},{8,9},{9,10},{10,1... | collective-permute-start | bytes 786440 | tf_op jit(solution)/shard_map/ppermute | solution.py:308
  114.5 9.2 %collective-permute-start.11 = (f32[512,128]{1,0:T(8,128)S(1)}, f32[512,128]{1,0:T(8,128)S(1)}, u32[]{:S(2)}, u32[]{:S(2)}) collective-permute-start(f32[512,128]{1,0:T(8,128)S(1)} %get-tuple-element.70), channel_id=1, source_target_pairs={{0,31},{1,0},{2,1},{3,2},{4,3},{5,4},{6,5},{7,6},{8,7},{9,8},{10,9... | collective-permute-start | bytes 786440 | tf_op jit(solution)/shard_map/ppermute | solution.py:308
  127.0 56.1 %copy-start.4 = (f32[2048,128]{1,0:T(8,128)}, f32[2048,128]{1,0:T(8,128)S(1)}, u32[]{:S(2)}) copy-start(f32[2048,128]{1,0:T(8,128)S(1)} %get-tuple-element.72.image.image_first) | copy-start | bytes 3145732
  183.1 52.9 %copy-start.5 = (f32[2048,128]{1,0:T(8,128)S(1)}, f32[2048,128]{1,0:T(8,128)}, u32[]{:S(2)}) copy-start(f32[2048,128]{1,0:T(8,128)} %copy-done.4) | copy-start | bytes 3145732
  183.1 5.9 %collective-permute-start.12 = (f32[512,128]{1,0:T(8,128)S(1)}, f32[512,128]{1,0:T(8,128)S(1)}, u32[]{:S(2)}, u32[]{:S(2)}) collective-permute-start(f32[512,128]{1,0:T(8,128)S(1)} %get-tuple-element.80), channel_id=1, source_target_pairs={{0,32},{32,64},{64,96},{96,128},{128,160},{160,192},{192,224},{224... | collective-permute-start | bytes 786440 | tf_op jit(solution)/shard_map/ppermute | solution.py:308
  184.3 6.1 %collective-permute-start.13 = (f32[512,128]{1,0:T(8,128)S(1)}, f32[512,128]{1,0:T(8,128)S(1)}, u32[]{:S(2)}, u32[]{:S(2)}) collective-permute-start(f32[512,128]{1,0:T(8,128)S(1)} %get-tuple-element.81), channel_id=1, source_target_pairs={{0,224},{32,0},{64,32},{96,64},{128,96},{160,128},{192,160},{224,1... | collective-permute-start | bytes 786440 | tf_op jit(solution)/shard_map/ppermute | solution.py:308
  184.3 8.5 %collective-permute-start.14 = (f32[512,128]{1,0:T(8,128)S(1)}, f32[512,128]{1,0:T(8,128)S(1)}, u32[]{:S(2)}, u32[]{:S(2)}) collective-permute-start(f32[512,128]{1,0:T(8,128)S(1)} %get-tuple-element.82), channel_id=1, source_target_pairs={{0,1},{1,2},{2,3},{3,4},{4,5},{5,6},{6,7},{7,8},{8,9},{9,10},{10,1... | collective-permute-start | bytes 786440 | tf_op jit(solution)/shard_map/ppermute | solution.py:308
  184.5 8.3 %collective-permute-start.15 = (f32[512,128]{1,0:T(8,128)S(1)}, f32[512,128]{1,0:T(8,128)S(1)}, u32[]{:S(2)}, u32[]{:S(2)}) collective-permute-start(f32[512,128]{1,0:T(8,128)S(1)} %get-tuple-element.83), channel_id=1, source_target_pairs={{0,31},{1,0},{2,1},{3,2},{4,3},{5,4},{6,5},{7,6},{8,7},{9,8},{10,9... | collective-permute-start | bytes 786440 | tf_op jit(solution)/shard_map/ppermute | solution.py:308
  207.3 13.9 %all-to-all-start.8 = ((f32[8,8,128]{2,1,0:T(8,128)}), f32[8,8,128]{2,1,0:T(8,128)S(1)}, u32[]{:S(2)}, u32[]{:S(2)}) async-start(f32[8,8,128]{2,1,0:T(8,128)} %get-tuple-element.84), calls=%async_computation.8 | async-start | bytes 65536 | tf_op jit(solution)/shard_map/all_to_all | solution.py:321
  214.8 11.9 %collective-permute-start.16 = (f32[512,128]{1,0:T(8,128)}, f32[512,128]{1,0:T(8,128)S(1)}, u32[]{:S(2)}, u32[]{:S(2)}) collective-permute-start(f32[512,128]{1,0:T(8,128)} %copy-done.36), channel_id=1, source_target_pairs={{0,32},{32,64},{64,96},{96,128},{128,160},{160,192},{192,224},{224... | collective-permute-start | bytes 786440 | tf_op jit(solution)/shard_map/ppermute | solution.py:308
  216.4 10.2 %collective-permute-start.17 = (f32[512,128]{1,0:T(8,128)}, f32[512,128]{1,0:T(8,128)S(1)}, u32[]{:S(2)}, u32[]{:S(2)}) collective-permute-start(f32[512,128]{1,0:T(8,128)} %copy-done.35), channel_id=1, source_target_pairs={{0,224},{32,0},{64,32},{96,64},{128,96},{160,128},{192,160},{224,1... | collective-permute-start | bytes 786440 | tf_op jit(solution)/shard_map/ppermute | solution.py:308
  216.4 11.0 %collective-permute-start.18 = (f32[512,128]{1,0:T(8,128)}, f32[512,128]{1,0:T(8,128)S(1)}, u32[]{:S(2)}, u32[]{:S(2)}) collective-permute-start(f32[512,128]{1,0:T(8,128)} %copy-done.34), channel_id=1, source_target_pairs={{0,1},{1,2},{2,3},{3,4},{4,5},{5,6},{6,7},{7,8},{8,9},{9,10},{10,1... | collective-permute-start | bytes 786440 | tf_op jit(solution)/shard_map/ppermute | solution.py:308
  216.4 11.7 %collective-permute-start.19 = (f32[512,128]{1,0:T(8,128)}, f32[512,128]{1,0:T(8,128)S(1)}, u32[]{:S(2)}, u32[]{:S(2)}) collective-permute-start(f32[512,128]{1,0:T(8,128)} %copy-done.33), channel_id=1, source_target_pairs={{0,31},{1,0},{2,1},{3,2},{4,3},{5,4},{6,5},{7,6},{8,7},{9,8},{10,9... | collective-permute-start | bytes 786440 | tf_op jit(solution)/shard_map/ppermute | solution.py:308
  221.8 14.1 %all-to-all-start.9 = ((f32[32,8,128]{2,1,0:T(8,128)}), f32[32,8,128]{2,1,0:T(8,128)S(1)}, u32[]{:S(2)}, u32[]{:S(2)}) async-start(f32[32,8,128]{2,1,0:T(8,128)} %add_and_copy.5), calls=%async_computation.9 | async-start | bytes 262144 | tf_op jit(solution)/shard_map/all_to_all | solution.py:321
  (28 other events, 48.1 us)

commit v3 on v2

--- a/solution.py
+++ b/solution.py
@@ -22,7 +22,7 @@
     return jax.ShapeDtypeStruct(dims, kind)
 
 
-def kernel(body, operands, outs, scratch=(), limit=40, scalars=1, flops=0):
+def kernel(body, operands, outs, scratch=(), limit=10, scalars=1, flops=0, aliases=None):
     specs = [SM] * scalars + [VM] * (len(operands) - scalars)
     moved = sum(value.size * value.dtype.itemsize for value in (*operands, *outs))
     return pl.pallas_call(
@@ -31,6 +31,7 @@
         in_specs=specs,
         out_specs=[VM] * len(outs),
         scratch_shapes=list(scratch),
+        input_output_aliases=aliases or {},
         compiler_params=pltpu.CompilerParams(vmem_limit_bytes=limit << 20),
         cost_estimate=pl.CostEstimate(flops=flops, bytes_accessed=moved, transcendentals=0),
         name=body.func.__name__ if isinstance(body, functools.partial) else body.__name__,
@@ -99,6 +100,12 @@
 def membership_table(members, levels):
     rows = lax.broadcasted_iota(jnp.int32, (levels, members.shape[1]), 0)
     return (rows == members[...]).astype(F32)
+
+
+def split_partial(weighted, basis, wide):
+    wide[:, :LANES], wide[:, LANES:] = split(weighted)
+    both = dot(wide[...], basis[...], ((0,), (0,)))
+    return both[:LANES] + both[LANES:]
 
 
 def open_faces(order, rhs, stiff, *rest):
@@ -114,7 +121,7 @@
         )
 
 
-def open_join(order, rhs, stiff, one, two, three, four, basis, residual, weight, weighted, partial, other, face_stiff):
+def open_join(order, rhs, stiff, one, two, three, four, basis, residual, weight, weighted, partial, other, face_stiff, wide):
     face = rhs.shape[0] // 4
     for k, block in enumerate((one, two, three, four)):
         for t in range(face // LANES):
@@ -124,27 +131,31 @@
     residual[...] = rhs[...] + residual[...]
     weight[...] = weight[...] / (weight[...] + other[...])
     weighted[...] = weight[...] * residual[...]
-    partial[...] = dot(weighted[...].astype(BF), basis[...], ((0,), (0,)))
-
-
-def sweeps(matrix, weighted, diagonal, fix, narrow):
+    partial[...] = split_partial(weighted[...], basis, wide)
+
+
+def sweeps(matrix, weighted, diagonal, fix, wide):
     fix[...] = weighted[...] / diagonal[...]
     for _ in range(LOCAL_STEPS):
-        narrow[...] = fix[...].astype(BF)
+        wide[:, :LANES], wide[:, LANES:] = split(fix[...])
 
         def work(rows):
-            product = dot(matrix[rows, :], narrow[...], ((1,), (0,)))
+            both = dot(matrix[rows, :], wide[...], ((1,), (0,)))
+            product = both[:, :LANES] + both[:, LANES:]
             fix[rows, :] = fix[rows, :] + (weighted[rows, :] - product) / diagonal[rows, :]
 
         chunked(matrix.shape[0], work)
 
 
-def first_fix(matrix, weighted, fix, diagonal, narrow):
+def read_diagonal(matrix, diagonal):
     for start in range(0, matrix.shape[0], LANES):
         square = matrix[pl.ds(start, LANES), pl.ds(start, LANES)].astype(F32)
         column = jnp.sum(jnp.where(eye(), square, 0.0), axis=1, keepdims=True)
         diagonal[pl.ds(start, LANES), :] = jnp.broadcast_to(column, (LANES, LANES))
-    sweeps(matrix, weighted, diagonal, fix, narrow)
+
+
+def local_fix(matrix, weighted, diagonal, fix, wide):
+    sweeps(matrix, weighted, diagonal, fix, wide)
 
 
 def add_coarse(basis, coarse, weight, fix, local):
@@ -163,6 +174,18 @@
         gather_rows(order, k * face, face, [(source, block)])
 
 
+def place_sub(order, one, two, target):
+    face = one.shape[0]
+    for k, block in enumerate((one, two)):
+        scatter_rows(order, k * face, face, [(block, target)])
+
+
+def place_grp(order, blocks, target):
+    face = blocks[0].shape[0]
+    for k, block in enumerate(blocks):
+        scatter_rows(order, (2 + k) * face, face, [(block, target)])
+
+
 def first_local(order, weight, fix, basis, coarse, local, *blocks):
     add_coarse(basis, coarse[...], weight, fix, local)
     send_faces(order, local, blocks)
@@ -182,11 +205,9 @@
     return jnp.sum(first[...] * second[...], axis=0, keepdims=True)
 
 
-def first_apply(order, matrix, local, residual, one, two, three, four, z_value, product, dots, *rest):
+def first_apply(order, matrix, local, residual, three, four, placed, z_value, product, dots, *rest):
     blocks, wide = rest[:4], rest[4]
-    face = local.shape[0] // 4
-    for k, block in enumerate((one, two, three, four)):
-        scatter_rows(order, k * face, face, [(block, z_value)])
+    place_grp(order, (three, four), z_value)
     z_value[...] = local[...] + z_value[...]
     apply_schur(matrix, z_value, product, wide)
     send_faces(order, product, blocks)
@@ -195,34 +216,31 @@
     )
 
 
-def image_partial(order, product, weight, one, two, three, four, basis, dots, image, payload, wide):
-    face = product.shape[0] // 4
-    for k, block in enumerate((one, two, three, four)):
-        scatter_rows(order, k * face, face, [(block, image)])
+def image_partial(order, product, weight, three, four, placed, basis, dots, image, weighted, payload, wide):
+    place_grp(order, (three, four), image)
     image[...] = product[...] + image[...]
-    wide[:, :LANES], wide[:, LANES:] = split(weight[...] * image[...])
-    both = dot(wide[...], basis[...], ((0,), (0,)))
+    weighted[...] = weight[...] * image[...]
     coarse = basis.shape[1]
-    payload[:, :coarse] = both[:LANES] + both[LANES:]
+    payload[:, :coarse] = split_partial(weighted[...], basis, wide)
     square = jnp.concatenate([dots[...], jnp.zeros((LANES - 8, LANES), F32)], axis=0)
     payload[:, coarse:] = square.T
 
 
-def group_level(chunks, members, total, copies, *, levels):
+def group_level(chunks, members, total, part, *, levels):
     value = jnp.sum(chunks[...], axis=0)
     total[...] = value
     coarse = members.shape[1]
-    copies[0, :, :levels] = dot(value[:, :coarse], membership_table(members, levels), ((1,), (1,)), HIGH)
+    part[:, :levels] = dot(value[:, :coarse], membership_table(members, levels), ((1,), (1,)), HIGH)
     if value.shape[1] > coarse:
-        copies[0, :, levels:] = value[:, coarse:]
-    for k in range(1, copies.shape[0]):
-        copies[k] = copies[0]
-
-
-def add_and_copy(chunks, copies):
-    value = jnp.sum(chunks[...], axis=0)
-    for k in range(copies.shape[0]):
-        copies[k] = value
+        part[:, levels:] = value[:, coarse:]
+
+
+def add_and_copy(*refs):
+    value = refs[0][...]
+    for other in refs[1:-1]:
+        value = value + other[...]
+    for k in range(refs[-1].shape[0]):
+        refs[-1][k] = value
 
 
 def coarse_solve(total, two, members, inverse_one, inverse_two):
@@ -252,27 +270,24 @@
         copies[k, :, coarse:] = dots
 
 
-def second_local(order, matrix, diagonal, weight, basis, residual, image, coarse, residual_out, local, info, *rest):
-    blocks, (weighted, fix, narrow) = rest[:4], rest[4:]
+def second_local(order, weight, basis, residual, image, fix_first, fix_image, coarse, residual_out, local, info, *rest):
+    blocks, fix = rest[:4], rest[4]
     levels = basis.shape[1]
     rows = coarse[:, levels:].T
     info[...] = rows[:8]
+    fix[...] = fix_first[...] - rows[2:3] * fix_image[...]
+    add_coarse(basis, coarse[:, :levels], weight, fix, local)
     residual_out[...] = residual[...] - rows[2:3] * image[...]
-    weighted[...] = weight[...] * residual_out[...]
-    sweeps(matrix, weighted, diagonal, fix, narrow)
-    add_coarse(basis, coarse[:, :levels], weight, fix, local)
     send_faces(order, local, blocks)
 
 
-def second_apply(order, matrix, local, residual, z_first, one, two, three, four, z_value, product, copies, *rest):
+def second_apply(order, matrix, local, residual, z_first, three, four, placed, z_value, product, dots, *rest):
     blocks, wide = rest[:4], rest[4]
-    face = local.shape[0] // 4
-    for k, block in enumerate((one, two, three, four)):
-        scatter_rows(order, k * face, face, [(block, z_value)])
+    place_grp(order, (three, four), z_value)
     z_value[...] = local[...] + z_value[...]
     apply_schur(matrix, z_value, product, wide)
     send_faces(order, product, blocks)
-    dots = jnp.concatenate(
+    dots[...] = jnp.concatenate(
         [
             0.5 * column_sum(residual, z_value),
             column_sum(z_value, product),
@@ -281,14 +296,10 @@
         ],
         axis=0,
     )
-    for k in range(copies.shape[0]):
-        copies[k] = dots
-
-
-def last_image(order, product, one, two, three, four, image):
-    face = product.shape[0] // 4
-    for k, block in enumerate((one, two, three, four)):
-        scatter_rows(order, k * face, face, [(block, image)])
+
+
+def last_image(order, product, three, four, placed, image):
+    place_grp(order, (three, four), image)
     image[...] = product[...] + image[...]
 
 
@@ -306,6 +317,11 @@
     count = lax.axis_size(axis)
     pairs = [(source, (source + steps) % count) for source in range(count)]
     return lax.ppermute(value, axis, pairs)
+
+
+def turned(value, step, inner):
+    pairs = [(k, k // inner * inner + (k + step) % inner) for k in range(lax.axis_size("grp"))]
+    return lax.ppermute(value, "grp", pairs)
 
 
 def exchanged(blocks):
@@ -330,13 +346,17 @@
     n_sub, n_grp = lax.axis_size("sub"), lax.axis_size("grp")
     inner = 4
     outer = n_grp // inner
-    groups_y = [[z * inner + y for y in range(inner)] for z in range(outer)]
     groups_z = [[z * inner + y for z in range(outer)] for y in range(inner)]
     share = cols // n_sub
     vector, block = shape(dofs, cols), shape(face, cols)
     face_rows = face + -(-face // LANES // 8) * 8
-    product_flops = 2 * dofs * dofs * cols
-    wide, narrow = pltpu.VMEM((dofs, 2 * cols), BF), pltpu.VMEM((dofs, cols), BF)
+    product_flops = 2 * dofs * dofs * 2 * cols
+    wide = pltpu.VMEM((dofs, 2 * cols), BF)
+
+    def swap(blocks):
+        one, two, three, four = exchanged(blocks)
+        (placed,) = kernel(place_sub, (order, one, two), [vector])
+        return three, four, placed
 
     blocks = kernel(
         open_faces,
@@ -344,31 +364,40 @@
         [shape(face_rows, cols)] * 4,
         [pltpu.VMEM((dofs, cols), F32), pltpu.VMEM((face, cols), F32)],
     )
+    first, matrix = lax.optimization_barrier((blocks[0], matrix))
+    (diagonal,) = kernel(read_diagonal, (matrix,), [vector], scalars=0)
+    arrived = exchanged([first, *blocks[1:]])
+    *arrived, diagonal = lax.optimization_barrier((*arrived, diagonal))
     residual0, weight, weighted, partial = kernel(
         open_join,
-        (order, rhs, stiff, *exchanged(blocks), basis),
+        (order, rhs, stiff, *arrived, basis),
         [vector, vector, vector, shape(cols, coarse)],
-        [pltpu.VMEM((dofs, cols), F32), pltpu.VMEM((face, cols), F32)],
-    )
-
-    def to_groups(value):
+        [pltpu.VMEM((dofs, cols), F32), pltpu.VMEM((face, cols), F32), wide],
+    )
+
+    def to_groups(value, weighted):
         chunks = spread(value.reshape(n_sub, share, value.shape[1]), "sub")
         width = value.shape[1]
         out = width - coarse + levels
-        total, copies = kernel(
+        total, part = kernel(
             functools.partial(group_level, levels=levels),
             (chunks, members),
-            [shape(share, width), shape(inner, share, out)],
+            [shape(share, width), shape(share, out)],
             scalars=0,
         )
-        chunks = spread(copies, "grp", groups_y)
-        (copies,) = kernel(add_and_copy, (chunks,), [shape(outer, share, out)], scalars=0)
-        return total, spread(copies, "grp", groups_z)
+        part, weighted = lax.optimization_barrier((part, weighted))
+        others = [turned(part, step, inner) for step in range(1, inner)]
+        (fix,) = kernel(
+            local_fix, (matrix, weighted, diagonal), [vector], [wide], scalars=0, flops=2 * product_flops
+        )
+        *others, fix = lax.optimization_barrier((*others, fix))
+        (copies,) = kernel(add_and_copy, (part, *others), [shape(outer, share, out)], scalars=0)
+        return total, spread(copies, "grp", groups_z), fix
 
     def from_groups(copies):
         return spread(copies, "sub").reshape(cols, copies.shape[2])
 
-    total0, chunks = to_groups(partial)
+    total0, chunks, fix0 = to_groups(partial, weighted)
     two0, copies = kernel(
         first_coarse,
         (chunks, total0, members, inverse_one, level2_inv),
@@ -376,25 +405,24 @@
         scalars=0,
     )
     coarse0 = from_groups(copies)
-    fix, diagonal = kernel(
-        first_fix, (matrix, weighted), [vector, vector], [narrow], scalars=0, flops=2 * product_flops
-    )
-    local, *blocks = kernel(first_local, (order, weight, fix, basis, coarse0), [vector] + [block] * 4)
+    local, *blocks = kernel(first_local, (order, weight, fix0, basis, coarse0), [vector] + [block] * 4)
 
     z0, product0, dots, *blocks = kernel(
         first_apply,
-        (order, matrix, local, residual0, *exchanged(blocks)),
+        (order, matrix, local, residual0, *swap(blocks)),
         [vector, vector, shape(8, cols)] + [block] * 4,
         [wide],
         flops=product_flops,
-    )
-    image0, payload = kernel(
+        aliases={6: 0},
+    )
+    image0, weighted, payload = kernel(
         image_partial,
-        (order, product0, weight, *exchanged(blocks), basis, dots),
-        [vector, shape(cols, coarse + cols)],
+        (order, product0, weight, *swap(blocks), basis, dots),
+        [vector, vector, shape(cols, coarse + cols)],
         [wide],
-    )
-    total_q, chunks = to_groups(payload)
+        aliases={5: 0},
+    )
+    total_q, chunks, fix_image = to_groups(payload, weighted)
     (copies,) = kernel(
         second_coarse,
         (chunks, total_q, total0, two0, members, inverse_one, level2_inv),
@@ -404,22 +432,25 @@
     coarse1 = from_groups(copies)
     residual1, local, info, *blocks = kernel(
         second_local,
-        (order, matrix, diagonal, weight, basis, residual0, image0, coarse1),
+        (order, weight, basis, residual0, image0, fix0, fix_image, coarse1),
         [vector, vector, shape(8, cols)] + [block] * 4,
-        [pltpu.VMEM((dofs, cols), F32), pltpu.VMEM((dofs, cols), F32), narrow],
-        flops=2 * product_flops,
-    )
-    z1, product1, copies, *blocks = kernel(
+        [pltpu.VMEM((dofs, cols), F32)],
+    )
+    z1, product1, dots, *blocks = kernel(
         second_apply,
-        (order, matrix, local, residual1, z0, *exchanged(blocks)),
-        [vector, vector, shape(n_sub, 8, cols)] + [block] * 4,
+        (order, matrix, local, residual1, z0, *swap(blocks)),
+        [vector, vector, shape(8, cols)] + [block] * 4,
         [wide],
         flops=product_flops,
-    )
-    arrived = exchanged(blocks)
-    (copies,) = kernel(add_and_copy, (spread(copies, "sub"),), [shape(n_grp, 8, cols)], scalars=0)
+        aliases={7: 0},
+    )
+    arrived = swap(blocks)
+    for mask in (1 << k for k in range(n_sub.bit_length() - 1)):
+        dots = dots + lax.ppermute(dots, "sub", [(k, k ^ mask) for k in range(n_sub)])
+    (image1,) = kernel(last_image, (order, product1, *arrived), [vector], aliases={4: 0})
+    dots, image1 = lax.optimization_barrier((dots, image1))
+    (copies,) = kernel(add_and_copy, (dots,), [shape(n_grp, 8, cols)], scalars=0)
     chunks = spread(copies, "grp")
-    (image1,) = kernel(last_image, (order, product1, *arrived), [vector])
     outs = kernel(
         finish, (chunks, info, z0, z1, image0, image1, residual1), [vector, vector], scalars=0
     )

time: 242 us -> 212 us (0.88)
  local copies, waits for them, and re-layouts: 27.7 us -> 6.12 us
  blocking collectives: 76.7 us -> 87.4 us
  starting transfers between devices: 56.8 us -> 47.1 us
  Pallas kernels: 59.6 us -> 53.7 us
  waiting for transfers between devices: 19.7 us -> 15.4 us
    unnamed x74 -> x24, local copies, waits for them, and re-layouts: 27.7 us -> 6.12 us
    all_to_all x3 -> x0, starting transfers between devices: 19.1 us -> none  [spread(): return lax.all_to_all(chunks, axis, 0, 0, axis_index_groups=groups)]
    all_to_all x7, blocking collectives: 76.7 us -> 87.4 us  [spread(): return lax.all_to_all(chunks, axis, 0, 0, axis_index_groups=groups)]
    ppermute x20, waiting for transfers between devices: 18 us -> 8.33 us  [passed_along(): return lax.ppermute(value, axis, pairs)]
    ppermute x0 -> x9, waiting for transfers between devices: none -> 7.08 us  [the longest x3 7.06 us: body(): lax.ppermute(dots, 'sub', [(k, k ^ mask) for k in range(n_sub)])]
    ppermute x0 -> x9, starting transfers between devices: none -> 6.65 us  [the longest x3 3.69 us: body(): lax.ppermute(dots, 'sub', [(k, k ^ mask) for k in range(n_sub)])]
    pallas_call x17 -> x23, Pallas kernels: 59.6 us -> 53.7 us  [kernel(): pl.pallas_call(body, out_shape=list(outs), in_specs=specs, out_specs=[VM]...]
    ppermute x20, starting transfers between devices: 37.7 us -> 40.5 us  [passed_along(): return lax.ppermute(value, axis, pairs)]
  transfers between devices with their start and end apart: 23 -> 29, of which waited for: 8 -> 10; matrix products, arithmetic and copies ran while one was open for 0% -> 0% of each run, Pallas kernels for 3% -> 8%
where the time goes in v3:
time: 212 us; the launch traced here: 211 us
  blocking collectives  87.4 us (41%)
  Pallas kernels  53.7 us (25%)
  starting transfers between devices  47.1 us (22%)
  waiting for transfers between devices  15.4 us (7%)
  local copies, waits for them, and re-layouts  6.12 us (3%)
    all_to_all x7, blocking collectives, spread(): return lax.all_to_all(chunks, axis, 0, 0, axis_index_groups=groups)  87.4 us
    pallas_call x23, Pallas kernels, kernel(): pl.pallas_call(body, out_shape=list(outs), in_specs=specs, out_specs=[VM]...  53.7 us
    ppermute x20, starting transfers between devices, passed_along(): return lax.ppermute(value, axis, pairs)  40.5 us
    ppermute x20, waiting for transfers between devices, passed_along(): return lax.ppermute(value, axis, pairs)  8.33 us
    ppermute x3, waiting for transfers between devices, body(): lax.ppermute(dots, 'sub', [(k, k ^ mask) for k in range(n_sub)])  7.06 us
    unnamed x24, local copies, waits for them, and re-layouts  6.12 us
  transfers between devices with their start and end apart: 29, of which 10 were waited for; matrix products, arithmetic and copies ran while one was open for 0% of the time, Pallas kernels for 8%

profile of v3, /device:TPU:1, one launch (start us, length us, event | category | flops | bytes accessed | tf_op | source)
XLA Modules:
  0.0 210.6 jit_solution(13234685062818703955)
XLA Ops:
  3.4 4.5 %open_faces.1 = (f32[520,128]{1,0:T(8,128)S(1)}, f32[520,128]{1,0:T(8,128)S(1)}, f32[520,128]{1,0:T(8,128)S(1)}, f32[520,128]{1,0:T(8,128)S(1)}) custom-call(s32[1,2048]{1,0:T(1,128)S(1)} %bitcast.23, f32[2048,128]{1,0:T(8,128)S(1)} %bitcast.21, f32[1,2048]{1,0:T(1,128)S(1)} %bitcast.41), custom_call_target="tpu_custom_call" | custom-call | bytes 2129920 | tf_op jit(solution)/shard_map/open_faces/pallas_call | solution.py:28
  7.9 3.3 %collective-permute-start.1 = (f32[520,128]{1,0:T(8,128)S(1)}, f32[520,128]{1,0:T(8,128)S(1)}, u32[]{:S(2)}, u32[]{:S(2)}) collective-permute-start(f32[520,128]{1,0:T(8,128)S(1)} %get-tuple-element.71), channel_id=1, source_target_pairs={{0,224},{32,0},{64,32},{96,64},{128,96},{160,128},{192,160},{224,1... | collective-permute-start | bytes 798728 | tf_op jit(solution)/shard_map/ppermute | solution.py:319
  11.8 6.7 %collective-permute-start.3 = (f32[520,128]{1,0:T(8,128)S(1)}, f32[520,128]{1,0:T(8,128)S(1)}, u32[]{:S(2)}, u32[]{:S(2)}) collective-permute-start(f32[520,128]{1,0:T(8,128)S(1)} %get-tuple-element.73), channel_id=1, source_target_pairs={{0,31},{1,0},{2,1},{3,2},{4,3},{5,4},{6,5},{7,6},{8,7},{9,8},{10,9... | collective-permute-start | bytes 798728 | tf_op jit(solution)/shard_map/ppermute | solution.py:319
  18.5 3.4 %copy-done = bf16[1,1,2048,2048]{3,2,1,0:T(8,128)(2,1)S(1)} copy-done((bf16[1,1,2048,2048]{3,2,1,0:T(8,128)(2,1)S(1)}, bf16[1,1,2048,2048]{3,2,1,0:T(8,128)(2,1)}, u32[]{:S(2)}) %copy-start) | copy-done | bytes 8388632
  22.3 1.9 collective-permute-done.2.three
  24.2 4.6 %open_join.1 = (f32[2048,128]{1,0:T(8,128)S(1)}, f32[2048,128]{1,0:T(8,128)S(1)}, f32[2048,128]{1,0:T(8,128)S(1)}, f32[128,256]{1,0:T(8,128)S(1)}) custom-call(s32[1,2048]{1,0:T(1,128)S(1)} %bitcast.24, f32[2048,128]{1,0:T(8,128)S(1)} %bitcast.22, f32[1,2048]{1,0:T(1,128)S(1)} %bitcast.42, f32[520,128]{1,0:T(8,128)S(1)} %collective-permute-done.one, ...), custom_call_target="tpu_custom_call" | custom-call | bytes 6455296 | tf_op jit(solution)/shard_map/open_join/pallas_call | solution.py:28
  28.8 10.5 %all_to_all.35.chunks = f32[8,16,256]{2,1,0:T(8,128)S(1)} all-to-all(f32[8,16,256]{2,1,0:T(8,128)S(1)} %bitcast.40), channel_id=1, replica_groups=mesh['sub'=8,'grp'=32] {'sub'}, dimensions={0} | all-to-all | bytes 262144 | tf_op jit(solution)/shard_map/all_to_all | solution.py:337
  41.1 4.9 %local_fix.2.fix.fix_first = f32[2048,128]{1,0:T(8,128)S(1)} custom-call(bf16[2048,2048]{1,0:T(8,128)(2,1)S(1)} %bitcast.13, f32[2048,128]{1,0:T(8,128)S(1)} %get-tuple-element.84.weighted, f32[2048,128]{1,0:T(8,128)S(1)} %read_diagonal.1.diagonal), custom_call_target="tpu_custom_call" | custom-call | flops 4294967296 | bytes 11534336 | tf_op jit(solution)/shard_map/local_fix/pallas_call | solution.py:28
  46.0 15.2 %all_to_all.36.chunks = f32[8,16,256]{2,1,0:T(8,128)S(1)} all-to-all(f32[8,16,256]{2,1,0:T(8,128)S(1)} %add_and_copy.3), channel_id=1, replica_groups={{0,4,8,12,16,20,24,28},{1,5,9,13,17,21,25,29},{2,6,10,14,18,22,26,30},{..., dimensions={0} | all-to-all | bytes 262144 | tf_op jit(solution)/shard_map/all_to_all | solution.py:337
  62.4 10.5 %all_to_all.37 = f32[8,16,256]{2,1,0:T(8,128)S(1)} all-to-all(f32[8,16,256]{2,1,0:T(8,128)S(1)} %get-tuple-element.91), channel_id=1, replica_groups=mesh['sub'=8,'grp'=32] {'sub'}, dimensions={0} | all-to-all | bytes 262144 | tf_op jit(solution)/shard_map/all_to_all | solution.py:337
  72.9 3.1 %first_local.1 = (f32[2048,128]{1,0:T(8,128)S(1)}, f32[512,128]{1,0:T(8,128)S(1)}, f32[512,128]{1,0:T(8,128)S(1)}, f32[512,128]{1,0:T(8,128)S(1)}, f32[512,128]{1,0:T(8,128)S(1)}) custom-call(s32[1,2048]{1,0:T(1,128)S(1)} %bitcast.25, f32[2048,128]{1,0:T(8,128)S(1)} %get-tuple-element.78.weight, f32[2048,128]{1,0:T(8,128)S(1)} %local_fix.2.fix.fix_first, ...), custom_call_target="tpu_custom_call" | custom-call | bytes 5382144 | tf_op jit(solution)/shard_map/first_local/pallas_call | solution.py:28
  77.0 2.3 %collective-permute-start.7 = (f32[512,128]{1,0:T(8,128)S(1)}, f32[512,128]{1,0:T(8,128)S(1)}, u32[]{:S(2)}, u32[]{:S(2)}) collective-permute-start(f32[512,128]{1,0:T(8,128)S(1)} %get-tuple-element.93), channel_id=1, source_target_pairs={{0,1},{1,2},{2,3},{3,4},{4,5},{5,6},{6,7},{7,8},{8,9},{9,10},{10,1... | collective-permute-start | bytes 786440 | tf_op jit(solution)/shard_map/ppermute | solution.py:319
  79.3 2.5 %collective-permute-start.8 = (f32[512,128]{1,0:T(8,128)S(1)}, f32[512,128]{1,0:T(8,128)S(1)}, u32[]{:S(2)}, u32[]{:S(2)}) collective-permute-start(f32[512,128]{1,0:T(8,128)S(1)} %get-tuple-element.94), channel_id=1, source_target_pairs={{0,31},{1,0},{2,1},{3,2},{4,3},{5,4},{6,5},{7,6},{8,7},{9,8},{10,9... | collective-permute-start | bytes 786440 | tf_op jit(solution)/shard_map/ppermute | solution.py:319
  85.5 6.5 %first_apply.1 = (f32[2048,128]{1,0:T(8,128)S(1)}, f32[2048,128]{1,0:T(8,128)S(1)}, f32[8,128]{1,0:T(8,128)S(1)}, f32[512,128]{1,0:T(8,128)S(1)}, f32[512,128]{1...) custom-call(s32[1,2048]{1,0:T(1,128)S(1)} %bitcast.27, ...), custom_call_target="tpu_custom_call", output_to_operand_aliasing={{0}: (6, {})} | custom-call | flops 2147483648 | bytes 15216640 | tf_op jit(solution)/shard_map/first_apply/pallas_call | solution.py:28
  92.0 3.5 %collective-permute-start.13 = (f32[512,128]{1,0:T(8,128)S(1)}, f32[512,128]{1,0:T(8,128)S(1)}, u32[]{:S(2)}, u32[]{:S(2)}) collective-permute-start(f32[512,128]{1,0:T(8,128)S(1)} %get-tuple-element.100), channel_id=1, source_target_pairs={{0,32},{32,64},{64,96},{96,128},{128,160},{160,192},{192,224},{224... | collective-permute-start | bytes 786440 | tf_op jit(solution)/shard_map/ppermute | solution.py:319
  96.0 5.1 %collective-permute-start.12 = (f32[512,128]{1,0:T(8,128)S(1)}, f32[512,128]{1,0:T(8,128)S(1)}, u32[]{:S(2)}, u32[]{:S(2)}) collective-permute-start(f32[512,128]{1,0:T(8,128)S(1)} %get-tuple-element.99), channel_id=1, source_target_pairs={{0,31},{1,0},{2,1},{3,2},{4,3},{5,4},{6,5},{7,6},{8,7},{9,8},{10,9... | collective-permute-start | bytes 786440 | tf_op jit(solution)/shard_map/ppermute | solution.py:319
  104.8 2.3 %image_partial.1 = (f32[2048,128]{1,0:T(8,128)S(1)}, f32[2048,128]{1,0:T(8,128)S(1)}, f32[128,384]{1,0:T(8,128)S(1)}) custom-call(s32[1,2048]{1,0:T(1,128)S(1)} %bitcast.29, f32[2048,128]{1,0:T(8,128)S(1)} %get-tuple-element.97.product, f32[2048,128]{1,0:T(8,128)S(1)} %get-tuple-element.78.weight, ...), custom_call_target="tpu_custom_call", output_to_operand_aliasing={{0}: (5, {})} | custom-call | bytes 7024640 | tf_op jit(solution)/shard_map/image_partial/pallas_call | solution.py:28
  107.1 13.5 %all_to_all.38.chunks = f32[8,16,384]{2,1,0:T(8,128)S(1)} all-to-all(f32[8,16,384]{2,1,0:T(8,128)S(1)} %bitcast.39), channel_id=1, replica_groups=mesh['sub'=8,'grp'=32] {'sub'}, dimensions={0} | all-to-all | bytes 393216 | tf_op jit(solution)/shard_map/all_to_all | solution.py:337
  122.4 5.0 %local_fix.3.fix_image = f32[2048,128]{1,0:T(8,128)S(1)} custom-call(bf16[2048,2048]{1,0:T(8,128)(2,1)S(1)} %bitcast.15, f32[2048,128]{1,0:T(8,128)S(1)} %get-tuple-element.108.weighted, f32[2048,128]{1,0:T(8,128)S(1)} %read_diagonal.1.diagonal), custom_call_target="tpu_custom_call" | custom-call | flops 4294967296 | bytes 11534336 | tf_op jit(solution)/shard_map/local_fix/pallas_call | solution.py:28
  127.4 14.0 %all_to_all.39.chunks = f32[8,16,384]{2,1,0:T(8,128)S(1)} all-to-all(f32[8,16,384]{2,1,0:T(8,128)S(1)} %add_and_copy.4), channel_id=1, replica_groups={{0,4,8,12,16,20,24,28},{1,5,9,13,17,21,25,29},{2,6,10,14,18,22,26,30},{..., dimensions={0} | all-to-all | bytes 393216 | tf_op jit(solution)/shard_map/all_to_all | solution.py:337
  142.6 11.2 %all_to_all.40 = f32[8,16,384]{2,1,0:T(8,128)S(1)} all-to-all(f32[8,16,384]{2,1,0:T(8,128)S(1)} %second_coarse.1), channel_id=1, replica_groups=mesh['sub'=8,'grp'=32] {'sub'}, dimensions={0} | all-to-all | bytes 393216 | tf_op jit(solution)/shard_map/all_to_all | solution.py:337
  153.8 3.2 %second_local.1 = (f32[2048,128]{1,0:T(8,128)S(1)}, f32[2048,128]{1,0:T(8,128)S(1)}, f32[8,128]{1,0:T(8,128)S(1)}, f32[512,128]{1,0:T(8,128)S(1)}, f32[512,128]{...) custom-call(s32[1,2048]{1,0:T(1,128)S(1)} %bitcast.30, f32[2048,128]{1,0:T(8,128)S(1)} %get-tuple-element.78.weight, ...), custom_call_target="tpu_custom_call" | custom-call | bytes 9646080 | tf_op jit(solution)/shard_map/second_local/pallas_call | solution.py:28
  158.2 2.3 %collective-permute-start.18 = (f32[512,128]{1,0:T(8,128)S(1)}, f32[512,128]{1,0:T(8,128)S(1)}, u32[]{:S(2)}, u32[]{:S(2)}) collective-permute-start(f32[512,128]{1,0:T(8,128)S(1)} %get-tuple-element.118), channel_id=1, source_target_pairs={{0,1},{1,2},{2,3},{3,4},{4,5},{5,6},{6,7},{7,8},{8,9},{9,10},{10,1... | collective-permute-start | bytes 786440 | tf_op jit(solution)/shard_map/ppermute | solution.py:319
  160.5 2.5 %collective-permute-start.19 = (f32[512,128]{1,0:T(8,128)S(1)}, f32[512,128]{1,0:T(8,128)S(1)}, u32[]{:S(2)}, u32[]{:S(2)}) collective-permute-start(f32[512,128]{1,0:T(8,128)S(1)} %get-tuple-element.119), channel_id=1, source_target_pairs={{0,31},{1,0},{2,1},{3,2},{4,3},{5,4},{6,5},{7,6},{8,7},{9,8},{10,9... | collective-permute-start | bytes 786440 | tf_op jit(solution)/shard_map/ppermute | solution.py:319
  166.7 6.5 %second_apply.1 = (f32[2048,128]{1,0:T(8,128)S(1)}, f32[2048,128]{1,0:T(8,128)S(1)}, f32[8,128]{1,0:T(8,128)S(1)}, f32[512,128]{1,0:T(8,128)S(1)}, f32[512,128]{...) custom-call(s32[1,2048]{1,0:T(1,128)S(1)} %bitcast.32, ...), custom_call_target="tpu_custom_call", output_to_operand_aliasing={{0}: (7, {})} | custom-call | flops 2147483648 | bytes 16265216 | tf_op jit(solution)/shard_map/second_apply/pallas_call | solution.py:28
  173.2 3.5 %collective-permute-start.27 = (f32[512,128]{1,0:T(8,128)S(1)}, f32[512,128]{1,0:T(8,128)S(1)}, u32[]{:S(2)}, u32[]{:S(2)}) collective-permute-start(f32[512,128]{1,0:T(8,128)S(1)} %get-tuple-element.126), channel_id=1, source_target_pairs={{0,32},{32,64},{64,96},{96,128},{128,160},{160,192},{192,224},{224... | collective-permute-start | bytes 786440 | tf_op jit(solution)/shard_map/ppermute | solution.py:319
  177.2 5.1 %collective-permute-start.26 = (f32[512,128]{1,0:T(8,128)S(1)}, f32[512,128]{1,0:T(8,128)S(1)}, u32[]{:S(2)}, u32[]{:S(2)}) collective-permute-start(f32[512,128]{1,0:T(8,128)S(1)} %get-tuple-element.125), channel_id=1, source_target_pairs={{0,31},{1,0},{2,1},{3,2},{4,3},{5,4},{6,5},{7,6},{8,7},{9,8},{10,9... | collective-permute-start | bytes 786440 | tf_op jit(solution)/shard_map/ppermute | solution.py:319
  182.2 3.2 %collective-permute-start.22 = (f32[8,128]{1,0:T(8,128)S(1)}, f32[8,128]{1,0:T(8,128)S(1)}, u32[]{:S(2)}, u32[]{:S(2)}) collective-permute-start(f32[8,128]{1,0:T(8,128)S(1)} %get-tuple-element.122), channel_id=1, source_target_pairs={{0,32},{32,0},{64,96},{96,64},{128,160},{160,128},{192,224},{224,1... | collective-permute-start | bytes 12296 | tf_op jit(solution)/shard_map/ppermute | solution.py:449
  186.3 2.7 %collective-permute-done.23 = f32[8,128]{1,0:T(8,128)S(1)} collective-permute-done((f32[8,128]{1,0:T(8,128)S(1)}, f32[8,128]{1,0:T(8,128)S(1)}, u32[]{:S(2)}, u32[]{:S(2)}) %collective-permute-start.23) | collective-permute-done | bytes 4128 | tf_op jit(solution)/shard_map/ppermute | solution.py:449
  189.5 3.5 %collective-permute-done.24 = f32[8,128]{1,0:T(8,128)S(1)} collective-permute-done((f32[8,128]{1,0:T(8,128)S(1)}, f32[8,128]{1,0:T(8,128)S(1)}, u32[]{:S(2)}, u32[]{:S(2)}) %collective-permute-start.24) | collective-permute-done | bytes 4128 | tf_op jit(solution)/shard_map/ppermute | solution.py:449
  196.4 12.6 %all_to_all.41.chunks = f32[32,8,128]{2,1,0:T(8,128)S(1)} all-to-all(f32[32,8,128]{2,1,0:T(8,128)S(1)} %add_and_copy.5), channel_id=1, replica_groups=mesh['sub'=8,'grp'=32] {'grp'}, dimensions={0} | all-to-all | bytes 262144 | tf_op jit(solution)/shard_map/all_to_all | solution.py:337
  208.9 1.7 finish.1
  (83 shorter events, 28.7 us)
Async XLA Ops:
  3.4 35.9 %copy-start.11 = (s32[1,256]{1,0:T(1,128)S(1)}, s32[1,256]{1,0:T(1,128)}, u32[]{:S(2)}) copy-start(s32[1,256]{1,0:T(1,128)} %members.7) | copy-start | bytes 3076
  7.9 14.4 %collective-permute-start.1 = (f32[520,128]{1,0:T(8,128)S(1)}, f32[520,128]{1,0:T(8,128)S(1)}, u32[]{:S(2)}, u32[]{:S(2)}) collective-permute-start(f32[520,128]{1,0:T(8,128)S(1)} %get-tuple-element.71), channel_id=1, source_target_pairs={{0,224},{32,0},{64,32},{96,64},{128,96},{160,128},{192,160},{224,1... | collective-permute-start | bytes 798728 | tf_op jit(solution)/shard_map/ppermute | solution.py:319
  11.1 11.2 %collective-permute-start = (f32[520,128]{1,0:T(8,128)S(1)}, f32[520,128]{1,0:T(8,128)S(1)}, u32[]{:S(2)}, u32[]{:S(2)}) collective-permute-start(f32[520,128]{1,0:T(8,128)S(1)} %get-tuple-element.70), channel_id=1, source_target_pairs={{0,32},{32,64},{64,96},{96,128},{128,160},{160,192},{192,224},{224... | collective-permute-start | bytes 798728 | tf_op jit(solution)/shard_map/ppermute | solution.py:319
  11.1 13.1 %collective-permute-start.2 = (f32[520,128]{1,0:T(8,128)S(1)}, f32[520,128]{1,0:T(8,128)S(1)}, u32[]{:S(2)}, u32[]{:S(2)}) collective-permute-start(f32[520,128]{1,0:T(8,128)S(1)} %get-tuple-element.72), channel_id=1, source_target_pairs={{0,1},{1,2},{2,3},{3,4},{4,5},{5,6},{6,7},{7,8},{8,9},{9,10},{10,1... | collective-permute-start | bytes 798728 | tf_op jit(solution)/shard_map/ppermute | solution.py:319
  11.8 12.4 %collective-permute-start.3 = (f32[520,128]{1,0:T(8,128)S(1)}, f32[520,128]{1,0:T(8,128)S(1)}, u32[]{:S(2)}, u32[]{:S(2)}) collective-permute-start(f32[520,128]{1,0:T(8,128)S(1)} %get-tuple-element.73), channel_id=1, source_target_pairs={{0,31},{1,0},{2,1},{3,2},{4,3},{5,4},{6,5},{7,6},{8,7},{9,8},{10,9... | collective-permute-start | bytes 798728 | tf_op jit(solution)/shard_map/ppermute | solution.py:319
  28.8 32.5 %copy-start.7 = (f32[1,256,256]{2,1,0:T(8,128)S(1)}, f32[1,256,256]{2,1,0:T(8,128)}, u32[]{:S(2)}) copy-start(f32[1,256,256]{2,1,0:T(8,128)} %param.14) | copy-start | bytes 786436
  28.8 32.5 %copy-start.8 = (f32[256,256]{1,0:T(8,128)S(1)}, f32[256,256]{1,0:T(8,128)}, u32[]{:S(2)}) copy-start(f32[256,256]{1,0:T(8,128)} %inverse_two.3) | copy-start | bytes 786436
  39.6 6.4 %collective-permute-start.6 = (f32[16,256]{1,0:T(8,128)S(1)}, f32[16,256]{1,0:T(8,128)S(1)}, u32[]{:S(2)}, u32[]{:S(2)}) collective-permute-start(f32[16,256]{1,0:T(8,128)S(1)} %get-tuple-element.83.refs_0_), channel_id=1, source_target_pairs={{0,3},{1,0},{2,1},{3,2},{4,7},{5,4},{6,5},{7,6},{8,11},{9,8},{10,9... | collective-permute-start | bytes 49160 | tf_op jit(solution)/shard_map/ppermute | solution.py:324
  39.8 6.2 %collective-permute-start.5 = (f32[16,256]{1,0:T(8,128)S(1)}, f32[16,256]{1,0:T(8,128)S(1)}, u32[]{:S(2)}, u32[]{:S(2)}) collective-permute-start(f32[16,256]{1,0:T(8,128)S(1)} %get-tuple-element.83.refs_0_), channel_id=1, source_target_pairs={{0,2},{1,3},{2,0},{3,1},{4,6},{5,7},{6,4},{7,5},{8,10},{9,11},{10,... | collective-permute-start | bytes 49160 | tf_op jit(solution)/shard_map/ppermute | solution.py:324
  39.8 6.2 %collective-permute-start.4 = (f32[16,256]{1,0:T(8,128)S(1)}, f32[16,256]{1,0:T(8,128)S(1)}, u32[]{:S(2)}, u32[]{:S(2)}) collective-permute-start(f32[16,256]{1,0:T(8,128)S(1)} %get-tuple-element.83.refs_0_), channel_id=1, source_target_pairs={{0,1},{1,2},{2,3},{3,0},{4,5},{5,6},{6,7},{7,4},{8,9},{9,10},{10,1... | collective-permute-start | bytes 49160 | tf_op jit(solution)/shard_map/ppermute | solution.py:324
  76.0 5.8 %collective-permute-start.9 = (f32[512,128]{1,0:T(8,128)S(1)}, f32[512,128]{1,0:T(8,128)S(1)}, u32[]{:S(2)}, u32[]{:S(2)}) collective-permute-start(f32[512,128]{1,0:T(8,128)S(1)} %get-tuple-element.95), channel_id=1, source_target_pairs={{0,32},{32,64},{64,96},{96,128},{128,160},{160,192},{192,224},{224... | collective-permute-start | bytes 786440 | tf_op jit(solution)/shard_map/ppermute | solution.py:319
  77.0 6.1 %collective-permute-start.10 = (f32[512,128]{1,0:T(8,128)S(1)}, f32[512,128]{1,0:T(8,128)S(1)}, u32[]{:S(2)}, u32[]{:S(2)}) collective-permute-start(f32[512,128]{1,0:T(8,128)S(1)} %get-tuple-element.96), channel_id=1, source_target_pairs={{0,224},{32,0},{64,32},{96,64},{128,96},{160,128},{192,160},{224,1... | collective-permute-start | bytes 786440 | tf_op jit(solution)/shard_map/ppermute | solution.py:319
  77.0 8.5 %collective-permute-start.7 = (f32[512,128]{1,0:T(8,128)S(1)}, f32[512,128]{1,0:T(8,128)S(1)}, u32[]{:S(2)}, u32[]{:S(2)}) collective-permute-start(f32[512,128]{1,0:T(8,128)S(1)} %get-tuple-element.93), channel_id=1, source_target_pairs={{0,1},{1,2},{2,3},{3,4},{4,5},{5,6},{6,7},{7,8},{8,9},{9,10},{10,1... | collective-permute-start | bytes 786440 | tf_op jit(solution)/shard_map/ppermute | solution.py:319
  79.3 6.3 %collective-permute-start.8 = (f32[512,128]{1,0:T(8,128)S(1)}, f32[512,128]{1,0:T(8,128)S(1)}, u32[]{:S(2)}, u32[]{:S(2)}) collective-permute-start(f32[512,128]{1,0:T(8,128)S(1)} %get-tuple-element.94), channel_id=1, source_target_pairs={{0,31},{1,0},{2,1},{3,2},{4,3},{5,4},{6,5},{7,6},{8,7},{9,8},{10,9... | collective-permute-start | bytes 786440 | tf_op jit(solution)/shard_map/ppermute | solution.py:319
  92.0 9.0 %collective-permute-start.13 = (f32[512,128]{1,0:T(8,128)S(1)}, f32[512,128]{1,0:T(8,128)S(1)}, u32[]{:S(2)}, u32[]{:S(2)}) collective-permute-start(f32[512,128]{1,0:T(8,128)S(1)} %get-tuple-element.100), channel_id=1, source_target_pairs={{0,32},{32,64},{64,96},{96,128},{128,160},{160,192},{192,224},{224... | collective-permute-start | bytes 786440 | tf_op jit(solution)/shard_map/ppermute | solution.py:319
  95.5 6.1 %collective-permute-start.14 = (f32[512,128]{1,0:T(8,128)S(1)}, f32[512,128]{1,0:T(8,128)S(1)}, u32[]{:S(2)}, u32[]{:S(2)}) collective-permute-start(f32[512,128]{1,0:T(8,128)S(1)} %get-tuple-element.101), channel_id=1, source_target_pairs={{0,224},{32,0},{64,32},{96,64},{128,96},{160,128},{192,160},{224,1... | collective-permute-start | bytes 786440 | tf_op jit(solution)/shard_map/ppermute | solution.py:319
  96.0 8.8 %collective-permute-start.11 = (f32[512,128]{1,0:T(8,128)S(1)}, f32[512,128]{1,0:T(8,128)S(1)}, u32[]{:S(2)}, u32[]{:S(2)}) collective-permute-start(f32[512,128]{1,0:T(8,128)S(1)} %get-tuple-element.98), channel_id=1, source_target_pairs={{0,1},{1,2},{2,3},{3,4},{4,5},{5,6},{6,7},{7,8},{8,9},{9,10},{10,1... | collective-permute-start | bytes 786440 | tf_op jit(solution)/shard_map/ppermute | solution.py:319
  96.0 8.8 %collective-permute-start.12 = (f32[512,128]{1,0:T(8,128)S(1)}, f32[512,128]{1,0:T(8,128)S(1)}, u32[]{:S(2)}, u32[]{:S(2)}) collective-permute-start(f32[512,128]{1,0:T(8,128)S(1)} %get-tuple-element.99), channel_id=1, source_target_pairs={{0,31},{1,0},{2,1},{3,2},{4,3},{5,4},{6,5},{7,6},{8,7},{9,8},{10,9... | collective-permute-start | bytes 786440 | tf_op jit(solution)/shard_map/ppermute | solution.py:319
  120.9 6.4 %collective-permute-start.17 = (f32[16,384]{1,0:T(8,128)S(1)}, f32[16,384]{1,0:T(8,128)S(1)}, u32[]{:S(2)}, u32[]{:S(2)}) collective-permute-start(f32[16,384]{1,0:T(8,128)S(1)} %get-tuple-element.107.refs_0_), channel_id=1, source_target_pairs={{0,3},{1,0},{2,1},{3,2},{4,7},{5,4},{6,5},{7,6},{8,11},{9,8},{10,9... | collective-permute-start | bytes 73736 | tf_op jit(solution)/shard_map/ppermute | solution.py:324
  121.3 6.0 %collective-permute-start.16 = (f32[16,384]{1,0:T(8,128)S(1)}, f32[16,384]{1,0:T(8,128)S(1)}, u32[]{:S(2)}, u32[]{:S(2)}) collective-permute-start(f32[16,384]{1,0:T(8,128)S(1)} %get-tuple-element.107.refs_0_), channel_id=1, source_target_pairs={{0,2},{1,3},{2,0},{3,1},{4,6},{5,7},{6,4},{7,5},{8,10},{9,11},{10,... | collective-permute-start | bytes 73736 | tf_op jit(solution)/shard_map/ppermute | solution.py:324
  121.3 6.0 %collective-permute-start.15 = (f32[16,384]{1,0:T(8,128)S(1)}, f32[16,384]{1,0:T(8,128)S(1)}, u32[]{:S(2)}, u32[]{:S(2)}) collective-permute-start(f32[16,384]{1,0:T(8,128)S(1)} %get-tuple-element.107.refs_0_), channel_id=1, source_target_pairs={{0,1},{1,2},{2,3},{3,0},{4,5},{5,6},{6,7},{7,4},{8,9},{9,10},{10,1... | collective-permute-start | bytes 73736 | tf_op jit(solution)/shard_map/ppermute | solution.py:324
  157.1 5.9 %collective-permute-start.20 = (f32[512,128]{1,0:T(8,128)S(1)}, f32[512,128]{1,0:T(8,128)S(1)}, u32[]{:S(2)}, u32[]{:S(2)}) collective-permute-start(f32[512,128]{1,0:T(8,128)S(1)} %get-tuple-element.120), channel_id=1, source_target_pairs={{0,32},{32,64},{64,96},{96,128},{128,160},{160,192},{192,224},{224... | collective-permute-start | bytes 786440 | tf_op jit(solution)/shard_map/ppermute | solution.py:319
  158.2 6.1 %collective-permute-start.21 = (f32[512,128]{1,0:T(8,128)S(1)}, f32[512,128]{1,0:T(8,128)S(1)}, u32[]{:S(2)}, u32[]{:S(2)}) collective-permute-start(f32[512,128]{1,0:T(8,128)S(1)} %get-tuple-element.121), channel_id=1, source_target_pairs={{0,224},{32,0},{64,32},{96,64},{128,96},{160,128},{192,160},{224,1... | collective-permute-start | bytes 786440 | tf_op jit(solution)/shard_map/ppermute | solution.py:319
  158.2 8.5 %collective-permute-start.18 = (f32[512,128]{1,0:T(8,128)S(1)}, f32[512,128]{1,0:T(8,128)S(1)}, u32[]{:S(2)}, u32[]{:S(2)}) collective-permute-start(f32[512,128]{1,0:T(8,128)S(1)} %get-tuple-element.118), channel_id=1, source_target_pairs={{0,1},{1,2},{2,3},{3,4},{4,5},{5,6},{6,7},{7,8},{8,9},{9,10},{10,1... | collective-permute-start | bytes 786440 | tf_op jit(solution)/shard_map/ppermute | solution.py:319
  160.5 6.3 %collective-permute-start.19 = (f32[512,128]{1,0:T(8,128)S(1)}, f32[512,128]{1,0:T(8,128)S(1)}, u32[]{:S(2)}, u32[]{:S(2)}) collective-permute-start(f32[512,128]{1,0:T(8,128)S(1)} %get-tuple-element.119), channel_id=1, source_target_pairs={{0,31},{1,0},{2,1},{3,2},{4,3},{5,4},{6,5},{7,6},{8,7},{9,8},{10,9... | collective-permute-start | bytes 786440 | tf_op jit(solution)/shard_map/ppermute | solution.py:319
  173.2 19.8 %collective-permute-start.27 = (f32[512,128]{1,0:T(8,128)S(1)}, f32[512,128]{1,0:T(8,128)S(1)}, u32[]{:S(2)}, u32[]{:S(2)}) collective-permute-start(f32[512,128]{1,0:T(8,128)S(1)} %get-tuple-element.126), channel_id=1, source_target_pairs={{0,32},{32,64},{64,96},{96,128},{128,160},{160,192},{192,224},{224... | collective-permute-start | bytes 786440 | tf_op jit(solution)/shard_map/ppermute | solution.py:319
  176.7 16.3 %collective-permute-start.28 = (f32[512,128]{1,0:T(8,128)S(1)}, f32[512,128]{1,0:T(8,128)S(1)}, u32[]{:S(2)}, u32[]{:S(2)}) collective-permute-start(f32[512,128]{1,0:T(8,128)S(1)} %get-tuple-element.127), channel_id=1, source_target_pairs={{0,224},{32,0},{64,32},{96,64},{128,96},{160,128},{192,160},{224,1... | collective-permute-start | bytes 786440 | tf_op jit(solution)/shard_map/ppermute | solution.py:319
  177.2 17.5 %collective-permute-start.25 = (f32[512,128]{1,0:T(8,128)S(1)}, f32[512,128]{1,0:T(8,128)S(1)}, u32[]{:S(2)}, u32[]{:S(2)}) collective-permute-start(f32[512,128]{1,0:T(8,128)S(1)} %get-tuple-element.124), channel_id=1, source_target_pairs={{0,1},{1,2},{2,3},{3,4},{4,5},{5,6},{6,7},{7,8},{8,9},{9,10},{10,1... | collective-permute-start | bytes 786440 | tf_op jit(solution)/shard_map/ppermute | solution.py:319
  177.2 17.5 %collective-permute-start.26 = (f32[512,128]{1,0:T(8,128)S(1)}, f32[512,128]{1,0:T(8,128)S(1)}, u32[]{:S(2)}, u32[]{:S(2)}) collective-permute-start(f32[512,128]{1,0:T(8,128)S(1)} %get-tuple-element.125), channel_id=1, source_target_pairs={{0,31},{1,0},{2,1},{3,2},{4,3},{5,4},{6,5},{7,6},{8,7},{9,8},{10,9... | collective-permute-start | bytes 786440 | tf_op jit(solution)/shard_map/ppermute | solution.py:319
  182.2 4.0 %collective-permute-start.22 = (f32[8,128]{1,0:T(8,128)S(1)}, f32[8,128]{1,0:T(8,128)S(1)}, u32[]{:S(2)}, u32[]{:S(2)}) collective-permute-start(f32[8,128]{1,0:T(8,128)S(1)} %get-tuple-element.122), channel_id=1, source_target_pairs={{0,32},{32,0},{64,96},{96,64},{128,160},{160,128},{192,224},{224,1... | collective-permute-start | bytes 12296 | tf_op jit(solution)/shard_map/ppermute | solution.py:449
  186.3 2.8 %collective-permute-start.23 = (f32[8,128]{1,0:T(8,128)S(1)}, f32[8,128]{1,0:T(8,128)S(1)}, u32[]{:S(2)}, u32[]{:S(2)}) collective-permute-start(f32[8,128]{1,0:T(8,128)S(1)} %add.9), channel_id=1, source_target_pairs={{0,64},{32,96},{64,0},{96,32},{128,192},{160,224},{192,128},{224,1... | collective-permute-start | bytes 12296 | tf_op jit(solution)/shard_map/ppermute | solution.py:449
  189.0 4.0 %collective-permute-start.24 = (f32[8,128]{1,0:T(8,128)S(1)}, f32[8,128]{1,0:T(8,128)S(1)}, u32[]{:S(2)}, u32[]{:S(2)}) collective-permute-start(f32[8,128]{1,0:T(8,128)S(1)} %add.10), channel_id=1, source_target_pairs={{0,128},{32,160},{64,192},{96,224},{128,0},{160,32},{192,64},{224,... | collective-permute-start | bytes 12296 | tf_op jit(solution)/shard_map/ppermute | solution.py:449
  (9 other events, 92.7 us)

commit v4 on v3

--- a/solution.py
+++ b/solution.py
@@ -16,14 +16,15 @@
 CHUNK = 512
 VM = pl.BlockSpec(memory_space=pltpu.VMEM)
 SM = pl.BlockSpec(memory_space=pltpu.SMEM)
+HB = pl.BlockSpec(memory_space=pltpu.HBM)
 
 
 def shape(*dims, kind=F32):
     return jax.ShapeDtypeStruct(dims, kind)
 
 
-def kernel(body, operands, outs, scratch=(), limit=10, scalars=1, flops=0, aliases=None):
-    specs = [SM] * scalars + [VM] * (len(operands) - scalars)
+def kernel(body, operands, outs, scratch=(), limit=10, scalars=1, flops=0, aliases=None, specs=None):
+    specs = specs or [SM] * scalars + [VM] * (len(operands) - scalars)
     moved = sum(value.size * value.dtype.itemsize for value in (*operands, *outs))
     return pl.pallas_call(
         body,
@@ -108,10 +109,28 @@
     return both[:LANES] + both[LANES:]
 
 
-def open_faces(order, rhs, stiff, *rest):
-    blocks, (own_stiff, face_stiff) = rest[:4], rest[4:]
+def pack(value, dots):
+    return jnp.concatenate([value[:, k : k + LANES] for k in range(0, value.shape[1], LANES)] + [dots], axis=0)
+
+
+def unpack(rows, share):
+    parts = [rows[k : k + share] for k in range(0, rows.shape[0] - 8, share)]
+    return jnp.concatenate(parts, axis=1), rows[rows.shape[0] - 8 :]
+
+
+def open_faces(order_far, rhs_far, stiff_far, *rest):
+    blocks, (order, rhs, stiff, own_stiff, face_stiff, sems) = rest[:4], rest[4:]
+    fetches = [
+        pltpu.make_async_copy(source, target, sems.at[k])
+        for k, (source, target) in enumerate(((order_far, order), (rhs_far, rhs), (stiff_far, stiff)))
+    ]
+    for fetch in fetches:
+        fetch.start()
     face = rhs.shape[0] // 4
+    fetches[2].wait()
     spread_stiff(stiff, own_stiff)
+    fetches[0].wait()
+    fetches[1].wait()
     for k, block in enumerate(blocks):
         gather_rows(order, k * face, face, [(rhs, block), (own_stiff, face_stiff)])
         block[pl.ds(face, block.shape[0] - face), :] = jnp.concatenate(
@@ -121,12 +140,22 @@
         )
 
 
-def open_join(order, rhs, stiff, one, two, three, four, basis, residual, weight, weighted, partial, other, face_stiff, wide):
-    face = rhs.shape[0] // 4
-    for k, block in enumerate((one, two, three, four)):
+def open_place(order, start, blocks, face, residual, other, face_stiff):
+    for k, block in enumerate(blocks):
         for t in range(face // LANES):
             face_stiff[pl.ds(t * LANES, LANES), :] = to_column(block[pl.ds(face + t, 1), :])
-        scatter_rows(order, k * face, face, [(block, residual), (face_stiff, other)])
+        scatter_rows(order, start + k * face, face, [(block, residual), (face_stiff, other)])
+
+
+def open_sub(order, one, two, residual, other, face_stiff):
+    open_place(order, 0, (one, two), face_stiff.shape[0], residual, other, face_stiff)
+
+
+def open_join(
+    order, rhs, stiff, three, four, basis, placed, placed_stiff, residual, other, weight, weighted, partial, face_stiff, wide
+):
+    face = face_stiff.shape[0]
+    open_place(order, 2 * face, (three, four), face, residual, other, face_stiff)
     spread_stiff(stiff, weight)
     residual[...] = rhs[...] + residual[...]
     weight[...] = weight[...] / (weight[...] + other[...])
@@ -168,27 +197,33 @@
     chunked(basis.shape[0], work)
 
 
-def send_faces(order, source, blocks):
+def send_grp(order, source, blocks):
+    face = source.shape[0] // 4
+    for k, block in enumerate(blocks):
+        gather_rows(order, (2 + k) * face, face, [(source, block)])
+
+
+def send_sub(order, source, *blocks):
     face = source.shape[0] // 4
     for k, block in enumerate(blocks):
         gather_rows(order, k * face, face, [(source, block)])
 
 
-def place_sub(order, one, two, target):
-    face = one.shape[0]
-    for k, block in enumerate((one, two)):
-        scatter_rows(order, k * face, face, [(block, target)])
-
-
-def place_grp(order, blocks, target):
+def place_sub(order, blocks, target):
     face = blocks[0].shape[0]
     for k, block in enumerate(blocks):
+        scatter_rows(order, k * face, face, [(block, target)])
+
+
+def place_grp(order, three, four, target):
+    face = three.shape[0]
+    for k, block in enumerate((three, four)):
         scatter_rows(order, (2 + k) * face, face, [(block, target)])
 
 
 def first_local(order, weight, fix, basis, coarse, local, *blocks):
     add_coarse(basis, coarse[...], weight, fix, local)
-    send_faces(order, local, blocks)
+    send_grp(order, local, blocks)
 
 
 def apply_schur(matrix, vector, product, wide):
@@ -205,34 +240,45 @@
     return jnp.sum(first[...] * second[...], axis=0, keepdims=True)
 
 
-def first_apply(order, matrix, local, residual, three, four, placed, z_value, product, dots, *rest):
-    blocks, wide = rest[:4], rest[4]
-    place_grp(order, (three, four), z_value)
+def first_apply(order, matrix, local, residual, one, two, placed, z_value, product, dots, *rest):
+    blocks, wide = rest[:2], rest[2]
+    place_sub(order, (one, two), z_value)
     z_value[...] = local[...] + z_value[...]
     apply_schur(matrix, z_value, product, wide)
-    send_faces(order, product, blocks)
+    send_grp(order, product, blocks)
     dots[...] = jnp.concatenate(
         [0.5 * column_sum(residual, z_value), column_sum(z_value, product), jnp.zeros((6, LANES), F32)], axis=0
     )
 
 
-def image_partial(order, product, weight, three, four, placed, basis, dots, image, weighted, payload, wide):
-    place_grp(order, (three, four), image)
+def image_partial(order, product, weight, one, two, placed, basis, dots, image, weighted, payload, wide):
+    place_sub(order, (one, two), image)
     image[...] = product[...] + image[...]
     weighted[...] = weight[...] * image[...]
-    coarse = basis.shape[1]
-    payload[:, :coarse] = split_partial(weighted[...], basis, wide)
-    square = jnp.concatenate([dots[...], jnp.zeros((LANES - 8, LANES), F32)], axis=0)
-    payload[:, coarse:] = square.T
-
-
-def group_level(chunks, members, total, part, *, levels):
-    value = jnp.sum(chunks[...], axis=0)
-    total[...] = value
-    coarse = members.shape[1]
-    part[:, :levels] = dot(value[:, :coarse], membership_table(members, levels), ((1,), (1,)), HIGH)
-    if value.shape[1] > coarse:
-        part[:, levels:] = value[:, coarse:]
+    value = split_partial(weighted[...], basis, wide)
+    share = value.shape[0] // payload.shape[0]
+    for k in range(payload.shape[0]):
+        payload[k] = pack(value[k * share : (k + 1) * share], dots[...])
+
+
+def first_groups(chunks, members, total, part, *, levels):
+    total[...] = jnp.sum(chunks[...], axis=0)
+    part[...] = dot(total[...], membership_table(members, levels), ((1,), (1,)), HIGH)
+
+
+def second_groups(chunks, members, total, part, *, levels):
+    total[...], dots = unpack(jnp.sum(chunks[...], axis=0), total.shape[0])
+    part[...] = pack(dot(total[...], membership_table(members, levels), ((1,), (1,)), HIGH), dots)
+
+
+def copy_row(*refs):
+    *parts, copies = refs
+    dots = parts[0][...]
+    for other in parts[1:]:
+        dots = dots + other[...]
+    row = jnp.concatenate([dots[k : k + 1] for k in range(3)], axis=1)
+    for k in range(copies.shape[0]):
+        copies[k] = row
 
 
 def add_and_copy(*refs):
@@ -256,37 +302,35 @@
         copies[k] = value
 
 
-def second_coarse(chunks, total_q, total, two, members, inverse_one, inverse_two, copies):
-    levels, coarse = inverse_two.shape[0], members.shape[1]
-    value = jnp.sum(chunks[...], axis=0)
-    dots = value[:, levels:]
-    step = dots[:, 0:1] / dots[:, 1:2]
+def second_coarse(chunks, total_q, total, two, members, inverse_one, inverse_two, copies, info, column):
+    share = total.shape[0]
+    two_q, dots = unpack(jnp.sum(chunks[...], axis=0), share)
+    step = dots[0:1] / dots[1:2]
+    info[...] = jnp.concatenate([dots[0:2], step, dots[3:]], axis=0)
+    column[...] = to_column(step)
+    mine = column[pl.ds(pl.multiple_of(lax.axis_index("sub") * share, 8), share), :][:, 0:1]
     solved = coarse_solve(
-        total[...] - step * total_q[:, :coarse], two[...] - step * value[:, :levels], members, inverse_one, inverse_two
-    )
-    dots = jnp.where(lax.broadcasted_iota(jnp.int32, dots.shape, 1) == 2, step, dots)
+        total[...] - mine * total_q[...], two[...] - mine * two_q, members, inverse_one, inverse_two
+    )
     for k in range(copies.shape[0]):
-        copies[k, :, :coarse] = solved
-        copies[k, :, coarse:] = dots
-
-
-def second_local(order, weight, basis, residual, image, fix_first, fix_image, coarse, residual_out, local, info, *rest):
-    blocks, fix = rest[:4], rest[4]
-    levels = basis.shape[1]
-    rows = coarse[:, levels:].T
-    info[...] = rows[:8]
-    fix[...] = fix_first[...] - rows[2:3] * fix_image[...]
-    add_coarse(basis, coarse[:, :levels], weight, fix, local)
-    residual_out[...] = residual[...] - rows[2:3] * image[...]
-    send_faces(order, local, blocks)
-
-
-def second_apply(order, matrix, local, residual, z_first, three, four, placed, z_value, product, dots, *rest):
-    blocks, wide = rest[:4], rest[4]
-    place_grp(order, (three, four), z_value)
+        copies[k] = solved
+
+
+def second_local(order, weight, basis, residual, image, fix_first, fix_image, coarse, info, residual_out, local, *rest):
+    blocks, fix = rest[:2], rest[2]
+    step = info[2:3]
+    fix[...] = fix_first[...] - step * fix_image[...]
+    add_coarse(basis, coarse[...], weight, fix, local)
+    residual_out[...] = residual[...] - step * image[...]
+    send_grp(order, local, blocks)
+
+
+def second_apply(order, matrix, local, residual, z_first, one, two, placed, z_value, product, dots, *rest):
+    blocks, wide = rest[:2], rest[2]
+    place_sub(order, (one, two), z_value)
     z_value[...] = local[...] + z_value[...]
     apply_schur(matrix, z_value, product, wide)
-    send_faces(order, product, blocks)
+    send_grp(order, product, blocks)
     dots[...] = jnp.concatenate(
         [
             0.5 * column_sum(residual, z_value),
@@ -298,17 +342,17 @@
     )
 
 
-def last_image(order, product, three, four, placed, image):
-    place_grp(order, (three, four), image)
+def last_image(order, product, one, two, placed, image):
+    place_sub(order, (one, two), image)
     image[...] = product[...] + image[...]
 
 
 def finish(chunks, info, z_first, z_second, image_first, image_second, residual, solution_out, residual_out):
     dots = jnp.sum(chunks[...], axis=0)
     rz_first, step_first = info[0:1], info[2:3]
-    rz = dots[0:1]
+    rz, zaz, zaz_first = (dots[:, k * LANES : (k + 1) * LANES] for k in range(3))
     ratio = rz / rz_first
-    step = rz / (dots[1:2] + 2.0 * ratio * dots[2:3] + ratio * ratio * info[1:2])
+    step = rz / (zaz + 2.0 * ratio * zaz_first + ratio * ratio * info[1:2])
     solution_out[...] = step_first * z_first[...] + step * (z_second[...] + ratio * z_first[...])
     residual_out[...] = residual[...] - step * (image_second[...] + ratio * image_first[...])
 
@@ -353,36 +397,50 @@
     product_flops = 2 * dofs * dofs * 2 * cols
     wide = pltpu.VMEM((dofs, 2 * cols), BF)
 
-    def swap(blocks):
-        one, two, three, four = exchanged(blocks)
-        (placed,) = kernel(place_sub, (order, one, two), [vector])
-        return three, four, placed
+    def swap(source, toward_grp):
+        three = passed_along(toward_grp[1], "grp", 1)
+        four = passed_along(toward_grp[0], "grp", -1)
+        first, second = kernel(send_sub, (order, source), [block] * 2)
+        one = passed_along(second, "sub", 1)
+        two = passed_along(first, "sub", -1)
+        (placed,) = kernel(place_grp, (order, three, four), [vector])
+        return one, two, placed
 
     blocks = kernel(
         open_faces,
         (order, rhs, stiff),
         [shape(face_rows, cols)] * 4,
-        [pltpu.VMEM((dofs, cols), F32), pltpu.VMEM((face, cols), F32)],
+        [
+            pltpu.SMEM((1, dofs), jnp.int32),
+            pltpu.VMEM((dofs, cols), F32),
+            pltpu.VMEM((1, dofs), F32),
+            pltpu.VMEM((dofs, cols), F32),
+            pltpu.VMEM((face, cols), F32),
+            pltpu.SemaphoreType.DMA((3,)),
+        ],
+        specs=[HB] * 3,
+        limit=60,
     )
     first, matrix = lax.optimization_barrier((blocks[0], matrix))
     (diagonal,) = kernel(read_diagonal, (matrix,), [vector], scalars=0)
-    arrived = exchanged([first, *blocks[1:]])
-    *arrived, diagonal = lax.optimization_barrier((*arrived, diagonal))
-    residual0, weight, weighted, partial = kernel(
+    one, two, three, four = exchanged([first, *blocks[1:]])
+    placed = kernel(open_sub, (order, one, two), [vector, vector], [pltpu.VMEM((face, cols), F32)])
+    three, four, diagonal = lax.optimization_barrier((three, four, diagonal))
+    residual0, _, weight, weighted, partial = kernel(
         open_join,
-        (order, rhs, stiff, *arrived, basis),
-        [vector, vector, vector, shape(cols, coarse)],
-        [pltpu.VMEM((dofs, cols), F32), pltpu.VMEM((face, cols), F32), wide],
-    )
-
-    def to_groups(value, weighted):
-        chunks = spread(value.reshape(n_sub, share, value.shape[1]), "sub")
-        width = value.shape[1]
-        out = width - coarse + levels
+        (order, rhs, stiff, three, four, basis, *placed),
+        [vector] * 4 + [shape(cols, coarse)],
+        [pltpu.VMEM((face, cols), F32), wide],
+        aliases={6: 0, 7: 1},
+    )
+
+    def to_groups(body, chunks, weighted):
+        chunks = spread(chunks, "sub")
+        part_shape = chunks.shape[1:] if chunks.shape[2] == LANES else (share, levels)
         total, part = kernel(
-            functools.partial(group_level, levels=levels),
+            functools.partial(body, levels=levels),
             (chunks, members),
-            [shape(share, width), shape(share, out)],
+            [shape(share, coarse), shape(*part_shape)],
             scalars=0,
         )
         part, weighted = lax.optimization_barrier((part, weighted))
@@ -391,13 +449,13 @@
             local_fix, (matrix, weighted, diagonal), [vector], [wide], scalars=0, flops=2 * product_flops
         )
         *others, fix = lax.optimization_barrier((*others, fix))
-        (copies,) = kernel(add_and_copy, (part, *others), [shape(outer, share, out)], scalars=0)
+        (copies,) = kernel(add_and_copy, (part, *others), [shape(outer, *part_shape)], scalars=0)
         return total, spread(copies, "grp", groups_z), fix
 
     def from_groups(copies):
         return spread(copies, "sub").reshape(cols, copies.shape[2])
 
-    total0, chunks, fix0 = to_groups(partial, weighted)
+    total0, chunks, fix0 = to_groups(first_groups, partial.reshape(n_sub, share, coarse), weighted)
     two0, copies = kernel(
         first_coarse,
         (chunks, total0, members, inverse_one, level2_inv),
@@ -405,51 +463,53 @@
         scalars=0,
     )
     coarse0 = from_groups(copies)
-    local, *blocks = kernel(first_local, (order, weight, fix0, basis, coarse0), [vector] + [block] * 4)
+    local, *blocks = kernel(first_local, (order, weight, fix0, basis, coarse0), [vector] + [block] * 2)
 
     z0, product0, dots, *blocks = kernel(
         first_apply,
-        (order, matrix, local, residual0, *swap(blocks)),
-        [vector, vector, shape(8, cols)] + [block] * 4,
+        (order, matrix, local, residual0, *swap(local, blocks)),
+        [vector, vector, shape(8, cols)] + [block] * 2,
         [wide],
         flops=product_flops,
         aliases={6: 0},
     )
     image0, weighted, payload = kernel(
         image_partial,
-        (order, product0, weight, *swap(blocks), basis, dots),
-        [vector, vector, shape(cols, coarse + cols)],
+        (order, product0, weight, *swap(product0, blocks), basis, dots),
+        [vector, vector, shape(n_sub, share * coarse // LANES + 8, LANES)],
         [wide],
         aliases={5: 0},
     )
-    total_q, chunks, fix_image = to_groups(payload, weighted)
-    (copies,) = kernel(
+    total_q, chunks, fix_image = to_groups(second_groups, payload, weighted)
+    copies, info = kernel(
         second_coarse,
         (chunks, total_q, total0, two0, members, inverse_one, level2_inv),
-        [shape(n_sub, share, coarse + cols)],
+        [shape(n_sub, share, coarse), shape(8, cols)],
+        [pltpu.VMEM((LANES, LANES), F32)],
         scalars=0,
     )
     coarse1 = from_groups(copies)
-    residual1, local, info, *blocks = kernel(
+    residual1, local, *blocks = kernel(
         second_local,
-        (order, weight, basis, residual0, image0, fix0, fix_image, coarse1),
-        [vector, vector, shape(8, cols)] + [block] * 4,
+        (order, weight, basis, residual0, image0, fix0, fix_image, coarse1, info),
+        [vector, vector] + [block] * 2,
         [pltpu.VMEM((dofs, cols), F32)],
     )
     z1, product1, dots, *blocks = kernel(
         second_apply,
-        (order, matrix, local, residual1, z0, *swap(blocks)),
-        [vector, vector, shape(8, cols)] + [block] * 4,
+        (order, matrix, local, residual1, z0, *swap(local, blocks)),
+        [vector, vector, shape(8, cols)] + [block] * 2,
         [wide],
         flops=product_flops,
         aliases={7: 0},
     )
-    arrived = swap(blocks)
-    for mask in (1 << k for k in range(n_sub.bit_length() - 1)):
-        dots = dots + lax.ppermute(dots, "sub", [(k, k ^ mask) for k in range(n_sub)])
+    dots = dots + lax.ppermute(dots, "sub", [(k, k ^ 1) for k in range(n_sub)])
+    blocks[0], dots = lax.optimization_barrier((blocks[0], dots))
+    dots = [dots] + [passed_along(dots, "sub", step) for step in range(2, n_sub, 2)]
+    arrived = swap(product1, blocks)
     (image1,) = kernel(last_image, (order, product1, *arrived), [vector], aliases={4: 0})
-    dots, image1 = lax.optimization_barrier((dots, image1))
-    (copies,) = kernel(add_and_copy, (dots,), [shape(n_grp, 8, cols)], scalars=0)
+    *dots, image1 = lax.optimization_barrier((*dots, image1))
+    (copies,) = kernel(copy_row, dots, [shape(n_grp, 1, 3 * cols)], scalars=0)
     chunks = spread(copies, "grp")
     outs = kernel(
         finish, (chunks, info, z0, z1, image0, image1, residual1), [vector, vector], scalars=0

time: 212 us -> 205 us (0.967)
  blocking collectives: 87.4 us -> 80.5 us
  Pallas kernels: 53.7 us -> 58.1 us
  local copies, waits for them, and re-layouts: 6.12 us -> 3.42 us
  starting transfers between devices: 47.1 us -> 44.5 us
    all_to_all x7, blocking collectives: 87.4 us -> 80.5 us  [spread(): return lax.all_to_all(chunks, axis, 0, 0, axis_index_groups=groups)]
    ppermute x3 -> x1, waiting for transfers between devices: 7.06 us -> 0.82 us  [body(): dots = dots + lax.ppermute(dots, 'sub', [(k, k ^ 1) for k in range(n_sub)])]
    ppermute x20 -> x23, waiting for transfers between devices: 8.33 us -> 14.4 us  [passed_along(): return lax.ppermute(value, axis, pairs)]
    pallas_call x23 -> x28, Pallas kernels: 53.7 us -> 58.1 us  [kernel(): pl.pallas_call(body, out_shape=list(outs), in_specs=specs, out_specs=[VM]...]
    ppermute x3 -> x1, starting transfers between devices: 3.69 us -> 0.82 us  [body(): dots = dots + lax.ppermute(dots, 'sub', [(k, k ^ 1) for k in range(n_sub)])]
    unnamed x24 -> x18, local copies, waits for them, and re-layouts: 6.12 us -> 3.42 us
    ppermute x20 -> x23, starting transfers between devices: 40.5 us -> 40.7 us  [passed_along(): return lax.ppermute(value, axis, pairs)]
  transfers between devices with their start and end apart: 29 -> 30, of which waited for: 10 -> 10; matrix products, arithmetic and copies ran while one was open for 0% -> 0% of each run, Pallas kernels for 8% -> 12%
where the time goes in v4:
time: 205 us; the launch traced here: 203 us
  blocking collectives  80.5 us (39%)
  Pallas kernels  58.1 us (28%)
  starting transfers between devices  44.5 us (22%)
  waiting for transfers between devices  15.2 us (7%)
  local copies, waits for them, and re-layouts  3.42 us (2%)
    all_to_all x7, blocking collectives, spread(): return lax.all_to_all(chunks, axis, 0, 0, axis_index_groups=groups)  80.5 us
    pallas_call x28, Pallas kernels, kernel(): pl.pallas_call(body, out_shape=list(outs), in_specs=specs, out_specs=[VM]...  58.1 us
    ppermute x23, starting transfers between devices, passed_along(): return lax.ppermute(value, axis, pairs)  40.7 us
    ppermute x23, waiting for transfers between devices, passed_along(): return lax.ppermute(value, axis, pairs)  14.4 us
  transfers between devices with their start and end apart: 30, of which 10 were waited for; matrix products, arithmetic and copies ran while one was open for 0% of the time, Pallas kernels for 12%

profile of v4, /device:TPU:1, one launch (start us, length us, event | category | flops | bytes accessed | tf_op | source)
XLA Modules:
  0.0 202.7 jit_solution(13026930196861436242)
XLA Ops:
  0.7 5.8 %open_faces.1 = (f32[520,128]{1,0:T(8,128)}, f32[520,128]{1,0:T(8,128)}, f32[520,128]{1,0:T(8,128)}, f32[520,128]{1,0:T(8,128)}) custom-call(s32[1,2048]{1,0:T(1,128)} %bitcast.22, f32[2048,128]{1,0:T(8,128)} %bitcast.20, f32[1,2048]{1,0:T(1,128)} %bitcast.44), custom_call_target="tpu_custom_call" | custom-call | bytes 2129920 | tf_op jit(solution)/shard_map/open_faces/pallas_call | solution.py:29
  6.5 2.2 %collective-permute-start = (f32[520,128]{1,0:T(8,128)}, f32[520,128]{1,0:T(8,128)S(1)}, u32[]{:S(2)}, u32[]{:S(2)}) collective-permute-start(f32[520,128]{1,0:T(8,128)} %get-tuple-element.76), channel_id=1, source_target_pairs={{0,1},{1,2},{2,3},{3,4},{4,5},{5,6},{6,7},{7,8},{8,9},{9,10},{10,1... | collective-permute-start | bytes 798728 | tf_op jit(solution)/shard_map/ppermute | solution.py:363
  8.7 6.8 %collective-permute-start.1 = (f32[520,128]{1,0:T(8,128)}, f32[520,128]{1,0:T(8,128)S(1)}, u32[]{:S(2)}, u32[]{:S(2)}) collective-permute-start(f32[520,128]{1,0:T(8,128)} %get-tuple-element.77), channel_id=1, source_target_pairs={{0,31},{1,0},{2,1},{3,2},{4,3},{5,4},{6,5},{7,6},{8,7},{9,8},{10,9... | collective-permute-start | bytes 798728 | tf_op jit(solution)/shard_map/ppermute | solution.py:363
  17.6 3.4 %copy-done = bf16[1,1,2048,2048]{3,2,1,0:T(8,128)(2,1)S(1)} copy-done((bf16[1,1,2048,2048]{3,2,1,0:T(8,128)(2,1)S(1)}, bf16[1,1,2048,2048]{3,2,1,0:T(8,128)(2,1)}, u32[]{:S(2)}) %copy-start) | copy-done | bytes 8388632
  22.2 2.2 %open_sub.1 = (f32[2048,128]{1,0:T(8,128)S(1)}, f32[2048,128]{1,0:T(8,128)S(1)}) custom-call(s32[1,2048]{1,0:T(1,128)S(1)} %bitcast.23, f32[520,128]{1,0:T(8,128)S(1)} %collective-permute-done.2.one, f32[520,128]{1,0:T(8,128)S(1)} %collective-permute-done.3.two), custom_call_target="tpu_custom_call" | custom-call | bytes 2637824 | tf_op jit(solution)/shard_map/open_sub/pallas_call | solution.py:29
  24.4 3.0 %open_join.1 = (f32[2048,128]{1,0:T(8,128)S(1)}, f32[2048,128]{1,0:T(8,128)S(1)}, f32[2048,128]{1,0:T(8,128)S(1)}, f32[2048,128]{1,0:T(8,128)S(1)}, f32[128,256]{1,0:T(8,128)S(1)}) custom-call(s32[1,2048]{1,0:T(1,128)S(1)} %bitcast.24, f32[2048,128]{1,0:T(8,128)S(1)} %bitcast.21, ...), custom_call_target="tpu_custom_call", output_to_operand_aliasing={{0}: (6, {}), {1}: (7, {})} | custom-call | bytes 9068544 | tf_op jit(solution)/shard_map/open_join/pallas_call | solution.py:29
  27.4 11.3 %all_to_all.35.chunks = f32[8,16,256]{2,1,0:T(8,128)S(1)} all-to-all(f32[8,16,256]{2,1,0:T(8,128)S(1)} %bitcast.43), channel_id=1, replica_groups=mesh['sub'=8,'grp'=32] {'sub'}, dimensions={0} | all-to-all | bytes 262144 | tf_op jit(solution)/shard_map/all_to_all | solution.py:381
  40.5 4.9 %local_fix.2.fix.fix_first = f32[2048,128]{1,0:T(8,128)S(1)} custom-call(bf16[2048,2048]{1,0:T(8,128)(2,1)S(1)} %bitcast.12, f32[2048,128]{1,0:T(8,128)S(1)} %get-tuple-element.90.weighted, f32[2048,128]{1,0:T(8,128)S(1)} %read_diagonal.1.diagonal), custom_call_target="tpu_custom_call" | custom-call | flops 4294967296 | bytes 11534336 | tf_op jit(solution)/shard_map/local_fix/pallas_call | solution.py:29
  45.5 13.6 %all_to_all.36.chunks = f32[8,16,256]{2,1,0:T(8,128)S(1)} all-to-all(f32[8,16,256]{2,1,0:T(8,128)S(1)} %add_and_copy.2), channel_id=1, replica_groups={{0,4,8,12,16,20,24,28},{1,5,9,13,17,21,25,29},{2,6,10,14,18,22,26,30},{..., dimensions={0} | all-to-all | bytes 262144 | tf_op jit(solution)/shard_map/all_to_all | solution.py:381
  60.2 10.5 %all_to_all.37 = f32[8,16,256]{2,1,0:T(8,128)S(1)} all-to-all(f32[8,16,256]{2,1,0:T(8,128)S(1)} %get-tuple-element.97), channel_id=1, replica_groups=mesh['sub'=8,'grp'=32] {'sub'}, dimensions={0} | all-to-all | bytes 262144 | tf_op jit(solution)/shard_map/all_to_all | solution.py:381
  72.8 2.4 %collective-permute-start.9 = (f32[512,128]{1,0:T(8,128)S(1)}, f32[512,128]{1,0:T(8,128)S(1)}, u32[]{:S(2)}, u32[]{:S(2)}) collective-permute-start(f32[512,128]{1,0:T(8,128)S(1)} %get-tuple-element.101), channel_id=1, source_target_pairs={{0,1},{1,2},{2,3},{3,4},{4,5},{5,6},{6,7},{7,8},{8,9},{9,10},{10,1... | collective-permute-start | bytes 786440 | tf_op jit(solution)/shard_map/ppermute | solution.py:363
  75.2 2.5 %collective-permute-start.10 = (f32[512,128]{1,0:T(8,128)S(1)}, f32[512,128]{1,0:T(8,128)S(1)}, u32[]{:S(2)}, u32[]{:S(2)}) collective-permute-start(f32[512,128]{1,0:T(8,128)S(1)} %get-tuple-element.102), channel_id=1, source_target_pairs={{0,31},{1,0},{2,1},{3,2},{4,3},{5,4},{6,5},{7,6},{8,7},{9,8},{10,9... | collective-permute-start | bytes 786440 | tf_op jit(solution)/shard_map/ppermute | solution.py:363
  81.0 2.2 %collective-permute-done.9.three = f32[512,128]{1,0:T(8,128)S(1)} collective-permute-done((f32[512,128]{1,0:T(8,128)S(1)}, f32[512,128]{1,0:T(8,128)S(1)}, u32[]{:S(2)}, u32[]{:S(2)}) %collective-permute-start.9) | collective-permute-done | bytes 262176 | tf_op jit(solution)/shard_map/ppermute | solution.py:363
  84.8 2.2 %collective-permute-done.8.two = f32[512,128]{1,0:T(8,128)S(1)} collective-permute-done((f32[512,128]{1,0:T(8,128)S(1)}, f32[512,128]{1,0:T(8,128)S(1)}, u32[]{:S(2)}, u32[]{:S(2)}) %collective-permute-start.8) | collective-permute-done | bytes 262176 | tf_op jit(solution)/shard_map/ppermute | solution.py:363
  87.0 5.5 %first_apply.1 = (f32[2048,128]{1,0:T(8,128)S(1)}, f32[2048,128]{1,0:T(8,128)S(1)}, f32[8,128]{1,0:T(8,128)S(1)}, f32[512,128]{1,0:T(8,128)S(1)}, f32[512,128]{1,0:T(8,128)S(1)}) custom-call(s32[1,2048]{1,0:T(1,128)S(1)} %bitcast.28, bf16[2048,2048]{1,0:T(8,128)(2,1)S(1)} %bitcast.13, ...), custom_call_target="tpu_custom_call", output_to_operand_aliasing={{0}: (6, {})} | custom-call | flops 2147483648 | bytes 14692352 | tf_op jit(solution)/shard_map/first_apply/pallas_call | solution.py:29
  92.6 4.8 %collective-permute-start.14 = (f32[512,128]{1,0:T(8,128)S(1)}, f32[512,128]{1,0:T(8,128)S(1)}, u32[]{:S(2)}, u32[]{:S(2)}) collective-permute-start(f32[512,128]{1,0:T(8,128)S(1)} %get-tuple-element.107), channel_id=1, source_target_pairs={{0,31},{1,0},{2,1},{3,2},{4,3},{5,4},{6,5},{7,6},{8,7},{9,8},{10,9... | collective-permute-start | bytes 786440 | tf_op jit(solution)/shard_map/ppermute | solution.py:363
  100.4 2.7 %collective-permute-done.13.three = f32[512,128]{1,0:T(8,128)S(1)} collective-permute-done((f32[512,128]{1,0:T(8,128)S(1)}, f32[512,128]{1,0:T(8,128)S(1)}, u32[]{:S(2)}, u32[]{:S(2)}) %collective-permute-start.13) | collective-permute-done | bytes 262176 | tf_op jit(solution)/shard_map/ppermute | solution.py:363
  105.4 2.3 %image_partial.1 = (f32[2048,128]{1,0:T(8,128)S(1)}, f32[2048,128]{1,0:T(8,128)S(1)}, f32[8,40,128]{2,1,0:T(8,128)S(1)}) custom-call(s32[1,2048]{1,0:T(1,128)S(1)} %bitcast.31, f32[2048,128]{1,0:T(8,128)S(1)} %get-tuple-element.103.source.product, f32[2048,128]{1,0:T(8,128)S(1)} %get-tuple-element.84.weight, ...), custom_call_target="tpu_custom_call", output_to_operand_aliasing={{0}: (5, {})} | custom-call | bytes 6991872 | tf_op jit(solution)/shard_map/image_partial/pallas_call | solution.py:29
  107.7 11.5 %all_to_all.38.chunks = f32[8,40,128]{2,1,0:T(8,128)S(1)} all-to-all(f32[8,40,128]{2,1,0:T(8,128)S(1)} %get-tuple-element.110), channel_id=1, replica_groups=mesh['sub'=8,'grp'=32] {'sub'}, dimensions={0} | all-to-all | bytes 327680 | tf_op jit(solution)/shard_map/all_to_all | solution.py:381
  121.1 4.8 %local_fix.3.fix_image = f32[2048,128]{1,0:T(8,128)S(1)} custom-call(bf16[2048,2048]{1,0:T(8,128)(2,1)S(1)} %bitcast.14, f32[2048,128]{1,0:T(8,128)S(1)} %get-tuple-element.114.weighted, f32[2048,128]{1,0:T(8,128)S(1)} %read_diagonal.1.diagonal), custom_call_target="tpu_custom_call" | custom-call | flops 4294967296 | bytes 11534336 | tf_op jit(solution)/shard_map/local_fix/pallas_call | solution.py:29
  125.9 11.0 %all_to_all.39.chunks = f32[8,40,128]{2,1,0:T(8,128)S(1)} all-to-all(f32[8,40,128]{2,1,0:T(8,128)S(1)} %add_and_copy.3), channel_id=1, replica_groups={{0,4,8,12,16,20,24,28},{1,5,9,13,17,21,25,29},{2,6,10,14,18,22,26,30},{..., dimensions={0} | all-to-all | bytes 327680 | tf_op jit(solution)/shard_map/all_to_all | solution.py:381
  138.2 10.5 %all_to_all.40 = f32[8,16,256]{2,1,0:T(8,128)S(1)} all-to-all(f32[8,16,256]{2,1,0:T(8,128)S(1)} %get-tuple-element.121), channel_id=1, replica_groups=mesh['sub'=8,'grp'=32] {'sub'}, dimensions={0} | all-to-all | bytes 262144 | tf_op jit(solution)/shard_map/all_to_all | solution.py:381
  148.6 2.2 %second_local.1 = (f32[2048,128]{1,0:T(8,128)S(1)}, f32[2048,128]{1,0:T(8,128)S(1)}, f32[512,128]{1,0:T(8,128)S(1)}, f32[512,128]{1,0:T(8,128)S(1)}) custom-call(s32[1,2048]{1,0:T(1,128)S(1)} %bitcast.32, f32[2048,128]{1,0:T(8,128)S(1)} %get-tuple-element.84.weight, bf16[2048,256]{1,0:T(8,128)(2,1)S(1)} %bitcast.19, ...), custom_call_target="tpu_custom_call" | custom-call | bytes 9056256 | tf_op jit(solution)/shard_map/second_local/pallas_call | solution.py:29
  150.9 2.4 %collective-permute-start.20 = (f32[512,128]{1,0:T(8,128)S(1)}, f32[512,128]{1,0:T(8,128)S(1)}, u32[]{:S(2)}, u32[]{:S(2)}) collective-permute-start(f32[512,128]{1,0:T(8,128)S(1)} %get-tuple-element.128), channel_id=1, source_target_pairs={{0,1},{1,2},{2,3},{3,4},{4,5},{5,6},{6,7},{7,8},{8,9},{9,10},{10,1... | collective-permute-start | bytes 786440 | tf_op jit(solution)/shard_map/ppermute | solution.py:363
  153.2 2.5 %collective-permute-start.21 = (f32[512,128]{1,0:T(8,128)S(1)}, f32[512,128]{1,0:T(8,128)S(1)}, u32[]{:S(2)}, u32[]{:S(2)}) collective-permute-start(f32[512,128]{1,0:T(8,128)S(1)} %get-tuple-element.129), channel_id=1, source_target_pairs={{0,31},{1,0},{2,1},{3,2},{4,3},{5,4},{6,5},{7,6},{8,7},{9,8},{10,9... | collective-permute-start | bytes 786440 | tf_op jit(solution)/shard_map/ppermute | solution.py:363
  159.0 2.2 %collective-permute-done.20.three = f32[512,128]{1,0:T(8,128)S(1)} collective-permute-done((f32[512,128]{1,0:T(8,128)S(1)}, f32[512,128]{1,0:T(8,128)S(1)}, u32[]{:S(2)}, u32[]{:S(2)}) %collective-permute-start.20) | collective-permute-done | bytes 262176 | tf_op jit(solution)/shard_map/ppermute | solution.py:363
  162.8 2.2 %collective-permute-done.19.two = f32[512,128]{1,0:T(8,128)S(1)} collective-permute-done((f32[512,128]{1,0:T(8,128)S(1)}, f32[512,128]{1,0:T(8,128)S(1)}, u32[]{:S(2)}, u32[]{:S(2)}) %collective-permute-start.19) | collective-permute-done | bytes 262176 | tf_op jit(solution)/shard_map/ppermute | solution.py:363
  165.1 5.5 %second_apply.1 = (f32[2048,128]{1,0:T(8,128)S(1)}, f32[2048,128]{1,0:T(8,128)S(1)}, f32[8,128]{1,0:T(8,128)S(1)}, f32[512,128]{1,0:T(8,128)S(1)}, f32[512,128]{1,0:T(8,128)S(1)}) custom-call(s32[1,2048]{1,0:T(1,128)S(1)} %bitcast.35, bf16[2048,2048]{1,0:T(8,128)(2,1)S(1)} %bitcast.15, ...), custom_call_target="tpu_custom_call", output_to_operand_aliasing={{0}: (7, {})} | custom-call | flops 2147483648 | bytes 15740928 | tf_op jit(solution)/shard_map/second_apply/pallas_call | solution.py:29
  172.2 4.0 %collective-permute-start.29 = (f32[512,128]{1,0:T(8,128)S(1)}, f32[512,128]{1,0:T(8,128)S(1)}, u32[]{:S(2)}, u32[]{:S(2)}) collective-permute-start(f32[512,128]{1,0:T(8,128)S(1)} %get-tuple-element.137), channel_id=1, source_target_pairs={{0,31},{1,0},{2,1},{3,2},{4,3},{5,4},{6,5},{7,6},{8,7},{9,8},{10,9... | collective-permute-start | bytes 786440 | tf_op jit(solution)/shard_map/ppermute | solution.py:363
  178.5 3.0 %collective-permute-start.25 = (f32[8,128]{1,0:T(8,128)S(1)}, f32[8,128]{1,0:T(8,128)S(1)}, u32[]{:S(2)}, u32[]{:S(2)}) collective-permute-start(f32[8,128]{1,0:T(8,128)S(1)} %add.3.refs_0_), channel_id=1, source_target_pairs={{0,192},{32,224},{64,0},{96,32},{128,64},{160,96},{192,128},{224,1... | collective-permute-start | bytes 12296 | tf_op jit(solution)/shard_map/ppermute | solution.py:363
  183.0 2.4 %collective-permute-start.23 = (f32[8,128]{1,0:T(8,128)S(1)}, f32[8,128]{1,0:T(8,128)S(1)}, u32[]{:S(2)}, u32[]{:S(2)}) collective-permute-start(f32[8,128]{1,0:T(8,128)S(1)} %add.3.refs_0_), channel_id=1, source_target_pairs={{0,64},{32,96},{64,128},{96,160},{128,192},{160,224},{192,0},{224,... | collective-permute-start | bytes 12296 | tf_op jit(solution)/shard_map/ppermute | solution.py:363
  188.8 12.2 %all_to_all.41.chunks = f32[32,1,384]{2,1,0:T(1,128)S(1)} all-to-all(f32[32,1,384]{2,1,0:T(1,128)S(1)} %copy_row.1), channel_id=1, replica_groups=mesh['sub'=8,'grp'=32] {'grp'}, dimensions={0} | all-to-all | bytes 98304 | tf_op jit(solution)/shard_map/all_to_all | solution.py:381
  (82 shorter events, 37.0 us)
Async XLA Ops:
  0.7 38.0 %copy-start.8 = (s32[1,256]{1,0:T(1,128)S(1)}, s32[1,256]{1,0:T(1,128)}, u32[]{:S(2)}) copy-start(s32[1,256]{1,0:T(1,128)} %members.7) | copy-start | bytes 3076
  6.5 15.3 %collective-permute-start = (f32[520,128]{1,0:T(8,128)}, f32[520,128]{1,0:T(8,128)S(1)}, u32[]{:S(2)}, u32[]{:S(2)}) collective-permute-start(f32[520,128]{1,0:T(8,128)} %get-tuple-element.76), channel_id=1, source_target_pairs={{0,1},{1,2},{2,3},{3,4},{4,5},{5,6},{6,7},{7,8},{8,9},{9,10},{10,1... | collective-permute-start | bytes 798728 | tf_op jit(solution)/shard_map/ppermute | solution.py:363
  8.7 13.1 %collective-permute-start.1 = (f32[520,128]{1,0:T(8,128)}, f32[520,128]{1,0:T(8,128)S(1)}, u32[]{:S(2)}, u32[]{:S(2)}) collective-permute-start(f32[520,128]{1,0:T(8,128)} %get-tuple-element.77), channel_id=1, source_target_pairs={{0,31},{1,0},{2,1},{3,2},{4,3},{5,4},{6,5},{7,6},{8,7},{9,8},{10,9... | collective-permute-start | bytes 798728 | tf_op jit(solution)/shard_map/ppermute | solution.py:363
  15.5 6.7 %collective-permute-start.3 = (f32[520,128]{1,0:T(8,128)}, f32[520,128]{1,0:T(8,128)S(1)}, u32[]{:S(2)}, u32[]{:S(2)}) collective-permute-start(f32[520,128]{1,0:T(8,128)} %get-tuple-element.81), channel_id=1, source_target_pairs={{0,224},{32,0},{64,32},{96,64},{128,96},{160,128},{192,160},{224,1... | collective-permute-start | bytes 798728 | tf_op jit(solution)/shard_map/ppermute | solution.py:363
  16.4 5.7 %collective-permute-start.2 = (f32[520,128]{1,0:T(8,128)}, f32[520,128]{1,0:T(8,128)S(1)}, u32[]{:S(2)}, u32[]{:S(2)}) collective-permute-start(f32[520,128]{1,0:T(8,128)} %get-tuple-element.80), channel_id=1, source_target_pairs={{0,32},{32,64},{64,96},{96,128},{128,160},{160,192},{192,224},{224... | collective-permute-start | bytes 798728 | tf_op jit(solution)/shard_map/ppermute | solution.py:363
  27.4 31.7 %copy-start.5 = (f32[1,256,256]{2,1,0:T(8,128)S(1)}, f32[1,256,256]{2,1,0:T(8,128)}, u32[]{:S(2)}) copy-start(f32[1,256,256]{2,1,0:T(8,128)} %param.14) | copy-start | bytes 786436
  39.0 6.5 %collective-permute-start.6 = (f32[16,256]{1,0:T(8,128)S(1)}, f32[16,256]{1,0:T(8,128)S(1)}, u32[]{:S(2)}, u32[]{:S(2)}) collective-permute-start(f32[16,256]{1,0:T(8,128)S(1)} %get-tuple-element.89.refs_0_), channel_id=1, source_target_pairs={{0,3},{1,0},{2,1},{3,2},{4,7},{5,4},{6,5},{7,6},{8,11},{9,8},{10,9... | collective-permute-start | bytes 49160 | tf_op jit(solution)/shard_map/ppermute | solution.py:368
  39.0 6.5 %collective-permute-start.5 = (f32[16,256]{1,0:T(8,128)S(1)}, f32[16,256]{1,0:T(8,128)S(1)}, u32[]{:S(2)}, u32[]{:S(2)}) collective-permute-start(f32[16,256]{1,0:T(8,128)S(1)} %get-tuple-element.89.refs_0_), channel_id=1, source_target_pairs={{0,2},{1,3},{2,0},{3,1},{4,6},{5,7},{6,4},{7,5},{8,10},{9,11},{10,... | collective-permute-start | bytes 49160 | tf_op jit(solution)/shard_map/ppermute | solution.py:368
  39.1 6.4 %collective-permute-start.4 = (f32[16,256]{1,0:T(8,128)S(1)}, f32[16,256]{1,0:T(8,128)S(1)}, u32[]{:S(2)}, u32[]{:S(2)}) collective-permute-start(f32[16,256]{1,0:T(8,128)S(1)} %get-tuple-element.89.refs_0_), channel_id=1, source_target_pairs={{0,1},{1,2},{2,3},{3,0},{4,5},{5,6},{6,7},{7,4},{8,9},{9,10},{10,1... | collective-permute-start | bytes 49160 | tf_op jit(solution)/shard_map/ppermute | solution.py:368
  72.8 10.4 %collective-permute-start.9 = (f32[512,128]{1,0:T(8,128)S(1)}, f32[512,128]{1,0:T(8,128)S(1)}, u32[]{:S(2)}, u32[]{:S(2)}) collective-permute-start(f32[512,128]{1,0:T(8,128)S(1)} %get-tuple-element.101), channel_id=1, source_target_pairs={{0,1},{1,2},{2,3},{3,4},{4,5},{5,6},{6,7},{7,8},{8,9},{9,10},{10,1... | collective-permute-start | bytes 786440 | tf_op jit(solution)/shard_map/ppermute | solution.py:363
  75.2 8.0 %collective-permute-start.10 = (f32[512,128]{1,0:T(8,128)S(1)}, f32[512,128]{1,0:T(8,128)S(1)}, u32[]{:S(2)}, u32[]{:S(2)}) collective-permute-start(f32[512,128]{1,0:T(8,128)S(1)} %get-tuple-element.102), channel_id=1, source_target_pairs={{0,31},{1,0},{2,1},{3,2},{4,3},{5,4},{6,5},{7,6},{8,7},{9,8},{10,9... | collective-permute-start | bytes 786440 | tf_op jit(solution)/shard_map/ppermute | solution.py:363
  79.3 5.5 %collective-permute-start.7 = (f32[512,128]{1,0:T(8,128)S(1)}, f32[512,128]{1,0:T(8,128)S(1)}, u32[]{:S(2)}, u32[]{:S(2)}) collective-permute-start(f32[512,128]{1,0:T(8,128)S(1)} %get-tuple-element.99), channel_id=1, source_target_pairs={{0,32},{32,64},{64,96},{96,128},{128,160},{160,192},{192,224},{224... | collective-permute-start | bytes 786440 | tf_op jit(solution)/shard_map/ppermute | solution.py:363
  81.0 6.1 %collective-permute-start.8 = (f32[512,128]{1,0:T(8,128)S(1)}, f32[512,128]{1,0:T(8,128)S(1)}, u32[]{:S(2)}, u32[]{:S(2)}) collective-permute-start(f32[512,128]{1,0:T(8,128)S(1)} %get-tuple-element.100), channel_id=1, source_target_pairs={{0,224},{32,0},{64,32},{96,64},{128,96},{160,128},{192,160},{224,1... | collective-permute-start | bytes 786440 | tf_op jit(solution)/shard_map/ppermute | solution.py:363
  92.6 10.5 %collective-permute-start.13 = (f32[512,128]{1,0:T(8,128)S(1)}, f32[512,128]{1,0:T(8,128)S(1)}, u32[]{:S(2)}, u32[]{:S(2)}) collective-permute-start(f32[512,128]{1,0:T(8,128)S(1)} %get-tuple-element.106), channel_id=1, source_target_pairs={{0,1},{1,2},{2,3},{3,4},{4,5},{5,6},{6,7},{7,8},{8,9},{9,10},{10,1... | collective-permute-start | bytes 786440 | tf_op jit(solution)/shard_map/ppermute | solution.py:363
  92.6 10.4 %collective-permute-start.14 = (f32[512,128]{1,0:T(8,128)S(1)}, f32[512,128]{1,0:T(8,128)S(1)}, u32[]{:S(2)}, u32[]{:S(2)}) collective-permute-start(f32[512,128]{1,0:T(8,128)S(1)} %get-tuple-element.107), channel_id=1, source_target_pairs={{0,31},{1,0},{2,1},{3,2},{4,3},{5,4},{6,5},{7,6},{8,7},{9,8},{10,9... | collective-permute-start | bytes 786440 | tf_op jit(solution)/shard_map/ppermute | solution.py:363
  99.1 5.6 %collective-permute-start.11 = (f32[512,128]{1,0:T(8,128)S(1)}, f32[512,128]{1,0:T(8,128)S(1)}, u32[]{:S(2)}, u32[]{:S(2)}) collective-permute-start(f32[512,128]{1,0:T(8,128)S(1)} %get-tuple-element.104), channel_id=1, source_target_pairs={{0,32},{32,64},{64,96},{96,128},{128,160},{160,192},{192,224},{224... | collective-permute-start | bytes 786440 | tf_op jit(solution)/shard_map/ppermute | solution.py:363
  99.3 6.1 %collective-permute-start.12 = (f32[512,128]{1,0:T(8,128)S(1)}, f32[512,128]{1,0:T(8,128)S(1)}, u32[]{:S(2)}, u32[]{:S(2)}) collective-permute-start(f32[512,128]{1,0:T(8,128)S(1)} %get-tuple-element.105), channel_id=1, source_target_pairs={{0,224},{32,0},{64,32},{96,64},{128,96},{160,128},{192,160},{224,1... | collective-permute-start | bytes 786440 | tf_op jit(solution)/shard_map/ppermute | solution.py:363
  119.6 6.3 %collective-permute-start.17 = (f32[40,128]{1,0:T(8,128)S(1)}, f32[40,128]{1,0:T(8,128)S(1)}, u32[]{:S(2)}, u32[]{:S(2)}) collective-permute-start(f32[40,128]{1,0:T(8,128)S(1)} %get-tuple-element.113.refs_0_), channel_id=1, source_target_pairs={{0,3},{1,0},{2,1},{3,2},{4,7},{5,4},{6,5},{7,6},{8,11},{9,8},{10,9... | collective-permute-start | bytes 61448 | tf_op jit(solution)/shard_map/ppermute | solution.py:368
  119.6 6.3 %collective-permute-start.16 = (f32[40,128]{1,0:T(8,128)S(1)}, f32[40,128]{1,0:T(8,128)S(1)}, u32[]{:S(2)}, u32[]{:S(2)}) collective-permute-start(f32[40,128]{1,0:T(8,128)S(1)} %get-tuple-element.113.refs_0_), channel_id=1, source_target_pairs={{0,2},{1,3},{2,0},{3,1},{4,6},{5,7},{6,4},{7,5},{8,10},{9,11},{10,... | collective-permute-start | bytes 61448 | tf_op jit(solution)/shard_map/ppermute | solution.py:368
  119.7 6.2 %collective-permute-start.15 = (f32[40,128]{1,0:T(8,128)S(1)}, f32[40,128]{1,0:T(8,128)S(1)}, u32[]{:S(2)}, u32[]{:S(2)}) collective-permute-start(f32[40,128]{1,0:T(8,128)S(1)} %get-tuple-element.113.refs_0_), channel_id=1, source_target_pairs={{0,1},{1,2},{2,3},{3,0},{4,5},{5,6},{6,7},{7,4},{8,9},{9,10},{10,1... | collective-permute-start | bytes 61448 | tf_op jit(solution)/shard_map/ppermute | solution.py:368
  150.9 10.4 %collective-permute-start.20 = (f32[512,128]{1,0:T(8,128)S(1)}, f32[512,128]{1,0:T(8,128)S(1)}, u32[]{:S(2)}, u32[]{:S(2)}) collective-permute-start(f32[512,128]{1,0:T(8,128)S(1)} %get-tuple-element.128), channel_id=1, source_target_pairs={{0,1},{1,2},{2,3},{3,4},{4,5},{5,6},{6,7},{7,8},{8,9},{9,10},{10,1... | collective-permute-start | bytes 786440 | tf_op jit(solution)/shard_map/ppermute | solution.py:363
  153.2 8.0 %collective-permute-start.21 = (f32[512,128]{1,0:T(8,128)S(1)}, f32[512,128]{1,0:T(8,128)S(1)}, u32[]{:S(2)}, u32[]{:S(2)}) collective-permute-start(f32[512,128]{1,0:T(8,128)S(1)} %get-tuple-element.129), channel_id=1, source_target_pairs={{0,31},{1,0},{2,1},{3,2},{4,3},{5,4},{6,5},{7,6},{8,7},{9,8},{10,9... | collective-permute-start | bytes 786440 | tf_op jit(solution)/shard_map/ppermute | solution.py:363
  157.4 5.5 %collective-permute-start.18 = (f32[512,128]{1,0:T(8,128)S(1)}, f32[512,128]{1,0:T(8,128)S(1)}, u32[]{:S(2)}, u32[]{:S(2)}) collective-permute-start(f32[512,128]{1,0:T(8,128)S(1)} %get-tuple-element.126), channel_id=1, source_target_pairs={{0,32},{32,64},{64,96},{96,128},{128,160},{160,192},{192,224},{224... | collective-permute-start | bytes 786440 | tf_op jit(solution)/shard_map/ppermute | solution.py:363
  159.0 6.1 %collective-permute-start.19 = (f32[512,128]{1,0:T(8,128)S(1)}, f32[512,128]{1,0:T(8,128)S(1)}, u32[]{:S(2)}, u32[]{:S(2)}) collective-permute-start(f32[512,128]{1,0:T(8,128)S(1)} %get-tuple-element.127), channel_id=1, source_target_pairs={{0,224},{32,0},{64,32},{96,64},{128,96},{160,128},{192,160},{224,1... | collective-permute-start | bytes 786440 | tf_op jit(solution)/shard_map/ppermute | solution.py:363
  170.6 1.6 collective-permute-start.22
  171.4 11.2 %collective-permute-start.28 = (f32[512,128]{1,0:T(8,128)S(1)}, f32[512,128]{1,0:T(8,128)S(1)}, u32[]{:S(2)}, u32[]{:S(2)}) collective-permute-start(f32[512,128]{1,0:T(8,128)S(1)} %get-tuple-element.136), channel_id=1, source_target_pairs={{0,1},{1,2},{2,3},{3,4},{4,5},{5,6},{6,7},{7,8},{8,9},{9,10},{10,1... | collective-permute-start | bytes 786440 | tf_op jit(solution)/shard_map/ppermute | solution.py:363
  172.2 10.8 %collective-permute-start.29 = (f32[512,128]{1,0:T(8,128)S(1)}, f32[512,128]{1,0:T(8,128)S(1)}, u32[]{:S(2)}, u32[]{:S(2)}) collective-permute-start(f32[512,128]{1,0:T(8,128)S(1)} %get-tuple-element.137), channel_id=1, source_target_pairs={{0,31},{1,0},{2,1},{3,2},{4,3},{5,4},{6,5},{7,6},{8,7},{9,8},{10,9... | collective-permute-start | bytes 786440 | tf_op jit(solution)/shard_map/ppermute | solution.py:363
  177.8 9.2 %collective-permute-start.26 = (f32[512,128]{1,0:T(8,128)S(1)}, f32[512,128]{1,0:T(8,128)S(1)}, u32[]{:S(2)}, u32[]{:S(2)}) collective-permute-start(f32[512,128]{1,0:T(8,128)S(1)} %get-tuple-element.134), channel_id=1, source_target_pairs={{0,32},{32,64},{64,96},{96,128},{128,160},{160,192},{192,224},{224... | collective-permute-start | bytes 786440 | tf_op jit(solution)/shard_map/ppermute | solution.py:363
  178.3 8.8 %collective-permute-start.27 = (f32[512,128]{1,0:T(8,128)S(1)}, f32[512,128]{1,0:T(8,128)S(1)}, u32[]{:S(2)}, u32[]{:S(2)}) collective-permute-start(f32[512,128]{1,0:T(8,128)S(1)} %get-tuple-element.135), channel_id=1, source_target_pairs={{0,224},{32,0},{64,32},{96,64},{128,96},{160,128},{192,160},{224,1... | collective-permute-start | bytes 786440 | tf_op jit(solution)/shard_map/ppermute | solution.py:363
  178.5 10.2 %collective-permute-start.25 = (f32[8,128]{1,0:T(8,128)S(1)}, f32[8,128]{1,0:T(8,128)S(1)}, u32[]{:S(2)}, u32[]{:S(2)}) collective-permute-start(f32[8,128]{1,0:T(8,128)S(1)} %add.3.refs_0_), channel_id=1, source_target_pairs={{0,192},{32,224},{64,0},{96,32},{128,64},{160,96},{192,128},{224,1... | collective-permute-start | bytes 12296 | tf_op jit(solution)/shard_map/ppermute | solution.py:363
  182.6 6.2 %collective-permute-start.24 = (f32[8,128]{1,0:T(8,128)S(1)}, f32[8,128]{1,0:T(8,128)S(1)}, u32[]{:S(2)}, u32[]{:S(2)}) collective-permute-start(f32[8,128]{1,0:T(8,128)S(1)} %add.3.refs_0_), channel_id=1, source_target_pairs={{0,128},{32,160},{64,192},{96,224},{128,0},{160,32},{192,64},{224,... | collective-permute-start | bytes 12296 | tf_op jit(solution)/shard_map/ppermute | solution.py:363
  183.0 5.8 %collective-permute-start.23 = (f32[8,128]{1,0:T(8,128)S(1)}, f32[8,128]{1,0:T(8,128)S(1)}, u32[]{:S(2)}, u32[]{:S(2)}) collective-permute-start(f32[8,128]{1,0:T(8,128)S(1)} %add.3.refs_0_), channel_id=1, source_target_pairs={{0,64},{32,96},{64,128},{96,160},{128,192},{160,224},{192,0},{224,... | collective-permute-start | bytes 12296 | tf_op jit(solution)/shard_map/ppermute | solution.py:363
  (7 other events, 126.9 us)

commit v5 on v4

--- a/solution.py
+++ b/solution.py
@@ -12,8 +12,8 @@
 BF = jnp.bfloat16
 F32 = jnp.float32
 LANES = 128
-GATHER = 32
-CHUNK = 512
+GATHER = 64
+CHUNK = 256
 VM = pl.BlockSpec(memory_space=pltpu.VMEM)
 SM = pl.BlockSpec(memory_space=pltpu.SMEM)
 HB = pl.BlockSpec(memory_space=pltpu.HBM)
@@ -176,14 +176,18 @@
         chunked(matrix.shape[0], work)
 
 
-def read_diagonal(matrix, diagonal):
+def prepare(matrix, members, inverse_two, rhs, diagonal, table_two, kept):
+    kept[...] = rhs[...]
+    table = membership_table(members, inverse_two.shape[0])
+    table_two[...] = dot(inverse_two[...], table, ((0,), (0,)), HIGH)
     for start in range(0, matrix.shape[0], LANES):
         square = matrix[pl.ds(start, LANES), pl.ds(start, LANES)].astype(F32)
         column = jnp.sum(jnp.where(eye(), square, 0.0), axis=1, keepdims=True)
         diagonal[pl.ds(start, LANES), :] = jnp.broadcast_to(column, (LANES, LANES))
 
 
-def local_fix(matrix, weighted, diagonal, fix, wide):
+def local_fix(matrix, weighted, diagonal, total, inverse_one, fix, part_one, wide):
+    part_one[...] = dot(total[...], inverse_one[...], ((1,), (1,)), HIGH)
     sweeps(matrix, weighted, diagonal, fix, wide)
 
 
@@ -289,29 +293,20 @@
         refs[-1][k] = value
 
 
-def coarse_solve(total, two, members, inverse_one, inverse_two):
-    solved = dot(two, inverse_two[...], ((1,), (1,)), HIGH)
-    table = membership_table(members, inverse_two.shape[0])
-    return dot(total, inverse_one[...], ((1,), (1,)), HIGH) + dot(solved, table, ((1,), (0,)), HIGH)
-
-
-def first_coarse(chunks, total, members, inverse_one, inverse_two, two, copies):
-    two[...] = jnp.sum(chunks[...], axis=0)
-    value = coarse_solve(total[...], two[...], members, inverse_one, inverse_two)
+def first_coarse(chunks, part_one, table_two, value, copies):
+    value[...] = part_one[...] + dot(jnp.sum(chunks[...], axis=0), table_two[...], ((1,), (0,)), HIGH)
     for k in range(copies.shape[0]):
-        copies[k] = value
-
-
-def second_coarse(chunks, total_q, total, two, members, inverse_one, inverse_two, copies, info, column):
-    share = total.shape[0]
-    two_q, dots = unpack(jnp.sum(chunks[...], axis=0), share)
+        copies[k] = value[...]
+
+
+def second_coarse(chunks, part_one, value, table_two, copies, info, column):
+    share = value.shape[0]
+    two, dots = unpack(jnp.sum(chunks[...], axis=0), share)
     step = dots[0:1] / dots[1:2]
     info[...] = jnp.concatenate([dots[0:2], step, dots[3:]], axis=0)
     column[...] = to_column(step)
     mine = column[pl.ds(pl.multiple_of(lax.axis_index("sub") * share, 8), share), :][:, 0:1]
-    solved = coarse_solve(
-        total[...] - mine * total_q[...], two[...] - mine * two_q, members, inverse_one, inverse_two
-    )
+    solved = value[...] - mine * (part_one[...] + dot(two, table_two[...], ((1,), (0,)), HIGH))
     for k in range(copies.shape[0]):
         copies[k] = solved
 
@@ -422,13 +417,15 @@
         limit=60,
     )
     first, matrix = lax.optimization_barrier((blocks[0], matrix))
-    (diagonal,) = kernel(read_diagonal, (matrix,), [vector], scalars=0)
+    diagonal, table_two, kept = kernel(
+        prepare, (matrix, members, level2_inv, rhs), [vector, shape(levels, coarse), vector], scalars=0
+    )
     one, two, three, four = exchanged([first, *blocks[1:]])
     placed = kernel(open_sub, (order, one, two), [vector, vector], [pltpu.VMEM((face, cols), F32)])
-    three, four, diagonal = lax.optimization_barrier((three, four, diagonal))
+    three, four, diagonal, table_two, kept = lax.optimization_barrier((three, four, diagonal, table_two, kept))
     residual0, _, weight, weighted, partial = kernel(
         open_join,
-        (order, rhs, stiff, three, four, basis, *placed),
+        (order, kept, stiff, three, four, basis, *placed),
         [vector] * 4 + [shape(cols, coarse)],
         [pltpu.VMEM((face, cols), F32), wide],
         aliases={6: 0, 7: 1},
@@ -443,23 +440,28 @@
             [shape(share, coarse), shape(*part_shape)],
             scalars=0,
         )
-        part, weighted = lax.optimization_barrier((part, weighted))
+        part, total, weighted = lax.optimization_barrier((part, total, weighted))
         others = [turned(part, step, inner) for step in range(1, inner)]
-        (fix,) = kernel(
-            local_fix, (matrix, weighted, diagonal), [vector], [wide], scalars=0, flops=2 * product_flops
+        fix, part_one = kernel(
+            local_fix,
+            (matrix, weighted, diagonal, total, inverse_one),
+            [vector, shape(share, coarse)],
+            [wide],
+            scalars=0,
+            flops=2 * product_flops,
         )
         *others, fix = lax.optimization_barrier((*others, fix))
         (copies,) = kernel(add_and_copy, (part, *others), [shape(outer, *part_shape)], scalars=0)
-        return total, spread(copies, "grp", groups_z), fix
+        return part_one, spread(copies, "grp", groups_z), fix
 
     def from_groups(copies):
         return spread(copies, "sub").reshape(cols, copies.shape[2])
 
-    total0, chunks, fix0 = to_groups(first_groups, partial.reshape(n_sub, share, coarse), weighted)
-    two0, copies = kernel(
+    part_one, chunks, fix0 = to_groups(first_groups, partial.reshape(n_sub, share, coarse), weighted)
+    value0, copies = kernel(
         first_coarse,
-        (chunks, total0, members, inverse_one, level2_inv),
-        [shape(share, levels), shape(n_sub, share, coarse)],
+        (chunks, part_one, table_two),
+        [shape(share, coarse), shape(n_sub, share, coarse)],
         scalars=0,
     )
     coarse0 = from_groups(copies)
@@ -480,10 +482,10 @@
         [wide],
         aliases={5: 0},
     )
-    total_q, chunks, fix_image = to_groups(second_groups, payload, weighted)
+    part_one, chunks, fix_image = to_groups(second_groups, payload, weighted)
     copies, info = kernel(
         second_coarse,
-        (chunks, total_q, total0, two0, members, inverse_one, level2_inv),
+        (chunks, part_one, value0, table_two),
         [shape(n_sub, share, coarse), shape(8, cols)],
         [pltpu.VMEM((LANES, LANES), F32)],
         scalars=0,

time: 205 us -> 203 us (level)
  local copies, waits for them, and re-layouts: 3.42 us -> 6.26 us
  Pallas kernels: 58.1 us -> 55.5 us
  blocking collectives: 80.5 us -> 78.4 us
    unnamed x18 -> x20, local copies, waits for them, and re-layouts: 3.42 us -> 6.26 us
    pallas_call x28, Pallas kernels: 58.1 us -> 55.5 us  [kernel(): pl.pallas_call(body, out_shape=list(outs), in_specs=specs, out_specs=[VM]...]
  transfers between devices with their start and end apart: 30 -> 30, of which waited for: 10 -> 8; matrix products, arithmetic and copies ran while one was open for 0% -> 0% of each run, Pallas kernels for 12% -> 12%
where the time goes in v5:
time: 203 us; the launch traced here: 201 us
  blocking collectives  78.4 us (39%)
  Pallas kernels  55.5 us (27%)
  starting transfers between devices  44.6 us (22%)
  waiting for transfers between devices  14.6 us (7%)
  local copies, waits for them, and re-layouts  6.26 us (3%)
    all_to_all x7, blocking collectives, spread(): return lax.all_to_all(chunks, axis, 0, 0, axis_index_groups=groups)  78.4 us
    pallas_call x28, Pallas kernels, kernel(): pl.pallas_call(body, out_shape=list(outs), in_specs=specs, out_specs=[VM]...  55.5 us
    ppermute x23, starting transfers between devices, passed_along(): return lax.ppermute(value, axis, pairs)  40.8 us
    ppermute x23, waiting for transfers between devices, passed_along(): return lax.ppermute(value, axis, pairs)  13.8 us
    unnamed x20, local copies, waits for them, and re-layouts  6.26 us
  transfers between devices with their start and end apart: 30, of which 8 were waited for; matrix products, arithmetic and copies ran while one was open for 0% of the time, Pallas kernels for 12%

profile of v5, /device:TPU:1, one launch (start us, length us, event | category | flops | bytes accessed | tf_op | source)
XLA Modules:
  0.0 200.6 jit_solution(8051609630705580878)
XLA Ops:
  0.7 5.8 %open_faces.1 = (f32[520,128]{1,0:T(8,128)}, f32[520,128]{1,0:T(8,128)}, f32[520,128]{1,0:T(8,128)}, f32[520,128]{1,0:T(8,128)}) custom-call(s32[1,2048]{1,0:T(1,128)} %bitcast.22, f32[2048,128]{1,0:T(8,128)} %bitcast.20, f32[1,2048]{1,0:T(1,128)} %bitcast.42), custom_call_target="tpu_custom_call" | custom-call | bytes 2129920 | tf_op jit(solution)/shard_map/open_faces/pallas_call | solution.py:29
  6.4 2.2 %collective-permute-start = (f32[520,128]{1,0:T(8,128)}, f32[520,128]{1,0:T(8,128)S(1)}, u32[]{:S(2)}, u32[]{:S(2)}) collective-permute-start(f32[520,128]{1,0:T(8,128)} %get-tuple-element.87), channel_id=1, source_target_pairs={{0,1},{1,2},{2,3},{3,4},{4,5},{5,6},{6,7},{7,8},{8,9},{9,10},{10,1... | collective-permute-start | bytes 798728 | tf_op jit(solution)/shard_map/ppermute | solution.py:358
  8.6 6.8 %collective-permute-start.1 = (f32[520,128]{1,0:T(8,128)}, f32[520,128]{1,0:T(8,128)S(1)}, u32[]{:S(2)}, u32[]{:S(2)}) collective-permute-start(f32[520,128]{1,0:T(8,128)} %get-tuple-element.88), channel_id=1, source_target_pairs={{0,31},{1,0},{2,1},{3,2},{4,3},{5,4},{6,5},{7,6},{8,7},{9,8},{10,9... | collective-permute-start | bytes 798728 | tf_op jit(solution)/shard_map/ppermute | solution.py:358
  17.5 3.4 %copy-done = bf16[1,1,2048,2048]{3,2,1,0:T(8,128)(2,1)S(1)} copy-done((bf16[1,1,2048,2048]{3,2,1,0:T(8,128)(2,1)S(1)}, bf16[1,1,2048,2048]{3,2,1,0:T(8,128)(2,1)}, u32[]{:S(2)}) %copy-start) | copy-done | bytes 8388632
  24.3 2.1 %open_sub.1 = (f32[2048,128]{1,0:T(8,128)S(1)}, f32[2048,128]{1,0:T(8,128)S(1)}) custom-call(s32[1,2048]{1,0:T(1,128)S(1)} %bitcast.23, f32[520,128]{1,0:T(8,128)S(1)} %collective-permute-done.2.one, f32[520,128]{1,0:T(8,128)S(1)} %collective-permute-done.3.two), custom_call_target="tpu_custom_call" | custom-call | bytes 2637824 | tf_op jit(solution)/shard_map/open_sub/pallas_call | solution.py:29
  26.4 3.0 %open_join.1 = (f32[2048,128]{1,0:T(8,128)S(1)}, f32[2048,128]{1,0:T(8,128)S(1)}, f32[2048,128]{1,0:T(8,128)S(1)}, f32[2048,128]{1,0:T(8,128)S(1)}, f32[128,256]{1,0:T(8,128)S(1)}) custom-call(s32[1,2048]{1,0:T(1,128)S(1)} %bitcast.24, f32[2048,128]{1,0:T(8,128)S(1)} %get-tuple-element.92.rhs, ...), custom_call_target="tpu_custom_call", output_to_operand_aliasing={{0}: (6, {}), {1}: (7, {})} | custom-call | bytes 9068544 | tf_op jit(solution)/shard_map/open_join/pallas_call | solution.py:29
  29.4 10.1 %all_to_all.35.chunks = f32[8,16,256]{2,1,0:T(8,128)S(1)} all-to-all(f32[8,16,256]{2,1,0:T(8,128)S(1)} %bitcast.41), channel_id=1, replica_groups=mesh['sub'=8,'grp'=32] {'sub'}, dimensions={0} | all-to-all | bytes 262144 | tf_op jit(solution)/shard_map/all_to_all | solution.py:376
  41.3 5.2 %local_fix.2 = (f32[2048,128]{1,0:T(8,128)S(1)}, f32[16,256]{1,0:T(8,128)S(1)}) custom-call(bf16[2048,2048]{1,0:T(8,128)(2,1)S(1)} %bitcast.12, f32[2048,128]{1,0:T(8,128)S(1)} %get-tuple-element.106.weighted, f32[2048,128]{1,0:T(8,128)S(1)} %get-tuple-element.107.diagonal, f32[16,256]{1,0:T(8,128)S(1)} %get-tuple-element.108.total, f32[256,256]{1,0:T(8,128)S(1)} %bitcast.44), custom_call_target="tpu_custom_call" | custom-call | flops 4294967296 | bytes 11829248 | tf_op jit(solution)/shard_map/local_fix/pallas_call | solution.py:29
  46.6 12.6 %all_to_all.36.chunks = f32[8,16,256]{2,1,0:T(8,128)S(1)} all-to-all(f32[8,16,256]{2,1,0:T(8,128)S(1)} %add_and_copy.2), channel_id=1, replica_groups={{0,4,8,12,16,20,24,28},{1,5,9,13,17,21,25,29},{2,6,10,14,18,22,26,30},{..., dimensions={0} | all-to-all | bytes 262144 | tf_op jit(solution)/shard_map/all_to_all | solution.py:376
  59.4 10.5 %all_to_all.37 = f32[8,16,256]{2,1,0:T(8,128)S(1)} all-to-all(f32[8,16,256]{2,1,0:T(8,128)S(1)} %get-tuple-element.116), channel_id=1, replica_groups=mesh['sub'=8,'grp'=32] {'sub'}, dimensions={0} | all-to-all | bytes 262144 | tf_op jit(solution)/shard_map/all_to_all | solution.py:376
  71.9 2.4 %collective-permute-start.9 = (f32[512,128]{1,0:T(8,128)S(1)}, f32[512,128]{1,0:T(8,128)S(1)}, u32[]{:S(2)}, u32[]{:S(2)}) collective-permute-start(f32[512,128]{1,0:T(8,128)S(1)} %get-tuple-element.120), channel_id=1, source_target_pairs={{0,1},{1,2},{2,3},{3,4},{4,5},{5,6},{6,7},{7,8},{8,9},{9,10},{10,1... | collective-permute-start | bytes 786440 | tf_op jit(solution)/shard_map/ppermute | solution.py:358
  74.3 2.7 %collective-permute-start.10 = (f32[512,128]{1,0:T(8,128)S(1)}, f32[512,128]{1,0:T(8,128)S(1)}, u32[]{:S(2)}, u32[]{:S(2)}) collective-permute-start(f32[512,128]{1,0:T(8,128)S(1)} %get-tuple-element.121), channel_id=1, source_target_pairs={{0,31},{1,0},{2,1},{3,2},{4,3},{5,4},{6,5},{7,6},{8,7},{9,8},{10,9... | collective-permute-start | bytes 786440 | tf_op jit(solution)/shard_map/ppermute | solution.py:358
  80.2 2.3 %collective-permute-done.9.three = f32[512,128]{1,0:T(8,128)S(1)} collective-permute-done((f32[512,128]{1,0:T(8,128)S(1)}, f32[512,128]{1,0:T(8,128)S(1)}, u32[]{:S(2)}, u32[]{:S(2)}) %collective-permute-start.9) | collective-permute-done | bytes 262176 | tf_op jit(solution)/shard_map/ppermute | solution.py:358
  84.0 2.2 %collective-permute-done.8.two = f32[512,128]{1,0:T(8,128)S(1)} collective-permute-done((f32[512,128]{1,0:T(8,128)S(1)}, f32[512,128]{1,0:T(8,128)S(1)}, u32[]{:S(2)}, u32[]{:S(2)}) %collective-permute-start.8) | collective-permute-done | bytes 262176 | tf_op jit(solution)/shard_map/ppermute | solution.py:358
  86.3 5.3 %first_apply.1 = (f32[2048,128]{1,0:T(8,128)S(1)}, f32[2048,128]{1,0:T(8,128)S(1)}, f32[8,128]{1,0:T(8,128)S(1)}, f32[512,128]{1,0:T(8,128)S(1)}, f32[512,128]{1,0:T(8,128)S(1)}) custom-call(s32[1,2048]{1,0:T(1,128)S(1)} %bitcast.28, bf16[2048,2048]{1,0:T(8,128)(2,1)S(1)} %bitcast.13, ...), custom_call_target="tpu_custom_call", output_to_operand_aliasing={{0}: (6, {})} | custom-call | flops 2147483648 | bytes 14692352 | tf_op jit(solution)/shard_map/first_apply/pallas_call | solution.py:29
  91.6 4.8 %collective-permute-start.14 = (f32[512,128]{1,0:T(8,128)S(1)}, f32[512,128]{1,0:T(8,128)S(1)}, u32[]{:S(2)}, u32[]{:S(2)}) collective-permute-start(f32[512,128]{1,0:T(8,128)S(1)} %get-tuple-element.126), channel_id=1, source_target_pairs={{0,31},{1,0},{2,1},{3,2},{4,3},{5,4},{6,5},{7,6},{8,7},{9,8},{10,9... | collective-permute-start | bytes 786440 | tf_op jit(solution)/shard_map/ppermute | solution.py:358
  99.3 2.7 %collective-permute-done.13.three = f32[512,128]{1,0:T(8,128)S(1)} collective-permute-done((f32[512,128]{1,0:T(8,128)S(1)}, f32[512,128]{1,0:T(8,128)S(1)}, u32[]{:S(2)}, u32[]{:S(2)}) %collective-permute-start.13) | collective-permute-done | bytes 262176 | tf_op jit(solution)/shard_map/ppermute | solution.py:358
  104.4 2.2 %image_partial.1 = (f32[2048,128]{1,0:T(8,128)S(1)}, f32[2048,128]{1,0:T(8,128)S(1)}, f32[8,40,128]{2,1,0:T(8,128)S(1)}) custom-call(s32[1,2048]{1,0:T(1,128)S(1)} %bitcast.31, f32[2048,128]{1,0:T(8,128)S(1)} %get-tuple-element.122.source.product, f32[2048,128]{1,0:T(8,128)S(1)} %get-tuple-element.99.weight, ...), custom_call_target="tpu_custom_call", output_to_operand_aliasing={{0}: (5, {})} | custom-call | bytes 6991872 | tf_op jit(solution)/shard_map/image_partial/pallas_call | solution.py:29
  106.6 11.5 %all_to_all.38.chunks = f32[8,40,128]{2,1,0:T(8,128)S(1)} all-to-all(f32[8,40,128]{2,1,0:T(8,128)S(1)} %get-tuple-element.129), channel_id=1, replica_groups=mesh['sub'=8,'grp'=32] {'sub'}, dimensions={0} | all-to-all | bytes 327680 | tf_op jit(solution)/shard_map/all_to_all | solution.py:376
  119.9 5.1 %local_fix.3 = (f32[2048,128]{1,0:T(8,128)S(1)}, f32[16,256]{1,0:T(8,128)S(1)}) custom-call(bf16[2048,2048]{1,0:T(8,128)(2,1)S(1)} %bitcast.14, f32[2048,128]{1,0:T(8,128)S(1)} %get-tuple-element.134.weighted, f32[2048,128]{1,0:T(8,128)S(1)} %get-tuple-element.107.diagonal, f32[16,256]{1,0:T(8,128)S(1)} %get-tuple-element.135.total, f32[256,256]{1,0:T(8,128)S(1)} %bitcast.45), custom_call_target="tpu_custom_call" | custom-call | flops 4294967296 | bytes 11829248 | tf_op jit(solution)/shard_map/local_fix/pallas_call | solution.py:29
  125.1 10.9 %all_to_all.39.chunks = f32[8,40,128]{2,1,0:T(8,128)S(1)} all-to-all(f32[8,40,128]{2,1,0:T(8,128)S(1)} %add_and_copy.3), channel_id=1, replica_groups={{0,4,8,12,16,20,24,28},{1,5,9,13,17,21,25,29},{2,6,10,14,18,22,26,30},{..., dimensions={0} | all-to-all | bytes 327680 | tf_op jit(solution)/shard_map/all_to_all | solution.py:376
  136.3 10.5 %all_to_all.40 = f32[8,16,256]{2,1,0:T(8,128)S(1)} all-to-all(f32[8,16,256]{2,1,0:T(8,128)S(1)} %get-tuple-element.143), channel_id=1, replica_groups=mesh['sub'=8,'grp'=32] {'sub'}, dimensions={0} | all-to-all | bytes 262144 | tf_op jit(solution)/shard_map/all_to_all | solution.py:376
  146.8 2.2 %second_local.1 = (f32[2048,128]{1,0:T(8,128)S(1)}, f32[2048,128]{1,0:T(8,128)S(1)}, f32[512,128]{1,0:T(8,128)S(1)}, f32[512,128]{1,0:T(8,128)S(1)}) custom-call(s32[1,2048]{1,0:T(1,128)S(1)} %bitcast.32, f32[2048,128]{1,0:T(8,128)S(1)} %get-tuple-element.99.weight, bf16[2048,256]{1,0:T(8,128)(2,1)S(1)} %bitcast.19, ...), custom_call_target="tpu_custom_call" | custom-call | bytes 9056256 | tf_op jit(solution)/shard_map/second_local/pallas_call | solution.py:29
  149.0 2.4 %collective-permute-start.20 = (f32[512,128]{1,0:T(8,128)S(1)}, f32[512,128]{1,0:T(8,128)S(1)}, u32[]{:S(2)}, u32[]{:S(2)}) collective-permute-start(f32[512,128]{1,0:T(8,128)S(1)} %get-tuple-element.150), channel_id=1, source_target_pairs={{0,1},{1,2},{2,3},{3,4},{4,5},{5,6},{6,7},{7,8},{8,9},{9,10},{10,1... | collective-permute-start | bytes 786440 | tf_op jit(solution)/shard_map/ppermute | solution.py:358
  151.4 2.5 %collective-permute-start.21 = (f32[512,128]{1,0:T(8,128)S(1)}, f32[512,128]{1,0:T(8,128)S(1)}, u32[]{:S(2)}, u32[]{:S(2)}) collective-permute-start(f32[512,128]{1,0:T(8,128)S(1)} %get-tuple-element.151), channel_id=1, source_target_pairs={{0,31},{1,0},{2,1},{3,2},{4,3},{5,4},{6,5},{7,6},{8,7},{9,8},{10,9... | collective-permute-start | bytes 786440 | tf_op jit(solution)/shard_map/ppermute | solution.py:358
  157.1 2.3 %collective-permute-done.20.three = f32[512,128]{1,0:T(8,128)S(1)} collective-permute-done((f32[512,128]{1,0:T(8,128)S(1)}, f32[512,128]{1,0:T(8,128)S(1)}, u32[]{:S(2)}, u32[]{:S(2)}) %collective-permute-start.20) | collective-permute-done | bytes 262176 | tf_op jit(solution)/shard_map/ppermute | solution.py:358
  160.9 2.2 %collective-permute-done.19.two = f32[512,128]{1,0:T(8,128)S(1)} collective-permute-done((f32[512,128]{1,0:T(8,128)S(1)}, f32[512,128]{1,0:T(8,128)S(1)}, u32[]{:S(2)}, u32[]{:S(2)}) %collective-permute-start.19) | collective-permute-done | bytes 262176 | tf_op jit(solution)/shard_map/ppermute | solution.py:358
  163.2 5.3 %second_apply.1 = (f32[2048,128]{1,0:T(8,128)S(1)}, f32[2048,128]{1,0:T(8,128)S(1)}, f32[8,128]{1,0:T(8,128)S(1)}, f32[512,128]{1,0:T(8,128)S(1)}, f32[512,128]{1,0:T(8,128)S(1)}) custom-call(s32[1,2048]{1,0:T(1,128)S(1)} %bitcast.35, bf16[2048,2048]{1,0:T(8,128)(2,1)S(1)} %bitcast.15, ...), custom_call_target="tpu_custom_call", output_to_operand_aliasing={{0}: (7, {})} | custom-call | flops 2147483648 | bytes 15740928 | tf_op jit(solution)/shard_map/second_apply/pallas_call | solution.py:29
  170.1 4.0 %collective-permute-start.29 = (f32[512,128]{1,0:T(8,128)S(1)}, f32[512,128]{1,0:T(8,128)S(1)}, u32[]{:S(2)}, u32[]{:S(2)}) collective-permute-start(f32[512,128]{1,0:T(8,128)S(1)} %get-tuple-element.159), channel_id=1, source_target_pairs={{0,31},{1,0},{2,1},{3,2},{4,3},{5,4},{6,5},{7,6},{8,7},{9,8},{10,9... | collective-permute-start | bytes 786440 | tf_op jit(solution)/shard_map/ppermute | solution.py:358
  176.3 3.0 %collective-permute-start.25 = (f32[8,128]{1,0:T(8,128)S(1)}, f32[8,128]{1,0:T(8,128)S(1)}, u32[]{:S(2)}, u32[]{:S(2)}) collective-permute-start(f32[8,128]{1,0:T(8,128)S(1)} %add.3.refs_0_), channel_id=1, source_target_pairs={{0,192},{32,224},{64,0},{96,32},{128,64},{160,96},{192,128},{224,1... | collective-permute-start | bytes 12296 | tf_op jit(solution)/shard_map/ppermute | solution.py:358
  180.9 2.4 %collective-permute-start.23 = (f32[8,128]{1,0:T(8,128)S(1)}, f32[8,128]{1,0:T(8,128)S(1)}, u32[]{:S(2)}, u32[]{:S(2)}) collective-permute-start(f32[8,128]{1,0:T(8,128)S(1)} %add.3.refs_0_), channel_id=1, source_target_pairs={{0,64},{32,96},{64,128},{96,160},{128,192},{160,224},{192,0},{224,... | collective-permute-start | bytes 12296 | tf_op jit(solution)/shard_map/ppermute | solution.py:358
  186.6 12.3 %all_to_all.41.chunks = f32[32,1,384]{2,1,0:T(1,128)S(1)} all-to-all(f32[32,1,384]{2,1,0:T(1,128)S(1)} %copy_row.1), channel_id=1, replica_groups=mesh['sub'=8,'grp'=32] {'grp'}, dimensions={0} | all-to-all | bytes 98304 | tf_op jit(solution)/shard_map/all_to_all | solution.py:376
  (84 shorter events, 36.7 us)
Async XLA Ops:
  0.6 25.8 %copy-start.6 = (f32[1,1,2048]{2,1,0:T(1,128)S(1)}, f32[1,1,2048]{2,1,0:T(1,128)}, u32[]{:S(2)}) copy-start(f32[1,1,2048]{2,1,0:T(1,128)} %param.10) | copy-start | bytes 24580
  6.4 17.8 %collective-permute-start = (f32[520,128]{1,0:T(8,128)}, f32[520,128]{1,0:T(8,128)S(1)}, u32[]{:S(2)}, u32[]{:S(2)}) collective-permute-start(f32[520,128]{1,0:T(8,128)} %get-tuple-element.87), channel_id=1, source_target_pairs={{0,1},{1,2},{2,3},{3,4},{4,5},{5,6},{6,7},{7,8},{8,9},{9,10},{10,1... | collective-permute-start | bytes 798728 | tf_op jit(solution)/shard_map/ppermute | solution.py:358
  8.6 15.7 %collective-permute-start.1 = (f32[520,128]{1,0:T(8,128)}, f32[520,128]{1,0:T(8,128)S(1)}, u32[]{:S(2)}, u32[]{:S(2)}) collective-permute-start(f32[520,128]{1,0:T(8,128)} %get-tuple-element.88), channel_id=1, source_target_pairs={{0,31},{1,0},{2,1},{3,2},{4,3},{5,4},{6,5},{7,6},{8,7},{9,8},{10,9... | collective-permute-start | bytes 798728 | tf_op jit(solution)/shard_map/ppermute | solution.py:358
  15.5 8.8 %collective-permute-start.3 = (f32[520,128]{1,0:T(8,128)}, f32[520,128]{1,0:T(8,128)S(1)}, u32[]{:S(2)}, u32[]{:S(2)}) collective-permute-start(f32[520,128]{1,0:T(8,128)} %get-tuple-element.96), channel_id=1, source_target_pairs={{0,224},{32,0},{64,32},{96,64},{128,96},{160,128},{192,160},{224,1... | collective-permute-start | bytes 798728 | tf_op jit(solution)/shard_map/ppermute | solution.py:358
  16.4 7.9 %collective-permute-start.2 = (f32[520,128]{1,0:T(8,128)}, f32[520,128]{1,0:T(8,128)S(1)}, u32[]{:S(2)}, u32[]{:S(2)}) collective-permute-start(f32[520,128]{1,0:T(8,128)} %get-tuple-element.95), channel_id=1, source_target_pairs={{0,32},{32,64},{64,96},{96,128},{128,160},{160,192},{192,224},{224... | collective-permute-start | bytes 798728 | tf_op jit(solution)/shard_map/ppermute | solution.py:358
  39.8 6.7 %collective-permute-start.6 = (f32[16,256]{1,0:T(8,128)S(1)}, f32[16,256]{1,0:T(8,128)S(1)}, u32[]{:S(2)}, u32[]{:S(2)}) collective-permute-start(f32[16,256]{1,0:T(8,128)S(1)} %get-tuple-element.105.refs_0_), channel_id=1, source_target_pairs={{0,3},{1,0},{2,1},{3,2},{4,7},{5,4},{6,5},{7,6},{8,11},{9,8},{10,9... | collective-permute-start | bytes 49160 | tf_op jit(solution)/shard_map/ppermute | solution.py:363
  39.8 6.7 %collective-permute-start.5 = (f32[16,256]{1,0:T(8,128)S(1)}, f32[16,256]{1,0:T(8,128)S(1)}, u32[]{:S(2)}, u32[]{:S(2)}) collective-permute-start(f32[16,256]{1,0:T(8,128)S(1)} %get-tuple-element.105.refs_0_), channel_id=1, source_target_pairs={{0,2},{1,3},{2,0},{3,1},{4,6},{5,7},{6,4},{7,5},{8,10},{9,11},{10,... | collective-permute-start | bytes 49160 | tf_op jit(solution)/shard_map/ppermute | solution.py:363
  40.0 6.6 %collective-permute-start.4 = (f32[16,256]{1,0:T(8,128)S(1)}, f32[16,256]{1,0:T(8,128)S(1)}, u32[]{:S(2)}, u32[]{:S(2)}) collective-permute-start(f32[16,256]{1,0:T(8,128)S(1)} %get-tuple-element.105.refs_0_), channel_id=1, source_target_pairs={{0,1},{1,2},{2,3},{3,0},{4,5},{5,6},{6,7},{7,4},{8,9},{9,10},{10,1... | collective-permute-start | bytes 49160 | tf_op jit(solution)/shard_map/ppermute | solution.py:363
  71.9 10.5 %collective-permute-start.9 = (f32[512,128]{1,0:T(8,128)S(1)}, f32[512,128]{1,0:T(8,128)S(1)}, u32[]{:S(2)}, u32[]{:S(2)}) collective-permute-start(f32[512,128]{1,0:T(8,128)S(1)} %get-tuple-element.120), channel_id=1, source_target_pairs={{0,1},{1,2},{2,3},{3,4},{4,5},{5,6},{6,7},{7,8},{8,9},{9,10},{10,1... | collective-permute-start | bytes 786440 | tf_op jit(solution)/shard_map/ppermute | solution.py:358
  74.3 8.2 %collective-permute-start.10 = (f32[512,128]{1,0:T(8,128)S(1)}, f32[512,128]{1,0:T(8,128)S(1)}, u32[]{:S(2)}, u32[]{:S(2)}) collective-permute-start(f32[512,128]{1,0:T(8,128)S(1)} %get-tuple-element.121), channel_id=1, source_target_pairs={{0,31},{1,0},{2,1},{3,2},{4,3},{5,4},{6,5},{7,6},{8,7},{9,8},{10,9... | collective-permute-start | bytes 786440 | tf_op jit(solution)/shard_map/ppermute | solution.py:358
  78.6 5.5 %collective-permute-start.7 = (f32[512,128]{1,0:T(8,128)S(1)}, f32[512,128]{1,0:T(8,128)S(1)}, u32[]{:S(2)}, u32[]{:S(2)}) collective-permute-start(f32[512,128]{1,0:T(8,128)S(1)} %get-tuple-element.118), channel_id=1, source_target_pairs={{0,32},{32,64},{64,96},{96,128},{128,160},{160,192},{192,224},{224... | collective-permute-start | bytes 786440 | tf_op jit(solution)/shard_map/ppermute | solution.py:358
  80.2 6.1 %collective-permute-start.8 = (f32[512,128]{1,0:T(8,128)S(1)}, f32[512,128]{1,0:T(8,128)S(1)}, u32[]{:S(2)}, u32[]{:S(2)}) collective-permute-start(f32[512,128]{1,0:T(8,128)S(1)} %get-tuple-element.119), channel_id=1, source_target_pairs={{0,224},{32,0},{64,32},{96,64},{128,96},{160,128},{192,160},{224,1... | collective-permute-start | bytes 786440 | tf_op jit(solution)/shard_map/ppermute | solution.py:358
  86.3 31.9 %copy-start.8 = (s32[1,256]{1,0:T(1,128)S(1)}, s32[1,256]{1,0:T(1,128)}, u32[]{:S(2)}) copy-start(s32[1,256]{1,0:T(1,128)} %members.5) | copy-start | bytes 3076
  91.6 10.5 %collective-permute-start.13 = (f32[512,128]{1,0:T(8,128)S(1)}, f32[512,128]{1,0:T(8,128)S(1)}, u32[]{:S(2)}, u32[]{:S(2)}) collective-permute-start(f32[512,128]{1,0:T(8,128)S(1)} %get-tuple-element.125), channel_id=1, source_target_pairs={{0,1},{1,2},{2,3},{3,4},{4,5},{5,6},{6,7},{7,8},{8,9},{9,10},{10,1... | collective-permute-start | bytes 786440 | tf_op jit(solution)/shard_map/ppermute | solution.py:358
  91.6 10.4 %collective-permute-start.14 = (f32[512,128]{1,0:T(8,128)S(1)}, f32[512,128]{1,0:T(8,128)S(1)}, u32[]{:S(2)}, u32[]{:S(2)}) collective-permute-start(f32[512,128]{1,0:T(8,128)S(1)} %get-tuple-element.126), channel_id=1, source_target_pairs={{0,31},{1,0},{2,1},{3,2},{4,3},{5,4},{6,5},{7,6},{8,7},{9,8},{10,9... | collective-permute-start | bytes 786440 | tf_op jit(solution)/shard_map/ppermute | solution.py:358
  98.0 5.6 %collective-permute-start.11 = (f32[512,128]{1,0:T(8,128)S(1)}, f32[512,128]{1,0:T(8,128)S(1)}, u32[]{:S(2)}, u32[]{:S(2)}) collective-permute-start(f32[512,128]{1,0:T(8,128)S(1)} %get-tuple-element.123), channel_id=1, source_target_pairs={{0,32},{32,64},{64,96},{96,128},{128,160},{160,192},{192,224},{224... | collective-permute-start | bytes 786440 | tf_op jit(solution)/shard_map/ppermute | solution.py:358
  98.3 6.1 %collective-permute-start.12 = (f32[512,128]{1,0:T(8,128)S(1)}, f32[512,128]{1,0:T(8,128)S(1)}, u32[]{:S(2)}, u32[]{:S(2)}) collective-permute-start(f32[512,128]{1,0:T(8,128)S(1)} %get-tuple-element.124), channel_id=1, source_target_pairs={{0,224},{32,0},{64,32},{96,64},{128,96},{160,128},{192,160},{224,1... | collective-permute-start | bytes 786440 | tf_op jit(solution)/shard_map/ppermute | solution.py:358
  118.4 6.6 %collective-permute-start.17 = (f32[40,128]{1,0:T(8,128)S(1)}, f32[40,128]{1,0:T(8,128)S(1)}, u32[]{:S(2)}, u32[]{:S(2)}) collective-permute-start(f32[40,128]{1,0:T(8,128)S(1)} %get-tuple-element.133.refs_0_), channel_id=1, source_target_pairs={{0,3},{1,0},{2,1},{3,2},{4,7},{5,4},{6,5},{7,6},{8,11},{9,8},{10,9... | collective-permute-start | bytes 61448 | tf_op jit(solution)/shard_map/ppermute | solution.py:363
  118.4 6.6 %collective-permute-start.16 = (f32[40,128]{1,0:T(8,128)S(1)}, f32[40,128]{1,0:T(8,128)S(1)}, u32[]{:S(2)}, u32[]{:S(2)}) collective-permute-start(f32[40,128]{1,0:T(8,128)S(1)} %get-tuple-element.133.refs_0_), channel_id=1, source_target_pairs={{0,2},{1,3},{2,0},{3,1},{4,6},{5,7},{6,4},{7,5},{8,10},{9,11},{10,... | collective-permute-start | bytes 61448 | tf_op jit(solution)/shard_map/ppermute | solution.py:363
  118.5 6.5 %collective-permute-start.15 = (f32[40,128]{1,0:T(8,128)S(1)}, f32[40,128]{1,0:T(8,128)S(1)}, u32[]{:S(2)}, u32[]{:S(2)}) collective-permute-start(f32[40,128]{1,0:T(8,128)S(1)} %get-tuple-element.133.refs_0_), channel_id=1, source_target_pairs={{0,1},{1,2},{2,3},{3,0},{4,5},{5,6},{6,7},{7,4},{8,9},{9,10},{10,1... | collective-permute-start | bytes 61448 | tf_op jit(solution)/shard_map/ppermute | solution.py:363
  149.0 10.3 %collective-permute-start.20 = (f32[512,128]{1,0:T(8,128)S(1)}, f32[512,128]{1,0:T(8,128)S(1)}, u32[]{:S(2)}, u32[]{:S(2)}) collective-permute-start(f32[512,128]{1,0:T(8,128)S(1)} %get-tuple-element.150), channel_id=1, source_target_pairs={{0,1},{1,2},{2,3},{3,4},{4,5},{5,6},{6,7},{7,8},{8,9},{9,10},{10,1... | collective-permute-start | bytes 786440 | tf_op jit(solution)/shard_map/ppermute | solution.py:358
  151.4 8.0 %collective-permute-start.21 = (f32[512,128]{1,0:T(8,128)S(1)}, f32[512,128]{1,0:T(8,128)S(1)}, u32[]{:S(2)}, u32[]{:S(2)}) collective-permute-start(f32[512,128]{1,0:T(8,128)S(1)} %get-tuple-element.151), channel_id=1, source_target_pairs={{0,31},{1,0},{2,1},{3,2},{4,3},{5,4},{6,5},{7,6},{8,7},{9,8},{10,9... | collective-permute-start | bytes 786440 | tf_op jit(solution)/shard_map/ppermute | solution.py:358
  155.4 5.5 %collective-permute-start.18 = (f32[512,128]{1,0:T(8,128)S(1)}, f32[512,128]{1,0:T(8,128)S(1)}, u32[]{:S(2)}, u32[]{:S(2)}) collective-permute-start(f32[512,128]{1,0:T(8,128)S(1)} %get-tuple-element.148), channel_id=1, source_target_pairs={{0,32},{32,64},{64,96},{96,128},{128,160},{160,192},{192,224},{224... | collective-permute-start | bytes 786440 | tf_op jit(solution)/shard_map/ppermute | solution.py:358
  157.1 6.1 %collective-permute-start.19 = (f32[512,128]{1,0:T(8,128)S(1)}, f32[512,128]{1,0:T(8,128)S(1)}, u32[]{:S(2)}, u32[]{:S(2)}) collective-permute-start(f32[512,128]{1,0:T(8,128)S(1)} %get-tuple-element.149), channel_id=1, source_target_pairs={{0,224},{32,0},{64,32},{96,64},{128,96},{160,128},{192,160},{224,1... | collective-permute-start | bytes 786440 | tf_op jit(solution)/shard_map/ppermute | solution.py:358
  168.5 1.7 collective-permute-start.22
  169.3 11.2 %collective-permute-start.28 = (f32[512,128]{1,0:T(8,128)S(1)}, f32[512,128]{1,0:T(8,128)S(1)}, u32[]{:S(2)}, u32[]{:S(2)}) collective-permute-start(f32[512,128]{1,0:T(8,128)S(1)} %get-tuple-element.158), channel_id=1, source_target_pairs={{0,1},{1,2},{2,3},{3,4},{4,5},{5,6},{6,7},{7,8},{8,9},{9,10},{10,1... | collective-permute-start | bytes 786440 | tf_op jit(solution)/shard_map/ppermute | solution.py:358
  170.1 10.8 %collective-permute-start.29 = (f32[512,128]{1,0:T(8,128)S(1)}, f32[512,128]{1,0:T(8,128)S(1)}, u32[]{:S(2)}, u32[]{:S(2)}) collective-permute-start(f32[512,128]{1,0:T(8,128)S(1)} %get-tuple-element.159), channel_id=1, source_target_pairs={{0,31},{1,0},{2,1},{3,2},{4,3},{5,4},{6,5},{7,6},{8,7},{9,8},{10,9... | collective-permute-start | bytes 786440 | tf_op jit(solution)/shard_map/ppermute | solution.py:358
  175.7 9.2 %collective-permute-start.26 = (f32[512,128]{1,0:T(8,128)S(1)}, f32[512,128]{1,0:T(8,128)S(1)}, u32[]{:S(2)}, u32[]{:S(2)}) collective-permute-start(f32[512,128]{1,0:T(8,128)S(1)} %get-tuple-element.156), channel_id=1, source_target_pairs={{0,32},{32,64},{64,96},{96,128},{128,160},{160,192},{192,224},{224... | collective-permute-start | bytes 786440 | tf_op jit(solution)/shard_map/ppermute | solution.py:358
  176.1 8.8 %collective-permute-start.27 = (f32[512,128]{1,0:T(8,128)S(1)}, f32[512,128]{1,0:T(8,128)S(1)}, u32[]{:S(2)}, u32[]{:S(2)}) collective-permute-start(f32[512,128]{1,0:T(8,128)S(1)} %get-tuple-element.157), channel_id=1, source_target_pairs={{0,224},{32,0},{64,32},{96,64},{128,96},{160,128},{192,160},{224,1... | collective-permute-start | bytes 786440 | tf_op jit(solution)/shard_map/ppermute | solution.py:358
  176.3 10.2 %collective-permute-start.25 = (f32[8,128]{1,0:T(8,128)S(1)}, f32[8,128]{1,0:T(8,128)S(1)}, u32[]{:S(2)}, u32[]{:S(2)}) collective-permute-start(f32[8,128]{1,0:T(8,128)S(1)} %add.3.refs_0_), channel_id=1, source_target_pairs={{0,192},{32,224},{64,0},{96,32},{128,64},{160,96},{192,128},{224,1... | collective-permute-start | bytes 12296 | tf_op jit(solution)/shard_map/ppermute | solution.py:358
  180.5 6.1 %collective-permute-start.24 = (f32[8,128]{1,0:T(8,128)S(1)}, f32[8,128]{1,0:T(8,128)S(1)}, u32[]{:S(2)}, u32[]{:S(2)}) collective-permute-start(f32[8,128]{1,0:T(8,128)S(1)} %add.3.refs_0_), channel_id=1, source_target_pairs={{0,128},{32,160},{64,192},{96,224},{128,0},{160,32},{192,64},{224,... | collective-permute-start | bytes 12296 | tf_op jit(solution)/shard_map/ppermute | solution.py:358
  180.9 5.6 %collective-permute-start.23 = (f32[8,128]{1,0:T(8,128)S(1)}, f32[8,128]{1,0:T(8,128)S(1)}, u32[]{:S(2)}, u32[]{:S(2)}) collective-permute-start(f32[8,128]{1,0:T(8,128)S(1)} %add.3.refs_0_), channel_id=1, source_target_pairs={{0,64},{32,96},{64,128},{96,160},{128,192},{160,224},{192,0},{224,... | collective-permute-start | bytes 12296 | tf_op jit(solution)/shard_map/ppermute | solution.py:358
  (8 other events, 90.9 us)

commit v6 on v5

--- a/solution.py
+++ b/solution.py
@@ -506,7 +506,6 @@
         aliases={7: 0},
     )
     dots = dots + lax.ppermute(dots, "sub", [(k, k ^ 1) for k in range(n_sub)])
-    blocks[0], dots = lax.optimization_barrier((blocks[0], dots))
     dots = [dots] + [passed_along(dots, "sub", step) for step in range(2, n_sub, 2)]
     arrived = swap(product1, blocks)
     (image1,) = kernel(last_image, (order, product1, *arrived), [vector], aliases={4: 0})

time: 203 us -> 202 us (level)
    ppermute x23, starting transfers between devices: 40.8 us -> 38.1 us  [passed_along(): return lax.ppermute(value, axis, pairs)]
    ppermute x1, starting transfers between devices: 0.83 us -> 2.93 us  [body(): dots = dots + lax.ppermute(dots, 'sub', [(k, k ^ 1) for k in range(n_sub)])]
where the time goes in v6:
time: 202 us; the launch traced here: 199 us
  blocking collectives  78.3 us (39%)
  Pallas kernels  55.6 us (28%)
  starting transfers between devices  44 us (22%)
  waiting for transfers between devices  13.8 us (7%)
  local copies, waits for them, and re-layouts  6.26 us (3%)
    all_to_all x7, blocking collectives, spread(): return lax.all_to_all(chunks, axis, 0, 0, axis_index_groups=groups)  78.3 us
    pallas_call x28, Pallas kernels, kernel(): pl.pallas_call(body, out_shape=list(outs), in_specs=specs, out_specs=[VM]...  55.6 us
    ppermute x23, starting transfers between devices, passed_along(): return lax.ppermute(value, axis, pairs)  38.1 us
    ppermute x23, waiting for transfers between devices, passed_along(): return lax.ppermute(value, axis, pairs)  13 us
    unnamed x20, local copies, waits for them, and re-layouts  6.26 us
  transfers between devices with their start and end apart: 30, of which 8 were waited for; matrix products, arithmetic and copies ran while one was open for 0% of the time, Pallas kernels for 12%

profile of v6, /device:TPU:1, one launch (start us, length us, event | category | flops | bytes accessed | tf_op | source)
XLA Modules:
  0.0 199.0 jit_solution(16206337690515699302)
XLA Ops:
  0.7 5.8 %open_faces.1 = (f32[520,128]{1,0:T(8,128)}, f32[520,128]{1,0:T(8,128)}, f32[520,128]{1,0:T(8,128)}, f32[520,128]{1,0:T(8,128)}) custom-call(s32[1,2048]{1,0:T(1,128)} %bitcast.22, f32[2048,128]{1,0:T(8,128)} %bitcast.20, f32[1,2048]{1,0:T(1,128)} %bitcast.42), custom_call_target="tpu_custom_call" | custom-call | bytes 2129920 | tf_op jit(solution)/shard_map/open_faces/pallas_call | solution.py:29
  6.4 2.2 %collective-permute-start = (f32[520,128]{1,0:T(8,128)}, f32[520,128]{1,0:T(8,128)S(1)}, u32[]{:S(2)}, u32[]{:S(2)}) collective-permute-start(f32[520,128]{1,0:T(8,128)} %get-tuple-element.85), channel_id=1, source_target_pairs={{0,1},{1,2},{2,3},{3,4},{4,5},{5,6},{6,7},{7,8},{8,9},{9,10},{10,1... | collective-permute-start | bytes 798728 | tf_op jit(solution)/shard_map/ppermute | solution.py:358
  8.6 6.8 %collective-permute-start.1 = (f32[520,128]{1,0:T(8,128)}, f32[520,128]{1,0:T(8,128)S(1)}, u32[]{:S(2)}, u32[]{:S(2)}) collective-permute-start(f32[520,128]{1,0:T(8,128)} %get-tuple-element.86), channel_id=1, source_target_pairs={{0,31},{1,0},{2,1},{3,2},{4,3},{5,4},{6,5},{7,6},{8,7},{9,8},{10,9... | collective-permute-start | bytes 798728 | tf_op jit(solution)/shard_map/ppermute | solution.py:358
  17.5 3.4 %copy-done = bf16[1,1,2048,2048]{3,2,1,0:T(8,128)(2,1)S(1)} copy-done((bf16[1,1,2048,2048]{3,2,1,0:T(8,128)(2,1)S(1)}, bf16[1,1,2048,2048]{3,2,1,0:T(8,128)(2,1)}, u32[]{:S(2)}) %copy-start) | copy-done | bytes 8388632
  24.3 2.1 %open_sub.1 = (f32[2048,128]{1,0:T(8,128)S(1)}, f32[2048,128]{1,0:T(8,128)S(1)}) custom-call(s32[1,2048]{1,0:T(1,128)S(1)} %bitcast.23, f32[520,128]{1,0:T(8,128)S(1)} %collective-permute-done.2.one, f32[520,128]{1,0:T(8,128)S(1)} %collective-permute-done.3.two), custom_call_target="tpu_custom_call" | custom-call | bytes 2637824 | tf_op jit(solution)/shard_map/open_sub/pallas_call | solution.py:29
  26.4 3.0 %open_join.1 = (f32[2048,128]{1,0:T(8,128)S(1)}, f32[2048,128]{1,0:T(8,128)S(1)}, f32[2048,128]{1,0:T(8,128)S(1)}, f32[2048,128]{1,0:T(8,128)S(1)}, f32[128,256]{1,0:T(8,128)S(1)}) custom-call(s32[1,2048]{1,0:T(1,128)S(1)} %bitcast.24, f32[2048,128]{1,0:T(8,128)S(1)} %get-tuple-element.90.rhs, ...), custom_call_target="tpu_custom_call", output_to_operand_aliasing={{0}: (6, {}), {1}: (7, {})} | custom-call | bytes 9068544 | tf_op jit(solution)/shard_map/open_join/pallas_call | solution.py:29
  29.4 10.1 %all_to_all.35.chunks = f32[8,16,256]{2,1,0:T(8,128)S(1)} all-to-all(f32[8,16,256]{2,1,0:T(8,128)S(1)} %bitcast.41), channel_id=1, replica_groups=mesh['sub'=8,'grp'=32] {'sub'}, dimensions={0} | all-to-all | bytes 262144 | tf_op jit(solution)/shard_map/all_to_all | solution.py:376
  41.3 5.2 %local_fix.2 = (f32[2048,128]{1,0:T(8,128)S(1)}, f32[16,256]{1,0:T(8,128)S(1)}) custom-call(bf16[2048,2048]{1,0:T(8,128)(2,1)S(1)} %bitcast.12, f32[2048,128]{1,0:T(8,128)S(1)} %get-tuple-element.104.weighted, f32[2048,128]{1,0:T(8,128)S(1)} %get-tuple-element.105.diagonal, f32[16,256]{1,0:T(8,128)S(1)} %get-tuple-element.106.total, f32[256,256]{1,0:T(8,128)S(1)} %bitcast.44), custom_call_target="tpu_custom_call" | custom-call | flops 4294967296 | bytes 11829248 | tf_op jit(solution)/shard_map/local_fix/pallas_call | solution.py:29
  46.6 12.6 %all_to_all.36.chunks = f32[8,16,256]{2,1,0:T(8,128)S(1)} all-to-all(f32[8,16,256]{2,1,0:T(8,128)S(1)} %add_and_copy.2), channel_id=1, replica_groups={{0,4,8,12,16,20,24,28},{1,5,9,13,17,21,25,29},{2,6,10,14,18,22,26,30},{..., dimensions={0} | all-to-all | bytes 262144 | tf_op jit(solution)/shard_map/all_to_all | solution.py:376
  59.4 10.5 %all_to_all.37 = f32[8,16,256]{2,1,0:T(8,128)S(1)} all-to-all(f32[8,16,256]{2,1,0:T(8,128)S(1)} %get-tuple-element.114), channel_id=1, replica_groups=mesh['sub'=8,'grp'=32] {'sub'}, dimensions={0} | all-to-all | bytes 262144 | tf_op jit(solution)/shard_map/all_to_all | solution.py:376
  69.9 2.0 %first_local.1 = (f32[2048,128]{1,0:T(8,128)S(1)}, f32[512,128]{1,0:T(8,128)S(1)}, f32[512,128]{1,0:T(8,128)S(1)}) custom-call(s32[1,2048]{1,0:T(1,128)S(1)} %bitcast.25, f32[2048,128]{1,0:T(8,128)S(1)} %get-tuple-element.97.weight, f32[2048,128]{1,0:T(8,128)S(1)} %get-tuple-element.108.fix.fix_first, bf16[2048,256]{1,0:T(8,128)(2,1)S(1)} %bitcast.17, ...), custom_call_target="tpu_custom_call" | custom-call | bytes 4857856 | tf_op jit(solution)/shard_map/first_local/pallas_call | solution.py:29
  71.9 2.4 %collective-permute-start.9 = (f32[512,128]{1,0:T(8,128)S(1)}, f32[512,128]{1,0:T(8,128)S(1)}, u32[]{:S(2)}, u32[]{:S(2)}) collective-permute-start(f32[512,128]{1,0:T(8,128)S(1)} %get-tuple-element.118), channel_id=1, source_target_pairs={{0,1},{1,2},{2,3},{3,4},{4,5},{5,6},{6,7},{7,8},{8,9},{9,10},{10,1... | collective-permute-start | bytes 786440 | tf_op jit(solution)/shard_map/ppermute | solution.py:358
  74.3 2.7 %collective-permute-start.10 = (f32[512,128]{1,0:T(8,128)S(1)}, f32[512,128]{1,0:T(8,128)S(1)}, u32[]{:S(2)}, u32[]{:S(2)}) collective-permute-start(f32[512,128]{1,0:T(8,128)S(1)} %get-tuple-element.119), channel_id=1, source_target_pairs={{0,31},{1,0},{2,1},{3,2},{4,3},{5,4},{6,5},{7,6},{8,7},{9,8},{10,9... | collective-permute-start | bytes 786440 | tf_op jit(solution)/shard_map/ppermute | solution.py:358
  80.2 2.3 %collective-permute-done.9.three = f32[512,128]{1,0:T(8,128)S(1)} collective-permute-done((f32[512,128]{1,0:T(8,128)S(1)}, f32[512,128]{1,0:T(8,128)S(1)}, u32[]{:S(2)}, u32[]{:S(2)}) %collective-permute-start.9) | collective-permute-done | bytes 262176 | tf_op jit(solution)/shard_map/ppermute | solution.py:358
  84.0 2.2 %collective-permute-done.8.two = f32[512,128]{1,0:T(8,128)S(1)} collective-permute-done((f32[512,128]{1,0:T(8,128)S(1)}, f32[512,128]{1,0:T(8,128)S(1)}, u32[]{:S(2)}, u32[]{:S(2)}) %collective-permute-start.8) | collective-permute-done | bytes 262176 | tf_op jit(solution)/shard_map/ppermute | solution.py:358
  86.3 5.3 %first_apply.1 = (f32[2048,128]{1,0:T(8,128)S(1)}, f32[2048,128]{1,0:T(8,128)S(1)}, f32[8,128]{1,0:T(8,128)S(1)}, f32[512,128]{1,0:T(8,128)S(1)}, f32[512,128]{1,0:T(8,128)S(1)}) custom-call(s32[1,2048]{1,0:T(1,128)S(1)} %bitcast.28, bf16[2048,2048]{1,0:T(8,128)(2,1)S(1)} %bitcast.13, ...), custom_call_target="tpu_custom_call", output_to_operand_aliasing={{0}: (6, {})} | custom-call | flops 2147483648 | bytes 14692352 | tf_op jit(solution)/shard_map/first_apply/pallas_call | solution.py:29
  91.6 4.8 %collective-permute-start.14 = (f32[512,128]{1,0:T(8,128)S(1)}, f32[512,128]{1,0:T(8,128)S(1)}, u32[]{:S(2)}, u32[]{:S(2)}) collective-permute-start(f32[512,128]{1,0:T(8,128)S(1)} %get-tuple-element.124), channel_id=1, source_target_pairs={{0,31},{1,0},{2,1},{3,2},{4,3},{5,4},{6,5},{7,6},{8,7},{9,8},{10,9... | collective-permute-start | bytes 786440 | tf_op jit(solution)/shard_map/ppermute | solution.py:358
  99.3 2.7 %collective-permute-done.13.three = f32[512,128]{1,0:T(8,128)S(1)} collective-permute-done((f32[512,128]{1,0:T(8,128)S(1)}, f32[512,128]{1,0:T(8,128)S(1)}, u32[]{:S(2)}, u32[]{:S(2)}) %collective-permute-start.13) | collective-permute-done | bytes 262176 | tf_op jit(solution)/shard_map/ppermute | solution.py:358
  104.4 2.2 %image_partial.1 = (f32[2048,128]{1,0:T(8,128)S(1)}, f32[2048,128]{1,0:T(8,128)S(1)}, f32[8,40,128]{2,1,0:T(8,128)S(1)}) custom-call(s32[1,2048]{1,0:T(1,128)S(1)} %bitcast.31, f32[2048,128]{1,0:T(8,128)S(1)} %get-tuple-element.120.source.product, f32[2048,128]{1,0:T(8,128)S(1)} %get-tuple-element.97.weight, ...), custom_call_target="tpu_custom_call", output_to_operand_aliasing={{0}: (5, {})} | custom-call | bytes 6991872 | tf_op jit(solution)/shard_map/image_partial/pallas_call | solution.py:29
  106.6 11.5 %all_to_all.38.chunks = f32[8,40,128]{2,1,0:T(8,128)S(1)} all-to-all(f32[8,40,128]{2,1,0:T(8,128)S(1)} %get-tuple-element.127), channel_id=1, replica_groups=mesh['sub'=8,'grp'=32] {'sub'}, dimensions={0} | all-to-all | bytes 327680 | tf_op jit(solution)/shard_map/all_to_all | solution.py:376
  119.9 5.1 %local_fix.3 = (f32[2048,128]{1,0:T(8,128)S(1)}, f32[16,256]{1,0:T(8,128)S(1)}) custom-call(bf16[2048,2048]{1,0:T(8,128)(2,1)S(1)} %bitcast.14, f32[2048,128]{1,0:T(8,128)S(1)} %get-tuple-element.132.weighted, f32[2048,128]{1,0:T(8,128)S(1)} %get-tuple-element.105.diagonal, f32[16,256]{1,0:T(8,128)S(1)} %get-tuple-element.133.total, f32[256,256]{1,0:T(8,128)S(1)} %bitcast.45), custom_call_target="tpu_custom_call" | custom-call | flops 4294967296 | bytes 11829248 | tf_op jit(solution)/shard_map/local_fix/pallas_call | solution.py:29
  125.1 11.0 %all_to_all.39.chunks = f32[8,40,128]{2,1,0:T(8,128)S(1)} all-to-all(f32[8,40,128]{2,1,0:T(8,128)S(1)} %add_and_copy.3), channel_id=1, replica_groups={{0,4,8,12,16,20,24,28},{1,5,9,13,17,21,25,29},{2,6,10,14,18,22,26,30},{..., dimensions={0} | all-to-all | bytes 327680 | tf_op jit(solution)/shard_map/all_to_all | solution.py:376
  136.4 10.4 %all_to_all.40 = f32[8,16,256]{2,1,0:T(8,128)S(1)} all-to-all(f32[8,16,256]{2,1,0:T(8,128)S(1)} %get-tuple-element.141), channel_id=1, replica_groups=mesh['sub'=8,'grp'=32] {'sub'}, dimensions={0} | all-to-all | bytes 262144 | tf_op jit(solution)/shard_map/all_to_all | solution.py:376
  146.8 2.2 %second_local.1 = (f32[2048,128]{1,0:T(8,128)S(1)}, f32[2048,128]{1,0:T(8,128)S(1)}, f32[512,128]{1,0:T(8,128)S(1)}, f32[512,128]{1,0:T(8,128)S(1)}) custom-call(s32[1,2048]{1,0:T(1,128)S(1)} %bitcast.32, f32[2048,128]{1,0:T(8,128)S(1)} %get-tuple-element.97.weight, bf16[2048,256]{1,0:T(8,128)(2,1)S(1)} %bitcast.19, ...), custom_call_target="tpu_custom_call" | custom-call | bytes 9056256 | tf_op jit(solution)/shard_map/second_local/pallas_call | solution.py:29
  149.0 2.4 %collective-permute-start.20 = (f32[512,128]{1,0:T(8,128)S(1)}, f32[512,128]{1,0:T(8,128)S(1)}, u32[]{:S(2)}, u32[]{:S(2)}) collective-permute-start(f32[512,128]{1,0:T(8,128)S(1)} %get-tuple-element.148), channel_id=1, source_target_pairs={{0,1},{1,2},{2,3},{3,4},{4,5},{5,6},{6,7},{7,8},{8,9},{9,10},{10,1... | collective-permute-start | bytes 786440 | tf_op jit(solution)/shard_map/ppermute | solution.py:358
  151.4 2.5 %collective-permute-start.21 = (f32[512,128]{1,0:T(8,128)S(1)}, f32[512,128]{1,0:T(8,128)S(1)}, u32[]{:S(2)}, u32[]{:S(2)}) collective-permute-start(f32[512,128]{1,0:T(8,128)S(1)} %get-tuple-element.149), channel_id=1, source_target_pairs={{0,31},{1,0},{2,1},{3,2},{4,3},{5,4},{6,5},{7,6},{8,7},{9,8},{10,9... | collective-permute-start | bytes 786440 | tf_op jit(solution)/shard_map/ppermute | solution.py:358
  157.0 2.3 %collective-permute-done.20.three = f32[512,128]{1,0:T(8,128)S(1)} collective-permute-done((f32[512,128]{1,0:T(8,128)S(1)}, f32[512,128]{1,0:T(8,128)S(1)}, u32[]{:S(2)}, u32[]{:S(2)}) %collective-permute-start.20) | collective-permute-done | bytes 262176 | tf_op jit(solution)/shard_map/ppermute | solution.py:358
  160.9 2.2 %collective-permute-done.19.two = f32[512,128]{1,0:T(8,128)S(1)} collective-permute-done((f32[512,128]{1,0:T(8,128)S(1)}, f32[512,128]{1,0:T(8,128)S(1)}, u32[]{:S(2)}, u32[]{:S(2)}) %collective-permute-start.19) | collective-permute-done | bytes 262176 | tf_op jit(solution)/shard_map/ppermute | solution.py:358
  163.1 5.3 %second_apply.1 = (f32[2048,128]{1,0:T(8,128)S(1)}, f32[2048,128]{1,0:T(8,128)S(1)}, f32[8,128]{1,0:T(8,128)S(1)}, f32[512,128]{1,0:T(8,128)S(1)}, f32[512,128]{1,0:T(8,128)S(1)}) custom-call(s32[1,2048]{1,0:T(1,128)S(1)} %bitcast.35, bf16[2048,2048]{1,0:T(8,128)(2,1)S(1)} %bitcast.15, ...), custom_call_target="tpu_custom_call", output_to_operand_aliasing={{0}: (7, {})} | custom-call | flops 2147483648 | bytes 15740928 | tf_op jit(solution)/shard_map/second_apply/pallas_call | solution.py:29
  168.5 4.8 %collective-permute-start.29 = (f32[512,128]{1,0:T(8,128)S(1)}, f32[512,128]{1,0:T(8,128)S(1)}, u32[]{:S(2)}, u32[]{:S(2)}) collective-permute-start(f32[512,128]{1,0:T(8,128)S(1)} %get-tuple-element.155), channel_id=1, source_target_pairs={{0,31},{1,0},{2,1},{3,2},{4,3},{5,4},{6,5},{7,6},{8,7},{9,8},{10,9... | collective-permute-start | bytes 786440 | tf_op jit(solution)/shard_map/ppermute | solution.py:358
  176.2 2.9 %collective-permute-start.22 = (f32[8,128]{1,0:T(8,128)S(1)}, f32[8,128]{1,0:T(8,128)S(1)}, u32[]{:S(2)}, u32[]{:S(2)}) collective-permute-start(f32[8,128]{1,0:T(8,128)S(1)} %get-tuple-element.150), channel_id=1, source_target_pairs={{0,32},{32,0},{64,96},{96,64},{128,160},{160,128},{192,224},{224,1... | collective-permute-start | bytes 12296 | tf_op jit(solution)/shard_map/ppermute | solution.py:508
  185.1 12.2 %all_to_all.41.chunks = f32[32,1,384]{2,1,0:T(1,128)S(1)} all-to-all(f32[32,1,384]{2,1,0:T(1,128)S(1)} %copy_row.1), channel_id=1, replica_groups=mesh['sub'=8,'grp'=32] {'grp'}, dimensions={0} | all-to-all | bytes 98304 | tf_op jit(solution)/shard_map/all_to_all | solution.py:376
  (84 shorter events, 34.9 us)
Async XLA Ops:
  0.6 25.8 %copy-start.6 = (f32[1,1,2048]{2,1,0:T(1,128)S(1)}, f32[1,1,2048]{2,1,0:T(1,128)}, u32[]{:S(2)}) copy-start(f32[1,1,2048]{2,1,0:T(1,128)} %param.10) | copy-start | bytes 24580
  6.4 17.8 %collective-permute-start = (f32[520,128]{1,0:T(8,128)}, f32[520,128]{1,0:T(8,128)S(1)}, u32[]{:S(2)}, u32[]{:S(2)}) collective-permute-start(f32[520,128]{1,0:T(8,128)} %get-tuple-element.85), channel_id=1, source_target_pairs={{0,1},{1,2},{2,3},{3,4},{4,5},{5,6},{6,7},{7,8},{8,9},{9,10},{10,1... | collective-permute-start | bytes 798728 | tf_op jit(solution)/shard_map/ppermute | solution.py:358
  8.6 15.7 %collective-permute-start.1 = (f32[520,128]{1,0:T(8,128)}, f32[520,128]{1,0:T(8,128)S(1)}, u32[]{:S(2)}, u32[]{:S(2)}) collective-permute-start(f32[520,128]{1,0:T(8,128)} %get-tuple-element.86), channel_id=1, source_target_pairs={{0,31},{1,0},{2,1},{3,2},{4,3},{5,4},{6,5},{7,6},{8,7},{9,8},{10,9... | collective-permute-start | bytes 798728 | tf_op jit(solution)/shard_map/ppermute | solution.py:358
  15.5 8.8 %collective-permute-start.3 = (f32[520,128]{1,0:T(8,128)}, f32[520,128]{1,0:T(8,128)S(1)}, u32[]{:S(2)}, u32[]{:S(2)}) collective-permute-start(f32[520,128]{1,0:T(8,128)} %get-tuple-element.94), channel_id=1, source_target_pairs={{0,224},{32,0},{64,32},{96,64},{128,96},{160,128},{192,160},{224,1... | collective-permute-start | bytes 798728 | tf_op jit(solution)/shard_map/ppermute | solution.py:358
  16.4 7.9 %collective-permute-start.2 = (f32[520,128]{1,0:T(8,128)}, f32[520,128]{1,0:T(8,128)S(1)}, u32[]{:S(2)}, u32[]{:S(2)}) collective-permute-start(f32[520,128]{1,0:T(8,128)} %get-tuple-element.93), channel_id=1, source_target_pairs={{0,32},{32,64},{64,96},{96,128},{128,160},{160,192},{192,224},{224... | collective-permute-start | bytes 798728 | tf_op jit(solution)/shard_map/ppermute | solution.py:358
  39.8 6.7 %collective-permute-start.6 = (f32[16,256]{1,0:T(8,128)S(1)}, f32[16,256]{1,0:T(8,128)S(1)}, u32[]{:S(2)}, u32[]{:S(2)}) collective-permute-start(f32[16,256]{1,0:T(8,128)S(1)} %get-tuple-element.103.refs_0_), channel_id=1, source_target_pairs={{0,3},{1,0},{2,1},{3,2},{4,7},{5,4},{6,5},{7,6},{8,11},{9,8},{10,9... | collective-permute-start | bytes 49160 | tf_op jit(solution)/shard_map/ppermute | solution.py:363
  39.8 6.7 %collective-permute-start.5 = (f32[16,256]{1,0:T(8,128)S(1)}, f32[16,256]{1,0:T(8,128)S(1)}, u32[]{:S(2)}, u32[]{:S(2)}) collective-permute-start(f32[16,256]{1,0:T(8,128)S(1)} %get-tuple-element.103.refs_0_), channel_id=1, source_target_pairs={{0,2},{1,3},{2,0},{3,1},{4,6},{5,7},{6,4},{7,5},{8,10},{9,11},{10,... | collective-permute-start | bytes 49160 | tf_op jit(solution)/shard_map/ppermute | solution.py:363
  40.0 6.6 %collective-permute-start.4 = (f32[16,256]{1,0:T(8,128)S(1)}, f32[16,256]{1,0:T(8,128)S(1)}, u32[]{:S(2)}, u32[]{:S(2)}) collective-permute-start(f32[16,256]{1,0:T(8,128)S(1)} %get-tuple-element.103.refs_0_), channel_id=1, source_target_pairs={{0,1},{1,2},{2,3},{3,0},{4,5},{5,6},{6,7},{7,4},{8,9},{9,10},{10,1... | collective-permute-start | bytes 49160 | tf_op jit(solution)/shard_map/ppermute | solution.py:363
  71.9 10.5 %collective-permute-start.9 = (f32[512,128]{1,0:T(8,128)S(1)}, f32[512,128]{1,0:T(8,128)S(1)}, u32[]{:S(2)}, u32[]{:S(2)}) collective-permute-start(f32[512,128]{1,0:T(8,128)S(1)} %get-tuple-element.118), channel_id=1, source_target_pairs={{0,1},{1,2},{2,3},{3,4},{4,5},{5,6},{6,7},{7,8},{8,9},{9,10},{10,1... | collective-permute-start | bytes 786440 | tf_op jit(solution)/shard_map/ppermute | solution.py:358
  74.3 8.2 %collective-permute-start.10 = (f32[512,128]{1,0:T(8,128)S(1)}, f32[512,128]{1,0:T(8,128)S(1)}, u32[]{:S(2)}, u32[]{:S(2)}) collective-permute-start(f32[512,128]{1,0:T(8,128)S(1)} %get-tuple-element.119), channel_id=1, source_target_pairs={{0,31},{1,0},{2,1},{3,2},{4,3},{5,4},{6,5},{7,6},{8,7},{9,8},{10,9... | collective-permute-start | bytes 786440 | tf_op jit(solution)/shard_map/ppermute | solution.py:358
  78.6 5.5 %collective-permute-start.7 = (f32[512,128]{1,0:T(8,128)S(1)}, f32[512,128]{1,0:T(8,128)S(1)}, u32[]{:S(2)}, u32[]{:S(2)}) collective-permute-start(f32[512,128]{1,0:T(8,128)S(1)} %get-tuple-element.116), channel_id=1, source_target_pairs={{0,32},{32,64},{64,96},{96,128},{128,160},{160,192},{192,224},{224... | collective-permute-start | bytes 786440 | tf_op jit(solution)/shard_map/ppermute | solution.py:358
  80.2 6.1 %collective-permute-start.8 = (f32[512,128]{1,0:T(8,128)S(1)}, f32[512,128]{1,0:T(8,128)S(1)}, u32[]{:S(2)}, u32[]{:S(2)}) collective-permute-start(f32[512,128]{1,0:T(8,128)S(1)} %get-tuple-element.117), channel_id=1, source_target_pairs={{0,224},{32,0},{64,32},{96,64},{128,96},{160,128},{192,160},{224,1... | collective-permute-start | bytes 786440 | tf_op jit(solution)/shard_map/ppermute | solution.py:358
  86.3 31.9 %copy-start.8 = (s32[1,256]{1,0:T(1,128)S(1)}, s32[1,256]{1,0:T(1,128)}, u32[]{:S(2)}) copy-start(s32[1,256]{1,0:T(1,128)} %members.5) | copy-start | bytes 3076
  91.6 10.5 %collective-permute-start.13 = (f32[512,128]{1,0:T(8,128)S(1)}, f32[512,128]{1,0:T(8,128)S(1)}, u32[]{:S(2)}, u32[]{:S(2)}) collective-permute-start(f32[512,128]{1,0:T(8,128)S(1)} %get-tuple-element.123), channel_id=1, source_target_pairs={{0,1},{1,2},{2,3},{3,4},{4,5},{5,6},{6,7},{7,8},{8,9},{9,10},{10,1... | collective-permute-start | bytes 786440 | tf_op jit(solution)/shard_map/ppermute | solution.py:358
  91.6 10.4 %collective-permute-start.14 = (f32[512,128]{1,0:T(8,128)S(1)}, f32[512,128]{1,0:T(8,128)S(1)}, u32[]{:S(2)}, u32[]{:S(2)}) collective-permute-start(f32[512,128]{1,0:T(8,128)S(1)} %get-tuple-element.124), channel_id=1, source_target_pairs={{0,31},{1,0},{2,1},{3,2},{4,3},{5,4},{6,5},{7,6},{8,7},{9,8},{10,9... | collective-permute-start | bytes 786440 | tf_op jit(solution)/shard_map/ppermute | solution.py:358
  98.0 5.6 %collective-permute-start.11 = (f32[512,128]{1,0:T(8,128)S(1)}, f32[512,128]{1,0:T(8,128)S(1)}, u32[]{:S(2)}, u32[]{:S(2)}) collective-permute-start(f32[512,128]{1,0:T(8,128)S(1)} %get-tuple-element.121), channel_id=1, source_target_pairs={{0,32},{32,64},{64,96},{96,128},{128,160},{160,192},{192,224},{224... | collective-permute-start | bytes 786440 | tf_op jit(solution)/shard_map/ppermute | solution.py:358
  98.3 6.1 %collective-permute-start.12 = (f32[512,128]{1,0:T(8,128)S(1)}, f32[512,128]{1,0:T(8,128)S(1)}, u32[]{:S(2)}, u32[]{:S(2)}) collective-permute-start(f32[512,128]{1,0:T(8,128)S(1)} %get-tuple-element.122), channel_id=1, source_target_pairs={{0,224},{32,0},{64,32},{96,64},{128,96},{160,128},{192,160},{224,1... | collective-permute-start | bytes 786440 | tf_op jit(solution)/shard_map/ppermute | solution.py:358
  118.4 6.6 %collective-permute-start.17 = (f32[40,128]{1,0:T(8,128)S(1)}, f32[40,128]{1,0:T(8,128)S(1)}, u32[]{:S(2)}, u32[]{:S(2)}) collective-permute-start(f32[40,128]{1,0:T(8,128)S(1)} %get-tuple-element.131.refs_0_), channel_id=1, source_target_pairs={{0,3},{1,0},{2,1},{3,2},{4,7},{5,4},{6,5},{7,6},{8,11},{9,8},{10,9... | collective-permute-start | bytes 61448 | tf_op jit(solution)/shard_map/ppermute | solution.py:363
  118.4 6.6 %collective-permute-start.16 = (f32[40,128]{1,0:T(8,128)S(1)}, f32[40,128]{1,0:T(8,128)S(1)}, u32[]{:S(2)}, u32[]{:S(2)}) collective-permute-start(f32[40,128]{1,0:T(8,128)S(1)} %get-tuple-element.131.refs_0_), channel_id=1, source_target_pairs={{0,2},{1,3},{2,0},{3,1},{4,6},{5,7},{6,4},{7,5},{8,10},{9,11},{10,... | collective-permute-start | bytes 61448 | tf_op jit(solution)/shard_map/ppermute | solution.py:363
  118.6 6.5 %collective-permute-start.15 = (f32[40,128]{1,0:T(8,128)S(1)}, f32[40,128]{1,0:T(8,128)S(1)}, u32[]{:S(2)}, u32[]{:S(2)}) collective-permute-start(f32[40,128]{1,0:T(8,128)S(1)} %get-tuple-element.131.refs_0_), channel_id=1, source_target_pairs={{0,1},{1,2},{2,3},{3,0},{4,5},{5,6},{6,7},{7,4},{8,9},{9,10},{10,1... | collective-permute-start | bytes 61448 | tf_op jit(solution)/shard_map/ppermute | solution.py:363
  149.0 10.4 %collective-permute-start.20 = (f32[512,128]{1,0:T(8,128)S(1)}, f32[512,128]{1,0:T(8,128)S(1)}, u32[]{:S(2)}, u32[]{:S(2)}) collective-permute-start(f32[512,128]{1,0:T(8,128)S(1)} %get-tuple-element.148), channel_id=1, source_target_pairs={{0,1},{1,2},{2,3},{3,4},{4,5},{5,6},{6,7},{7,8},{8,9},{9,10},{10,1... | collective-permute-start | bytes 786440 | tf_op jit(solution)/shard_map/ppermute | solution.py:358
  151.4 8.0 %collective-permute-start.21 = (f32[512,128]{1,0:T(8,128)S(1)}, f32[512,128]{1,0:T(8,128)S(1)}, u32[]{:S(2)}, u32[]{:S(2)}) collective-permute-start(f32[512,128]{1,0:T(8,128)S(1)} %get-tuple-element.149), channel_id=1, source_target_pairs={{0,31},{1,0},{2,1},{3,2},{4,3},{5,4},{6,5},{7,6},{8,7},{9,8},{10,9... | collective-permute-start | bytes 786440 | tf_op jit(solution)/shard_map/ppermute | solution.py:358
  155.4 5.5 %collective-permute-start.18 = (f32[512,128]{1,0:T(8,128)S(1)}, f32[512,128]{1,0:T(8,128)S(1)}, u32[]{:S(2)}, u32[]{:S(2)}) collective-permute-start(f32[512,128]{1,0:T(8,128)S(1)} %get-tuple-element.146), channel_id=1, source_target_pairs={{0,32},{32,64},{64,96},{96,128},{128,160},{160,192},{192,224},{224... | collective-permute-start | bytes 786440 | tf_op jit(solution)/shard_map/ppermute | solution.py:358
  157.0 6.1 %collective-permute-start.19 = (f32[512,128]{1,0:T(8,128)S(1)}, f32[512,128]{1,0:T(8,128)S(1)}, u32[]{:S(2)}, u32[]{:S(2)}) collective-permute-start(f32[512,128]{1,0:T(8,128)S(1)} %get-tuple-element.147), channel_id=1, source_target_pairs={{0,224},{32,0},{64,32},{96,64},{128,96},{160,128},{192,160},{224,1... | collective-permute-start | bytes 786440 | tf_op jit(solution)/shard_map/ppermute | solution.py:358
  168.4 11.5 %collective-permute-start.28 = (f32[512,128]{1,0:T(8,128)S(1)}, f32[512,128]{1,0:T(8,128)S(1)}, u32[]{:S(2)}, u32[]{:S(2)}) collective-permute-start(f32[512,128]{1,0:T(8,128)S(1)} %get-tuple-element.154), channel_id=1, source_target_pairs={{0,1},{1,2},{2,3},{3,4},{4,5},{5,6},{6,7},{7,8},{8,9},{9,10},{10,1... | collective-permute-start | bytes 786440 | tf_op jit(solution)/shard_map/ppermute | solution.py:358
  168.5 12.1 %collective-permute-start.29 = (f32[512,128]{1,0:T(8,128)S(1)}, f32[512,128]{1,0:T(8,128)S(1)}, u32[]{:S(2)}, u32[]{:S(2)}) collective-permute-start(f32[512,128]{1,0:T(8,128)S(1)} %get-tuple-element.155), channel_id=1, source_target_pairs={{0,31},{1,0},{2,1},{3,2},{4,3},{5,4},{6,5},{7,6},{8,7},{9,8},{10,9... | collective-permute-start | bytes 786440 | tf_op jit(solution)/shard_map/ppermute | solution.py:358
  174.9 8.2 %collective-permute-start.26 = (f32[512,128]{1,0:T(8,128)S(1)}, f32[512,128]{1,0:T(8,128)S(1)}, u32[]{:S(2)}, u32[]{:S(2)}) collective-permute-start(f32[512,128]{1,0:T(8,128)S(1)} %get-tuple-element.152), channel_id=1, source_target_pairs={{0,32},{32,64},{64,96},{96,128},{128,160},{160,192},{192,224},{224... | collective-permute-start | bytes 786440 | tf_op jit(solution)/shard_map/ppermute | solution.py:358
  175.2 7.9 %collective-permute-start.27 = (f32[512,128]{1,0:T(8,128)S(1)}, f32[512,128]{1,0:T(8,128)S(1)}, u32[]{:S(2)}, u32[]{:S(2)}) collective-permute-start(f32[512,128]{1,0:T(8,128)S(1)} %get-tuple-element.153), channel_id=1, source_target_pairs={{0,224},{32,0},{64,32},{96,64},{128,96},{160,128},{192,160},{224,1... | collective-permute-start | bytes 786440 | tf_op jit(solution)/shard_map/ppermute | solution.py:358
  176.2 3.8 %collective-permute-start.22 = (f32[8,128]{1,0:T(8,128)S(1)}, f32[8,128]{1,0:T(8,128)S(1)}, u32[]{:S(2)}, u32[]{:S(2)}) collective-permute-start(f32[8,128]{1,0:T(8,128)S(1)} %get-tuple-element.150), channel_id=1, source_target_pairs={{0,32},{32,0},{64,96},{96,64},{128,160},{160,128},{192,224},{224,1... | collective-permute-start | bytes 12296 | tf_op jit(solution)/shard_map/ppermute | solution.py:508
  180.0 4.8 %collective-permute-start.25 = (f32[8,128]{1,0:T(8,128)S(1)}, f32[8,128]{1,0:T(8,128)S(1)}, u32[]{:S(2)}, u32[]{:S(2)}) collective-permute-start(f32[8,128]{1,0:T(8,128)S(1)} %add.3.refs_0_), channel_id=1, source_target_pairs={{0,192},{32,224},{64,0},{96,32},{128,64},{160,96},{192,128},{224,1... | collective-permute-start | bytes 12296 | tf_op jit(solution)/shard_map/ppermute | solution.py:358
  180.0 4.8 %collective-permute-start.24 = (f32[8,128]{1,0:T(8,128)S(1)}, f32[8,128]{1,0:T(8,128)S(1)}, u32[]{:S(2)}, u32[]{:S(2)}) collective-permute-start(f32[8,128]{1,0:T(8,128)S(1)} %add.3.refs_0_), channel_id=1, source_target_pairs={{0,128},{32,160},{64,192},{96,224},{128,0},{160,32},{192,64},{224,... | collective-permute-start | bytes 12296 | tf_op jit(solution)/shard_map/ppermute | solution.py:358
  180.7 4.5 %collective-permute-start.23 = (f32[8,128]{1,0:T(8,128)S(1)}, f32[8,128]{1,0:T(8,128)S(1)}, u32[]{:S(2)}, u32[]{:S(2)}) collective-permute-start(f32[8,128]{1,0:T(8,128)S(1)} %add.3.refs_0_), channel_id=1, source_target_pairs={{0,64},{32,96},{64,128},{96,160},{128,192},{160,224},{192,0},{224,... | collective-permute-start | bytes 12296 | tf_op jit(solution)/shard_map/ppermute | solution.py:358
  (8 other events, 90.9 us)
